TPU v7x, 32 devices: a whole 2x2x4 slice. The times are simulated.
32 devices in a mesh: groups: 2 (over x), expert: 4 (over y, core), dp: 4 (over z).
Axes of the slice: x: 2, y: 2, z: 4, core: 2. Of those that a mesh axis runs over, the one named last changes fastest.
Arguments:
- tokens: bfloat16 [6144, 2048], P(('groups', 'expert', 'dp')), parts along dimension 0, may hold values from -6 to 6
- expert_ids: int32 [6144, 2], P(('groups', 'expert', 'dp')), parts along dimension 0, may hold values from 0 to 3, all different within a row; in each aligned block of 192 rows (0 to 191, 192 to 383, ...) at most 128 rows name the same one
- gate_weights: float32 [6144, 2], P(('groups', 'expert', 'dp')), parts along dimension 0, may hold values from 0.1 to 1
- out_grad: bfloat16 [6144, 2048], P(('groups', 'expert', 'dp')), parts along dimension 0, may hold values from -1.5 to 1.5
- w_gate: bfloat16 [4, 2048, 768], P('expert'), may hold values from -0.125 to 0.125
- w_up: bfloat16 [4, 2048, 768], P('expert'), may hold values from -0.125 to 0.125
- w_down: bfloat16 [4, 768, 2048], P('expert'), may hold values from -0.21875 to 0.21875
Outputs:
- token_grads: bfloat16 [6144, 2048], P(('groups', 'expert', 'dp')), parts along dimension 0
- gate_grads: float32 [6144, 2], P(('groups', 'expert', 'dp')), parts along dimension 0
- grad_gate: bfloat16 [8, 2048, 768], P(('groups', 'expert'), 'dp'), parts along dimension 0
- grad_up: bfloat16 [8, 2048, 768], P(('groups', 'expert'), 'dp'), parts along dimension 0
- grad_down: bfloat16 [8, 768, 2048], P(('groups', 'expert'), None, 'dp'), parts along dimension 0
There are 2 independent parts, one for each index of `groups`. A program takes and returns all parts, laid end to end along the dimension named above; an argument that names none is the same for every part. Nothing has to cross between parts.
Inputs may be any that keep to these rules, and one draw needn't show every extreme that they name: `expert_ids`: A token's 2 picks name different experts. Within the rows of one device no expert is named by more than 128 picks, and in every draw some device names some expert exactly 128 times.
All inputs are finite; a program needn't handle non-finite values.
Results may differ from a plain program's by a relative error of at most 0.009.
Values may be sent and summed in bfloat16 or wider, within the bound.
No kernel may reach another device: no remote copies, remote signals or barrier semaphores. Data moves between devices by JAX's collectives and lax.ppermute only.
A program may use at most 128 MiB of HBM per device.

v0:
```python
import jax
import jax.numpy as jnp
from jax import lax
from jax.sharding import PartitionSpec as P


def forward_rows(x_block, gate_w, up_w, down_w):
    gate_pre = jnp.dot(x_block, gate_w, preferred_element_type=jnp.float32)
    up_pre = jnp.dot(x_block, up_w, preferred_element_type=jnp.float32)
    activated = gate_pre * jax.nn.sigmoid(gate_pre)
    hidden = (activated * up_pre).astype(jnp.bfloat16)
    expert_out = jnp.dot(hidden, down_w, preferred_element_type=jnp.float32).astype(jnp.bfloat16)
    return (gate_pre, up_pre, hidden, expert_out)


def backward_rows(x_block, grad_block, gate_pre, up_pre, gate_w, up_w, down_w):
    hidden_grad = jnp.dot(grad_block, down_w.T, preferred_element_type=jnp.float32)
    sigmoid = jax.nn.sigmoid(gate_pre)
    activated = gate_pre * sigmoid
    gate_pre_grad = (hidden_grad * up_pre * (sigmoid * (1.0 + gate_pre * (1.0 - sigmoid)))).astype(
        jnp.bfloat16
    )
    up_pre_grad = (hidden_grad * activated).astype(jnp.bfloat16)
    input_grad = (
        jnp.dot(gate_pre_grad, gate_w.T, preferred_element_type=jnp.float32)
        + jnp.dot(up_pre_grad, up_w.T, preferred_element_type=jnp.float32)
    ).astype(jnp.bfloat16)
    grad_g = jnp.dot(x_block.T, gate_pre_grad, preferred_element_type=jnp.float32)
    grad_u = jnp.dot(x_block.T, up_pre_grad, preferred_element_type=jnp.float32)
    return (input_grad, grad_g, grad_u)


def on_device(tokens, expert_ids, gate_weights, out_grad, w_gate, w_up, w_down):
    tok_count, pick_width = expert_ids.shape
    features = tokens.shape[1]
    expert_count = lax.axis_size("expert")
    capacity = 4 * tok_count * pick_width // (3 * expert_count)
    picks_total = tok_count * pick_width
    slot_total = expert_count * capacity
    block_rows = 128
    padded_rows = (slot_total + block_rows - 1) // block_rows * block_rows
    gate_w = w_gate[0]
    up_w = w_up[0]
    down_w = w_down[0]
    hidden_units = gate_w.shape[1]
    flat_ids = expert_ids.reshape(-1)
    one_hot = (flat_ids[:, None] == jnp.arange(expert_count, dtype=jnp.int32)[None, :]).astype(
        jnp.int32
    )
    slot_rank = jnp.sum((jnp.cumsum(one_hot, axis=0) - 1) * one_hot, axis=1)
    send_counts = jnp.sum(one_hot, axis=0).reshape(expert_count, 1)
    position = flat_ids * capacity + slot_rank
    slot_table = (
        jnp.full((slot_total,), picks_total, jnp.int32)
        .at[position]
        .set(jnp.arange(picks_total, dtype=jnp.int32))
    )
    filled_slot = slot_table < picks_total
    safe_pick = jnp.minimum(slot_table, picks_total - 1)
    source_tok = safe_pick // pick_width
    outbound = jnp.where(filled_slot[:, None], tokens[source_tok], jnp.zeros((), jnp.bfloat16))
    flat_gate = gate_weights.reshape(-1)
    plain_grad = out_grad[source_tok]
    scaled = (flat_gate[safe_pick][:, None] * plain_grad.astype(jnp.float32)).astype(jnp.bfloat16)
    grad_out = jnp.where(filled_slot[:, None], scaled, jnp.zeros((), jnp.bfloat16))
    inbound, recv_counts = (
        lax.all_to_all(
            outbound.reshape(expert_count, capacity, features),
            "expert",
            split_axis=0,
            concat_axis=0,
            tiled=True,
        ),
        lax.all_to_all(send_counts, "expert", split_axis=0, concat_axis=0, tiled=True),
    )
    live_rows = (jnp.arange(capacity, dtype=jnp.int32)[None, :] < recv_counts).reshape(-1)
    rows_in = inbound.reshape(slot_total, features)
    row_order = jnp.argsort(jnp.where(live_rows, 0, 1).astype(jnp.int32), stable=True)
    used_rows = jnp.sum(live_rows.astype(jnp.int32))
    block_count = (used_rows + block_rows - 1) // block_rows
    packed_x = rows_in[row_order]

    def forward_block(block_index, buffers):
        gate_buf, up_buf, hidden_buf, out_buf = buffers
        offset = block_index * block_rows
        x_block = lax.dynamic_slice_in_dim(packed_x, offset, block_rows, 0)
        gate_pre, up_pre, hidden, expert_out = forward_rows(x_block, gate_w, up_w, down_w)
        return (
            lax.dynamic_update_slice_in_dim(gate_buf, gate_pre, offset, 0),
            lax.dynamic_update_slice_in_dim(up_buf, up_pre, offset, 0),
            lax.dynamic_update_slice_in_dim(hidden_buf, hidden, offset, 0),
            lax.dynamic_update_slice_in_dim(out_buf, expert_out, offset, 0),
        )

    start_buffers = (
        jnp.zeros((padded_rows, hidden_units), jnp.float32),
        jnp.zeros((padded_rows, hidden_units), jnp.float32),
        jnp.zeros((padded_rows, hidden_units), jnp.bfloat16),
        jnp.zeros((padded_rows, features), jnp.bfloat16),
    )
    gate_buf, up_buf, hidden_buf, out_buf = lax.fori_loop(
        0, block_count, forward_block, start_buffers
    )
    results = jnp.zeros((slot_total, features), jnp.bfloat16).at[row_order].set(out_buf)
    returned = lax.all_to_all(
        results.reshape(expert_count, capacity, features),
        "expert",
        split_axis=0,
        concat_axis=0,
        tiled=True,
    )
    back_rows = returned.reshape(slot_total, features)[position]
    grad_rows = jnp.repeat(out_grad, pick_width, axis=0)
    gate_grads = jnp.sum(
        grad_rows.astype(jnp.float32) * back_rows.astype(jnp.float32), axis=1
    ).reshape(tok_count, pick_width)
    grad_in = lax.all_to_all(
        grad_out.reshape(expert_count, capacity, features),
        "expert",
        split_axis=0,
        concat_axis=0,
        tiled=True,
    )
    packed_grad = grad_in.reshape(slot_total, features)[row_order]
    down_term = jnp.dot(hidden_buf.T, packed_grad, preferred_element_type=jnp.float32)

    def backward_block(block_index, state):
        input_buf, acc_gate, acc_up = state
        offset = block_index * block_rows
        x_block = lax.dynamic_slice_in_dim(packed_x, offset, block_rows, 0)
        grad_block = lax.dynamic_slice_in_dim(packed_grad, offset, block_rows, 0)
        gate_pre = lax.dynamic_slice_in_dim(gate_buf, offset, block_rows, 0)
        up_pre = lax.dynamic_slice_in_dim(up_buf, offset, block_rows, 0)
        input_grad, grad_g, grad_u = backward_rows(
            x_block, grad_block, gate_pre, up_pre, gate_w, up_w, down_w
        )
        return (
            lax.dynamic_update_slice_in_dim(input_buf, input_grad, offset, 0),
            acc_gate + grad_g,
            acc_up + grad_u,
        )

    start_state = (
        jnp.zeros((padded_rows, features), jnp.bfloat16),
        jnp.zeros((features, hidden_units), jnp.float32),
        jnp.zeros((features, hidden_units), jnp.float32),
    )
    input_buf, acc_gate, acc_up = lax.fori_loop(0, block_count, backward_block, start_state)
    input_rows = jnp.zeros((slot_total, features), jnp.bfloat16).at[row_order].set(input_buf)
    input_back = lax.all_to_all(
        input_rows.reshape(expert_count, capacity, features),
        "expert",
        split_axis=0,
        concat_axis=0,
        tiled=True,
    )
    pick_input = input_back.reshape(slot_total, features)[position].astype(jnp.float32)
    token_grads = jnp.sum(pick_input.reshape(tok_count, pick_width, features), axis=1).astype(
        jnp.bfloat16
    )
    gate_share, up_share, down_share = (
        lax.psum_scatter(
            acc_gate.astype(jnp.bfloat16), "dp", scatter_dimension=0, tiled=True
        ).astype(jnp.float32),
        lax.psum_scatter(acc_up.astype(jnp.bfloat16), "dp", scatter_dimension=0, tiled=True).astype(
            jnp.float32
        ),
        lax.psum_scatter(
            down_term.astype(jnp.bfloat16), "dp", scatter_dimension=1, tiled=True
        ).astype(jnp.float32),
    )
    return (
        token_grads,
        gate_grads,
        gate_share.astype(jnp.bfloat16)[None],
        up_share.astype(jnp.bfloat16)[None],
        down_share.astype(jnp.bfloat16)[None],
    )


def solution(mesh):
    placed = (
        P(("groups", "expert", "dp"), None),
        P(("groups", "expert", "dp"), None),
        P(("groups", "expert", "dp"), None),
        P(("groups", "expert", "dp"), None),
        P("expert", None, None),
        P("expert", None, None),
        P("expert", None, None),
    )
    return jax.shard_map(
        on_device,
        mesh=mesh,
        in_specs=placed,
        out_specs=(
            P(("groups", "expert", "dp"), None),
            P(("groups", "expert", "dp"), None),
            P(("groups", "expert"), "dp", None),
            P(("groups", "expert"), "dp", None),
            P(("groups", "expert"), None, "dp"),
        ),
        check_vma=False,
    )
```

profile of v0, /device:TPU:0, one launch (start us, length us, event | category | flops | bytes accessed | tf_op | source)
XLA Modules:
  0.0 358.9 jit_solution(2890735354723587228)
XLA Ops:
  8.4 1.2 reduce-window.6
  10.9 4.2 %all-to-all-start = ((s32[4,1,1]{2,1,0:T(1,128)}), s32[4,1,1]{2,1,0:T(1,128)S(1)}, u32[]{:S(2)}, u32[]{:S(2)}) async-start(s32[4,1,1]{2,1,0:T(1,128)} %copy.30), calls=%async_computation | async-start | bytes 4096 | tf_op jit(solution)/shard_map/all_to_all | solution.py:74
  16.1 2.9 scatter_custom_fusion
  20.0 3.3 gather_fusion.3
  23.3 3.3 gather_fusion.1
  26.6 3.5 gather_fusion
  30.1 5.7 %broadcast_select_fusion = (bf16[4,128,2048]{2,1,0:T(8,128)(2,1)}, bf16[4,128,2048]{2,1,0:T(8,128)(2,1)}) fusion(bf16[4,128,2048]{2,1,0:T(8,128)(2,1)} %bitcast.80, pred[4,128]{1,0:T(4,128)(4,1)S(1)} %compare_bitcast_fusion, bf16[4,128,2048]{2,1,0:T(8,128)(2,1)} %bitcast.81, f32[4,128]{1,0:T(4,128)S(1)} %bitcast.85), kind=kLoop, calls=%fused_computation.42 | loop fusion | flops 5242880 | bytes 8391168 | tf_op jit(solution)/shard_map/jit(_where)/select_n | solution.py:61
  35.8 30.2 %all_to_all.29 = bf16[4,128,2048]{2,1,0:T(8,128)(2,1)} all-to-all(bf16[4,128,2048]{2,1,0:T(8,128)(2,1)} %get-tuple-element.211), channel_id=1, replica_groups=mesh['groups'=2,'expert'=4,'dp'=4] {'expert'}, dimensions={0} | all-to-all | bytes 4194304 | tf_op jit(solution)/shard_map/all_to_all | solution.py:67
  66.0 4.4 %all-to-all-start.1 = ((bf16[4,128,2048]{2,1,0:T(8,128)(2,1)}), bf16[4,128,2048]{2,1,0:T(8,128)(2,1)}, u32[]{:S(2)}, u32[]{:S(2)}) async-start(bf16[4,128,2048]{2,1,0:T(8,128)(2,1)} %get-tuple-element.212), calls=%async_computation.1 | async-start | bytes 4194304 | tf_op jit(solution)/shard_map/all_to_all | solution.py:117
  72.2 3.8 %sort.17 = (s32[512]{0:T(512)}, s32[512]{0:T(512)S(1)}) sort(s32[512]{0:T(512)S(1)} %get-tuple-element.214, s32[512]{0:T(512)S(1)} %iota.19), dimensions={0}, to_apply=%region_1.2 | sort | flops 4608 | bytes 8192 | tf_op jit(solution)/shard_map/jit(argsort)/sort | solution.py:78
  76.0 7.1 %gather_fusion.4 = bf16[512,2048]{1,0:T(8,128)(2,1)} fusion(bf16[512,2048]{1,0:T(8,128)(2,1)} %bitcast.78, s32[1024]{0:T(1024)S(1)} %pad_clamp_fusion.1), kind=kCustom, calls=%fused_computation.4 | custom fusion | bytes 4196352 | tf_op jit(solution)/shard_map/gather | solution.py:81
  83.1 13.1 %all-to-all-done.1 = bf16[4,128,2048]{2,1,0:T(8,128)(2,1)} async-done(((bf16[4,128,2048]{2,1,0:T(8,128)(2,1)}), bf16[4,128,2048]{2,1,0:T(8,128)(2,1)}, u32[]{:S(2)}, u32[]{:S(2)}) %all-to-all-start.1) | async-done | bytes 2097184 | tf_op jit(solution)/shard_map/all_to_all | solution.py:117
  96.2 7.2 %gather_fusion.2 = bf16[512,2048]{1,0:T(8,128)(2,1)} fusion(bf16[512,2048]{1,0:T(8,128)(2,1)} %bitcast.6, s32[1024]{0:T(1024)S(1)} %pad_clamp_fusion.1), kind=kCustom, calls=%fused_computation.2 | custom fusion | bytes 4196352 | tf_op jit(solution)/shard_map/gather | solution.py:124
  104.4 1.3 broadcast.114
  105.7 1.6 broadcast.102.clone
  107.3 23.1 %while.30 = (s32[]{:T(128)}, f32[512,768]{1,0:T(8,128)}, f32[512,768]{1,0:T(8,128)S(1)}, bf16[512,768]{1,0:T(8,128)(2,1)}, bf16[512,2048]{1,0:T(8,128)(2,1)}, /*...) while((s32[]{:T(128)}, f32[512,768]{1,0:T(8,128)}, ...), condition=%wide.region_8.9_spmd, body=%wide.region_7.8_spmd.sunk | while | flops 1208811520 | bytes 39127284 | solution.py:101
  107.3 2.8 constant_dynamic-update-slice_fusion.7
  110.3 2.5 constant_dynamic-update-slice_fusion.6
  113.6 1.4 fusion.64
  115.0 2.8 constant_dynamic-update-slice_fusion.7
  118.0 2.5 constant_dynamic-update-slice_fusion.6
  121.3 1.4 fusion.64
  122.7 2.8 constant_dynamic-update-slice_fusion.7
  125.7 2.5 constant_dynamic-update-slice_fusion.6
  129.0 1.4 fusion.64
  130.4 5.4 %convolution_convert_fusion.1 = bf16[768,2048]{1,0:T(8,128)(2,1)} fusion(bf16[512,768]{1,0:T(8,128)(2,1)} %get-tuple-element.134, bf16[512,2048]{1,0:T(8,128)(2,1)} %gather_fusion.2), kind=kOutput, calls=%fused_computation.39 | convolution fusion | flops 1612185600 | bytes 6029312 | tf_op jit(solution)/shard_map/dot_general | solution.py:125
  135.9 1.6 broadcast.102
  137.5 3.0 broadcast.104.clone
  140.5 3.0 broadcast.104
  143.5 54.0 %while.31 = (s32[]{:T(128)}, bf16[512,2048]{1,0:T(8,128)(2,1)}, f32[2048,768]{1,0:T(8,128)}, f32[2048,768]{1,0:T(8,128)}, s32[]{:T(128)}, /*index=5*/bf16[512,20...) while((s32[]{:T(128)}, bf16[512,2048]{1,0:T(8,128)(2,1)}, ...), condition=%wide.region_10.11_spmd, body=%wide.region_9.10_spmd.sunk | while | flops 2018213888 | bytes 118359400 | solution.py:148
  143.7 3.5 multiply_convert_fusion.5
  147.2 1.1 fusion.74
  149.1 2.0 fusion.75
  151.2 6.6 %convolution_add_fusion.6 = f32[2048,768]{1,0:T(8,128)} fusion(f32[2048,768]{1,0:T(8,128)} %get-tuple-element.430, bf16[128,768]{1,0:T(8,128)(2,1)S(1)} %get-tuple-element.368, bf16[512,2048]{1,0:T(8,128)(2,1)S(1)} %copy-done.8, s32[]{:T(128)S(6)} %select_n.90), kind=kOutput, calls=%fused_computation.22.clone.1 | convolution fusion | flops 404226048 | bytes 13303812 | tf_op jit(solution)/shard_map/while/body/dot_general | solution.py:29
  157.8 1.3 convolution_add_fusion.5
  159.1 2.6 copy-done.6
  161.7 3.5 multiply_convert_fusion.5
  165.2 1.1 fusion.74
  167.1 2.0 fusion.75
  169.1 6.6 %convolution_add_fusion.6 = f32[2048,768]{1,0:T(8,128)} fusion(f32[2048,768]{1,0:T(8,128)} %get-tuple-element.430, bf16[128,768]{1,0:T(8,128)(2,1)S(1)} %get-tuple-element.368, bf16[512,2048]{1,0:T(8,128)(2,1)S(1)} %copy-done.8, s32[]{:T(128)S(6)} %select_n.90), kind=kOutput, calls=%fused_computation.22.clone.1 | convolution fusion | flops 404226048 | bytes 13303812 | tf_op jit(solution)/shard_map/while/body/dot_general | solution.py:29
  175.7 1.3 convolution_add_fusion.5
  177.0 2.6 copy-done.6
  179.6 3.5 multiply_convert_fusion.5
  183.2 1.1 fusion.74
  185.0 2.0 fusion.75
  187.0 6.6 %convolution_add_fusion.6 = f32[2048,768]{1,0:T(8,128)} fusion(f32[2048,768]{1,0:T(8,128)} %get-tuple-element.430, bf16[128,768]{1,0:T(8,128)(2,1)S(1)} %get-tuple-element.368, bf16[512,2048]{1,0:T(8,128)(2,1)S(1)} %copy-done.8, s32[]{:T(128)S(6)} %select_n.90), kind=kOutput, calls=%fused_computation.22.clone.1 | convolution fusion | flops 404226048 | bytes 13303812 | tf_op jit(solution)/shard_map/while/body/dot_general | solution.py:29
  193.6 1.3 convolution_add_fusion.5
  194.9 2.6 copy-done.6
  197.5 4.8 %convert_element_type.76 = bf16[2048,768]{1,0:T(8,128)(2,1)} convert(f32[2048,768]{1,0:T(8,128)} %get-tuple-element.133) | non-fusion elementwise | flops 1572864 | bytes 9437184 | tf_op jit(solution)/shard_map/convert_element_type | solution.py:165
  202.3 4.8 %convert_element_type.75 = bf16[2048,768]{1,0:T(8,128)(2,1)} convert(f32[2048,768]{1,0:T(8,128)} %get-tuple-element.132) | non-fusion elementwise | flops 1572864 | bytes 9437184 | tf_op jit(solution)/shard_map/convert_element_type | solution.py:163
  207.2 6.2 %scatter_custom_fusion.2 = bf16[512,2048]{1,0:T(8,128)(2,1)} fusion(s32[512]{0:T(512)S(1)} %compare_select_fusion.2, bf16[512,2048]{1,0:T(8,128)(2,1)} %get-tuple-element.131, bf16[]{:T(256)} %constant.43.clone.1), kind=kCustom, calls=%fused_computation.43 | custom fusion | bytes 2097664 | tf_op jit(solution)/shard_map/scatter | solution.py:104
  213.4 26.9 %all-to-all-start.4 = ((bf16[4,128,2048]{2,1,0:T(8,128)(2,1)}), bf16[4,128,2048]{2,1,0:T(8,128)(2,1)}, u32[]{:S(2)}, u32[]{:S(2)}) async-start(bf16[4,128,2048]{2,1,0:T(8,128)(2,1)} %bitcast.83), calls=%async_computation.4 | async-start | bytes 4194304 | tf_op jit(solution)/shard_map/all_to_all | solution.py:105
  240.3 6.2 %scatter_custom_fusion.1 = bf16[512,2048]{1,0:T(8,128)(2,1)} fusion(s32[512]{0:T(512)S(1)} %compare_select_fusion.2, bf16[512,2048]{1,0:T(8,128)(2,1)} %get-tuple-element.130, bf16[]{:T(256)} %constant.43.clone.1), kind=kCustom, calls=%fused_computation.45 | custom fusion | bytes 2097664 | tf_op jit(solution)/shard_map/scatter | solution.py:149
  246.5 19.4 %all-to-all-done.4 = bf16[4,128,2048]{2,1,0:T(8,128)(2,1)} async-done(((bf16[4,128,2048]{2,1,0:T(8,128)(2,1)}), bf16[4,128,2048]{2,1,0:T(8,128)(2,1)}, u32[]{:S(2)}, u32[]{:S(2)}) %all-to-all-start.4) | async-done | bytes 2097184 | tf_op jit(solution)/shard_map/all_to_all | solution.py:105
  265.9 4.7 %all-to-all-start.3 = ((bf16[4,128,2048]{2,1,0:T(8,128)(2,1)}), bf16[4,128,2048]{2,1,0:T(8,128)(2,1)}, u32[]{:S(2)}, u32[]{:S(2)}) async-start(bf16[4,128,2048]{2,1,0:T(8,128)(2,1)} %bitcast.82), calls=%async_computation.3 | async-start | bytes 4194304 | tf_op jit(solution)/shard_map/all_to_all | solution.py:150
  270.6 3.3 broadcast_in_dim.76
  273.9 5.3 %broadcast_in_dim.77 = f32[384,2048]{1,0:T(8,128)} reshape(f32[192,2,2048]{2,1,0:T(2,128)} %broadcast_in_dim.76) | data formatting | bytes 6291456 | tf_op jit(solution)/shard_map/broadcast_in_dim | solution.py:113
  279.2 6.3 %gather_fusion.6 = bf16[384,2048]{1,0:T(8,128)(2,1)S(1)} fusion(bf16[512,2048]{1,0:T(8,128)(2,1)} %bitcast.15, s32[1024]{0:T(1024)S(1)} %pad_clamp_fusion), kind=kCustom, calls=%fused_computation.6 | custom fusion | bytes 3147264 | tf_op jit(solution)/shard_map/gather | solution.py:112
  285.5 2.3 multiply_reduce_fusion
  288.6 7.8 %all-to-all-done.3 = bf16[4,128,2048]{2,1,0:T(8,128)(2,1)} async-done(((bf16[4,128,2048]{2,1,0:T(8,128)(2,1)}), bf16[4,128,2048]{2,1,0:T(8,128)(2,1)}, u32[]{:S(2)}, u32[]{:S(2)}) %all-to-all-start.3) | async-done | bytes 2097184 | tf_op jit(solution)/shard_map/all_to_all | solution.py:150
  296.4 7.4 %gather_fusion.5 = bf16[384,2048]{1,0:T(8,128)(2,1)} fusion(bf16[512,2048]{1,0:T(8,128)(2,1)} %bitcast.13, s32[1024]{0:T(1024)S(1)} %pad_clamp_fusion), kind=kCustom, calls=%fused_computation.5 | custom fusion | bytes 3147264 | tf_op jit(solution)/shard_map/gather | solution.py:157
  303.7 2.8 gather.32
  306.5 5.2 %reduce_sum.56 = bf16[192,2048]{1,0:T(8,128)(2,1)} reduce(bf16[192,2,2048]{2,1,0:T(2,128)(2,1)S(1)} %gather.32, bf16[]{:T(256)} %constant.43.clone.1), dimensions={1}, to_apply=%region_12.13 | reduce | flops 393216 | bytes 2359298 | tf_op jit(solution)/shard_map/reduce_sum | solution.py:158
  311.7 40.2 %reduce-scatter.4.cloned.1.call-done = bf16[512,768]{1,0:T(8,128)(2,1)} async-done(((bf16[2048,768]{1,0:T(8,128)(2,1)}), bf16[512,768]{1,0:T(8,128)(2,1)}) %reduce-scatter.4.cloned.1.call-update) | async-done | bytes 786448 | tf_op jit(solution)/shard_map/reduce_scatter | solution.py:162
  (95 shorter events, 12.9 us)
Async XLA Ops:
  7.2 12.8 %copy-start = (bf16[192,2048]{1,0:T(8,128)(2,1)S(1)}, bf16[192,2048]{1,0:T(8,128)(2,1)}, u32[]{:S(2)}) copy-start(bf16[192,2048]{1,0:T(8,128)(2,1)} %param.11) | copy-start | bytes 2359300
  10.9 24.9 %all-to-all-start = ((s32[4,1,1]{2,1,0:T(1,128)}), s32[4,1,1]{2,1,0:T(1,128)S(1)}, u32[]{:S(2)}, u32[]{:S(2)}) async-start(s32[4,1,1]{2,1,0:T(1,128)} %copy.30), calls=%async_computation | async-start | bytes 4096 | tf_op jit(solution)/shard_map/all_to_all | solution.py:74
  20.0 3.3 copy-start.2
  66.0 30.2 %all-to-all-start.1 = ((bf16[4,128,2048]{2,1,0:T(8,128)(2,1)}), bf16[4,128,2048]{2,1,0:T(8,128)(2,1)}, u32[]{:S(2)}, u32[]{:S(2)}) async-start(bf16[4,128,2048]{2,1,0:T(8,128)(2,1)} %get-tuple-element.212), calls=%async_computation.1 | async-start | bytes 4194304 | tf_op jit(solution)/shard_map/all_to_all | solution.py:117
  70.5 241.2 %reduce-scatter.8.cloned.1.call-start = ((), (), s32[]{:S(2)}) async-start(), calls=%async_computation.10 | async-start | bytes 3932160 | tf_op jit(solution)/shard_map/reduce_scatter | solution.py:168
  107.3 3.0 copy-start.4
  110.3 3.3 copy-start.7
  115.0 3.0 copy-start.4
  118.0 3.3 copy-start.7
  122.7 3.0 copy-start.4
  125.7 3.3 copy-start.7
  135.8 175.9 %reduce-scatter.6.cloned.1.call-start = ((), (), s32[]{:S(2)}) async-start(), calls=%async_computation.9 | async-start | bytes 3932160 | tf_op jit(solution)/shard_map/reduce_scatter | solution.py:165
  143.7 3.5 copy-start.5
  147.2 1.9 copy-start.3
  149.1 2.1 copy-start.8
  149.1 8.7 %slice-start = ((s8[6291456]{0:T(1024)(128)(4,1)}), s8[2097152]{0:T(1024)(128)(4,1)S(1)}, s32[]{:S(2)}) async-start(s8[6291456]{0:T(1024)(128)(4,1)} %bitcast.76), calls=%async_computation.11 | async-start | bytes 4194304 | tf_op jit(solution)/shard_map/while
  151.2 6.6 %slice-start.1 = ((s8[6291456]{0:T(1024)(128)(4,1)}), s8[4194304]{0:T(1024)(128)(4,1)S(1)}, s32[]{:S(2)}) async-start(s8[6291456]{0:T(1024)(128)(4,1)} %bitcast.76), calls=%async_computation.12 | async-start | bytes 8388608 | tf_op jit(solution)/shard_map/while
  159.1 2.6 copy-start.6
  161.7 3.5 copy-start.5
  165.2 1.9 copy-start.3
  167.1 2.0 copy-start.8
  167.1 8.6 %slice-start = ((s8[6291456]{0:T(1024)(128)(4,1)}), s8[2097152]{0:T(1024)(128)(4,1)S(1)}, s32[]{:S(2)}) async-start(s8[6291456]{0:T(1024)(128)(4,1)} %bitcast.76), calls=%async_computation.11 | async-start | bytes 4194304 | tf_op jit(solution)/shard_map/while
  169.1 6.6 %slice-start.1 = ((s8[6291456]{0:T(1024)(128)(4,1)}), s8[4194304]{0:T(1024)(128)(4,1)S(1)}, s32[]{:S(2)}) async-start(s8[6291456]{0:T(1024)(128)(4,1)} %bitcast.76), calls=%async_computation.12 | async-start | bytes 8388608 | tf_op jit(solution)/shard_map/while
  177.0 2.6 copy-start.6
  179.6 3.5 copy-start.5
  183.1 1.9 copy-start.3
  185.0 2.0 copy-start.8
  185.0 8.6 %slice-start = ((s8[6291456]{0:T(1024)(128)(4,1)}), s8[2097152]{0:T(1024)(128)(4,1)S(1)}, s32[]{:S(2)}) async-start(s8[6291456]{0:T(1024)(128)(4,1)} %bitcast.76), calls=%async_computation.11 | async-start | bytes 4194304 | tf_op jit(solution)/shard_map/while
  187.0 6.6 %slice-start.1 = ((s8[6291456]{0:T(1024)(128)(4,1)}), s8[4194304]{0:T(1024)(128)(4,1)S(1)}, s32[]{:S(2)}) async-start(s8[6291456]{0:T(1024)(128)(4,1)} %bitcast.76), calls=%async_computation.12 | async-start | bytes 8388608 | tf_op jit(solution)/shard_map/while
  194.9 2.6 copy-start.6
  202.3 149.7 %reduce-scatter.4.cloned.1.call-start = ((), (), s32[]{:S(2)}) async-start(), calls=%async_computation.8 | async-start | bytes 3932160 | tf_op jit(solution)/shard_map/reduce_scatter | solution.py:162
  213.4 52.4 %all-to-all-start.4 = ((bf16[4,128,2048]{2,1,0:T(8,128)(2,1)}), bf16[4,128,2048]{2,1,0:T(8,128)(2,1)}, u32[]{:S(2)}, u32[]{:S(2)}) async-start(bf16[4,128,2048]{2,1,0:T(8,128)(2,1)} %bitcast.83), calls=%async_computation.4 | async-start | bytes 4194304 | tf_op jit(solution)/shard_map/all_to_all | solution.py:105
  265.9 30.5 %all-to-all-start.3 = ((bf16[4,128,2048]{2,1,0:T(8,128)(2,1)}), bf16[4,128,2048]{2,1,0:T(8,128)(2,1)}, u32[]{:S(2)}, u32[]{:S(2)}) async-start(bf16[4,128,2048]{2,1,0:T(8,128)(2,1)} %bitcast.82), calls=%async_computation.3 | async-start | bytes 4194304 | tf_op jit(solution)/shard_map/all_to_all | solution.py:150
  296.4 55.6 %copy-start.1 = (bf16[192,2048]{1,0:T(8,128)(2,1)S(1)}, bf16[192,2048]{1,0:T(8,128)(2,1)}, u32[]{:S(2)}) copy-start(bf16[192,2048]{1,0:T(8,128)(2,1)} %param.11) | copy-start | bytes 2359300
Sparse Core Ops, SparseCore 0:
  135.9 68.4 reduce-scatter.7
  207.3 81.3 reduce-scatter.5
  291.6 60.2 reduce-scatter.3
where the time goes:
time: 365 us; the launch traced here: 359 us
  local copies, waits for them, and re-layouts  91.1 us (25%)
  waiting for transfers between devices  80.5 us (22%)
  matrix products  68.9 us (19%)
  starting transfers between devices  40.6 us (11%)
  other arithmetic  32.1 us (9%)
  blocking collectives  30.2 us (8%)
  between operations  15 us (4%)
    reduce_scatter x1, waiting for transfers between devices, on_device(): lax.psum_scatter(acc_gate.astype(jnp.bfloat16), 'dp', scatter_dimension=0...  40.2 us
    all_to_all x1, blocking collectives, on_device(): lax.all_to_all(outbound.reshape(expert_count, capacity, features), 'exper...  30.2 us
    all_to_all x1, starting transfers between devices, on_device(): lax.all_to_all(results.reshape(expert_count, capacity, features), 'expert...  26.9 us
    dot_general x3, matrix products, backward_rows(): grad_u = jnp.dot(x_block.T, up_pre_grad, preferred_element_type=jnp.float32)  19.8 us
    all_to_all x1, waiting for transfers between devices, on_device(): lax.all_to_all(results.reshape(expert_count, capacity, features), 'expert...  19.4 us
    all_to_all x1, waiting for transfers between devices, on_device(): lax.all_to_all(grad_out.reshape(expert_count, capacity, features), 'exper...  13.1 us
    while x48, local copies, waits for them, and re-layouts  10.8 us
    another operation x6, local copies, waits for them, and re-layouts  10.6 us
  transfers between devices with their start and end apart: 7, of which 4 were waited for; matrix products, arithmetic and copies ran while one was open for 39% of the time, Pallas kernels for 0%

commit v1 on v0

v1 whole, which is shorter than its diff:
```python
import jax
import jax.numpy as jnp
from jax import lax
from jax.sharding import PartitionSpec as P

BF = jnp.bfloat16
F32 = jnp.float32


def dot(a, b, ca, cb):
    return lax.dot_general(a, b, (((ca,), (cb,)), ((), ())), preferred_element_type=F32)


def core_swap(x, experts):
    return lax.ppermute(x, "expert", [(i, i ^ 1) for i in range(experts)])


def chip_shift(x, experts, k):
    return lax.ppermute(x, "expert", [((i + 2 * k) % experts, i) for i in range(experts)])


def gather_blocks(x, experts):
    blocks = []
    for k in range(experts // 2):
        mine = x if k == 0 else chip_shift(x, experts, k)
        blocks += [mine, core_swap(mine, experts)]
    return jnp.concatenate(blocks, axis=0)


def return_blocks(x, experts, tok_count):
    chips = experts // 2
    x = x.reshape(chips, 2, tok_count, -1)
    other = core_swap(x[:, 1], experts)
    pair = (x[:, 0].astype(F32) + other.astype(F32)).astype(x.dtype)
    total = pair[0].astype(F32)
    for k in range(1, chips):
        total = total + chip_shift(pair[k], experts, chips - k).astype(F32)
    return total


def on_device(tokens, expert_ids, gate_weights, out_grad, w_gate, w_up, w_down):
    tok_count, pick_width = expert_ids.shape
    experts = lax.axis_size("expert")
    me = lax.axis_index("expert")
    gate_w, up_w, down_w = w_gate[0], w_up[0], w_down[0]

    routing = jnp.concatenate([expert_ids.astype(F32), gate_weights], axis=1)
    routing = gather_blocks(routing, experts)
    x = gather_blocks(tokens, experts)
    og = gather_blocks(out_grad, experts)

    chosen = routing[:, :pick_width] == me.astype(F32)
    weight = jnp.sum(jnp.where(chosen, routing[:, pick_width:], 0.0), axis=1, keepdims=True)

    gate_pre = dot(x, gate_w, 1, 0)
    up_pre = dot(x, up_w, 1, 0)
    sigmoid = jax.nn.sigmoid(gate_pre)
    activated = gate_pre * sigmoid
    hidden = activated * up_pre
    hidden_scaled = (hidden * weight).astype(BF)
    raw = dot(og, down_w, 1, 1)
    gate_sum = jnp.sum(hidden.astype(BF).astype(F32) * raw, axis=1, keepdims=True)
    hidden_grad = raw * weight
    gate_pre_grad = (hidden_grad * up_pre * (sigmoid * (1.0 + gate_pre * (1.0 - sigmoid)))).astype(BF)
    up_pre_grad = (hidden_grad * activated).astype(BF)

    grad_d = dot(hidden_scaled, og, 0, 0).astype(BF)
    grad_g = dot(x, gate_pre_grad, 0, 0).astype(BF)
    grad_u = dot(x, up_pre_grad, 0, 0).astype(BF)
    down_share = lax.psum_scatter(grad_d, "dp", scatter_dimension=1, tiled=True)
    gate_share = lax.psum_scatter(grad_g, "dp", scatter_dimension=0, tiled=True)
    up_share = lax.psum_scatter(grad_u, "dp", scatter_dimension=0, tiled=True)

    input_grad = (dot(gate_pre_grad, gate_w, 1, 1) + dot(up_pre_grad, up_w, 1, 1)).astype(BF)
    token_grads = return_blocks(input_grad, experts, tok_count).astype(BF)
    gate_grads = return_blocks(jnp.where(chosen, gate_sum, 0.0), experts, tok_count)
    return (
        token_grads,
        gate_grads,
        gate_share[None],
        up_share[None],
        down_share[None],
    )


def solution(mesh):
    rows = P(("groups", "expert", "dp"), None)
    weights = P("expert", None, None)
    return jax.shard_map(
        on_device,
        mesh=mesh,
        in_specs=(rows, rows, rows, rows, weights, weights, weights),
        out_specs=(
            rows,
            rows,
            P(("groups", "expert"), "dp", None),
            P(("groups", "expert"), "dp", None),
            P(("groups", "expert"), None, "dp"),
        ),
        check_vma=False,
    )
```

time: 365 us -> 267 us (0.73); the launches traced: 359 us -> 267 us
  waiting for transfers between devices: 80.5 us -> 180 us
  local copies, waits for them, and re-layouts: 91.1 us -> 19.3 us
  starting transfers between devices: 40.6 us -> 8.75 us
  matrix products: 68.9 us -> 38.5 us
  blocking collectives: 30.2 us -> 0 us
  other arithmetic: 32.1 us -> 5.7 us
    reduce_scatter x3, waiting for transfers between devices: 40.2 us -> 129 us  [the longest x1 63.2 us: on_device(): gate_share = lax.psum_scatter(grad_g, 'dp', scatter_dimension=0, tiled=True)]
    ppermute x0 -> x13, waiting for transfers between devices: none -> 51 us  [the longest x5 46.1 us: chip_shift(): lax.ppermute(x, 'expert', [((i + 2 * k) % experts, i) for i in range(expe...]
    gather x8 -> x0, local copies, waits for them, and re-layouts: 40.9 us -> none  [the longest x2 10.2 us: on_device(): input_back.reshape(slot_total, features)[position].astype(jnp.float32)]
    all_to_all x4 -> x0, starting transfers between devices: 40.3 us -> none  [the longest x1 26.9 us: on_device(): lax.all_to_all(results.reshape(expert_count, capacity, features), 'expert...]
    all_to_all x4 -> x0, waiting for transfers between devices: 40.2 us -> none  [the longest x1 19.4 us: on_device(): lax.all_to_all(results.reshape(expert_count, capacity, features), 'expert...]
    dot_general x25 -> x8, matrix products: 68.9 us -> 38.5 us  [dot(): lax.dot_general(a, b, (((ca,), (cb,)), ((), ())), preferred_element_type=...]
    all_to_all x1 -> x0, blocking collectives: 30.2 us -> none  [on_device(): lax.all_to_all(outbound.reshape(expert_count, capacity, features), 'exper...]
    scatter x3 -> x0, local copies, waits for them, and re-layouts: 15.3 us -> none  [the longest x1 6.2 us: on_device(): jnp.zeros((slot_total, features), jnp.bfloat16).at[row_order].set(out_buf)]
  transfers between devices with their start and end apart: 7 -> 16, of which waited for: 4 -> 7; matrix products, arithmetic and copies ran while one was open for 39% -> 20% of each run, Pallas kernels for 0% -> 0%
where the time goes in v1:
time: 267 us
  waiting for transfers between devices  180 us (67%)
  matrix products  38.5 us (14%)
  local copies, waits for them, and re-layouts  19.3 us (7%)
  between operations  14 us (5%)
  starting transfers between devices  8.75 us (3%)
  other arithmetic  5.7 us (2%)
    reduce_scatter x1, waiting for transfers between devices, on_device(): gate_share = lax.psum_scatter(grad_g, 'dp', scatter_dimension=0, tiled=True)  63.2 us
    reduce_scatter x1, waiting for transfers between devices, on_device(): up_share = lax.psum_scatter(grad_u, 'dp', scatter_dimension=0, tiled=True)  63.2 us
    ppermute x5, waiting for transfers between devices, chip_shift(): lax.ppermute(x, 'expert', [((i + 2 * k) % experts, i) for i in range(expe...  46.1 us
    dot_general x8, matrix products, dot(): lax.dot_general(a, b, (((ca,), (cb,)), ((), ())), preferred_element_type=...  38.5 us
    unnamed x34, local copies, waits for them, and re-layouts  16.8 us
    ppermute x5, starting transfers between devices, chip_shift(): lax.ppermute(x, 'expert', [((i + 2 * k) % experts, i) for i in range(expe...  6.78 us
  transfers between devices with their start and end apart: 16, of which 7 were waited for; matrix products, arithmetic and copies ran while one was open for 20% of the time, Pallas kernels for 0%

profile of v1, /device:TPU:0, one launch (start us, length us, event | category | flops | bytes accessed | tf_op | source)
XLA Modules:
  0.0 266.7 jit_solution(4340939415605218919)
XLA Ops:
  7.2 0.0 copy-start
  7.2 0.0 copy-start.6
  7.2 0.0 reduce-scatter.8.cloned.1.call-start
  7.2 0.5 collective-permute-start.6
  7.8 2.6 collective-permute-start.7
  10.4 0.1 collective-permute-start.1
  10.4 0.7 convert_element_type.57
  11.1 0.7 pad_maximum_fusion.1
  11.8 1.9 collective-permute-start.4
  13.8 0.0 collective-permute-start.3
  13.8 2.1 constant_dynamic-update-slice_fusion.7
  15.8 29.9 %collective-permute-done.4 = f32[192,4]{0,1:T(4,128)S(1)} collective-permute-done((f32[192,4]{0,1:T(4,128)S(1)}, f32[192,4]{0,1:T(4,128)S(1)}, u32[]{:S(2)}, u32[]{:S(2)}) %collective-permute-start.4) | collective-permute-done | bytes 3104 | tf_op jit(solution)/shard_map/ppermute | solution.py:19
  45.7 0.0 collective-permute-start
  45.7 0.0 collective-permute-done.3
  45.7 0.5 collective-permute-start.5
  46.2 2.1 constant_dynamic-update-slice_fusion.3
  48.3 0.1 pad_maximum_fusion
  48.4 0.0 collective-permute-done.7
  48.4 0.1 collective-permute-start.8
  48.5 0.0 collective-permute-done.1
  48.5 0.5 collective-permute-start.2
  49.0 0.0 collective-permute-done.6
  49.0 2.3 constant_dynamic-update-slice_fusion.6
  51.3 2.1 constant_dynamic-update-slice_fusion.5
  53.4 0.0 collective-permute-done
  53.4 1.2 constant_dynamic-update-slice_fusion.2
  54.6 1.2 constant_dynamic-update-slice_fusion.1
  55.8 1.0 constant_dynamic-update-slice_fusion.4
  56.8 4.8 %fusion.3 = f32[768,768]{0,1:T(8,128)S(1)} fusion(bf16[768,2048]{1,0:T(8,128)(2,1)} %constant_dynamic-update-slice_fusion.4, bf16[1,2048,768]{2,1,0:T(8,128)(2,1)S(1)} %copy-done), kind=kOutput, calls=%fused_computation.8 | convolution fusion | flops 2415919104 | bytes 8650752 | tf_op jit(solution)/shard_map/dot_general | solution.py:11
  61.7 2.9 %fusion.6 = f32[768,768]{0,1:T(8,128)S(1)} fusion(bf16[768,2048]{1,0:T(8,128)(2,1)S(1)} %copy-done.2, bf16[1,2048,768]{2,1,0:T(8,128)(2,1)S(1)} %copy-done.7), kind=kOutput, calls=%fused_computation.11 | convolution fusion | flops 2415919104 | bytes 8650752 | tf_op jit(solution)/shard_map/dot_general | solution.py:11
  64.6 0.0 collective-permute-done.2
  64.6 0.1 constant_dynamic-update-slice_fusion
  64.7 1.4 copy-done.10
  66.1 1.7 copy-done.5
  67.7 4.1 %convolution_convert_fusion = bf16[768,2048]{1,0:T(8,128)(2,1)} fusion(bf16[768,2048]{1,0:T(8,128)(2,1)S(1)} %constant_dynamic-update-slice_fusion, f32[768]{0:T(1024)S(1)} %fusion.14, f32[768,768]{0,1:T(8,128)S(1)} %fusion.6, f32[768,768]{0,1:T(8,128)S(1)} %fusion.3), kind=kOutput, calls=%fused_computation.1 | convolution fusion | flops 2421620736 | bytes 11013120 | tf_op jit(solution)/shard_map/dot_general | solution.py:11
  71.9 0.0 reduce-scatter.8.cloned.1.call-update
  71.9 0.2 reduce-scatter.6.cloned.1.call-start
  72.1 8.9 %multiply_reduce_fusion = (f32[768]{0:T(1024)S(1)}, bf16[768,768]{0,1:T(8,128)(2,1)}, bf16[768,768]{0,1:T(8,128)(2,1)S(1)}) fusion(f32[768,768]{0,1:T(8,128)} %copy-done.10, f32[768,768]{0,1:T(8,128)} %copy-done.9, f32[768]{0:T(1024)S(1)} %fusion.14, bf16[768,2048]{1,0:T(8,128)(2,1)} %copy-done.5, bf16[1,768,2048]{2,1,0:T(8,128)(2,1)} %param.13), kind=kOutput, calls=%fused_computation.16 | convolution fusion | flops 2427124992 | bytes 13375488 | tf_op jit(solution)/shard_map/dot_general | solution.py:11
  81.0 1.0 copy-done.11
  82.1 4.1 %convolution_convert_fusion.1 = bf16[2048,768]{1,0:T(8,128)(2,1)} fusion(bf16[768,2048]{1,0:T(8,128)(2,1)S(1)} %copy-done.3, bf16[768,768]{0,1:T(8,128)(2,1)S(1)} %get-tuple-element.7), kind=kOutput, calls=%fused_computation.2 | convolution fusion | flops 2417491968 | bytes 7471104 | tf_op jit(solution)/shard_map/dot_general | solution.py:11
  86.2 0.0 reduce-scatter.6.cloned.1.call-update
  86.2 0.0 reduce-scatter.4.cloned.1.call-start
  86.3 6.6 %convolution_convert_fusion.2 = bf16[2048,768]{1,0:T(8,128)(2,1)} fusion(bf16[768,2048]{1,0:T(8,128)(2,1)} %constant_dynamic-update-slice_fusion.4, bf16[768,768]{0,1:T(8,128)(2,1)} %get-tuple-element.6), kind=kOutput, calls=%fused_computation.3 | convolution fusion | flops 2417491968 | bytes 7471104 | tf_op jit(solution)/shard_map/dot_general | solution.py:11
  92.9 0.0 reduce-scatter.4.cloned.1.call-update
  93.0 0.0 copy-start.8
  93.0 4.1 %fusion.1 = f32[768,2048]{1,0:T(8,128)S(1)} fusion(bf16[768,768]{0,1:T(8,128)(2,1)} %get-tuple-element.6, bf16[1,2048,768]{2,1,0:T(8,128)(2,1)S(1)} %copy-done), kind=kOutput, calls=%fused_computation.6 | convolution fusion | flops 2415919104 | bytes 10616832 | tf_op jit(solution)/shard_map/dot_general | solution.py:11
  97.1 2.9 %add_convert_fusion = bf16[768,2048]{1,0:T(8,128)(2,1)S(1)} fusion(f32[768,2048]{1,0:T(8,128)S(1)} %fusion.1, bf16[768,768]{0,1:T(8,128)(2,1)S(1)} %copy-done.12, bf16[1,2048,768]{2,1,0:T(8,128)(2,1)S(1)} %copy-done.8), kind=kOutput, calls=%fused_computation | convolution fusion | flops 2419064832 | bytes 13762560 | tf_op jit(solution)/shard_map/dot_general | solution.py:11
  100.0 1.7 copy-done.1
  101.7 1.3 slice_bitcast_fusion
  103.0 0.0 collective-permute-start.9
  103.0 0.1 reshape.23
  103.1 3.7 %collective-permute-done.9 = bf16[2,192,2048]{2,1,0:T(8,128)(2,1)} collective-permute-done((bf16[2,192,2048]{2,1,0:T(8,128)(2,1)}, bf16[2,192,2048]{2,1,0:T(8,128)(2,1)}, u32[]{:S(2)}, u32[]{:S(2)}) %collective-permute-start.9) | collective-permute-done | bytes 1572896 | tf_op jit(solution)/shard_map/ppermute | solution.py:15
  106.8 2.5 fusion
  109.3 0.1 slice_bitcast_fusion.2
  109.3 1.8 collective-permute-start.10
  111.1 0.1 collective-permute-start.11
  111.2 1.2 collective-permute-done.11
  112.4 0.4 collective-permute-start.12
  112.7 16.3 %collective-permute-done.12 = f32[192,2]{0,1:T(2,128)S(1)} collective-permute-done((f32[192,2]{0,1:T(2,128)S(1)}, f32[192,2]{0,1:T(2,128)S(1)}, u32[]{:S(2)}, u32[]{:S(2)}) %collective-permute-start.12) | collective-permute-done | bytes 1568 | tf_op jit(solution)/shard_map/ppermute | solution.py:19
  129.0 0.6 fusion.16
  129.6 1.2 fusion.11
  130.7 3.0 %reduce-scatter.8.cloned.1.call-done = bf16[768,512]{1,0:T(8,128)(2,1)} async-done(((bf16[768,2048]{1,0:T(8,128)(2,1)}), bf16[768,512]{1,0:T(8,128)(2,1)}) %reduce-scatter.8.cloned.1.call-update) | async-done | bytes 786448 | tf_op jit(solution)/shard_map/reduce_scatter | solution.py:70
  133.8 63.2 %reduce-scatter.6.cloned.1.call-done = bf16[512,768]{1,0:T(8,128)(2,1)} async-done(((bf16[2048,768]{1,0:T(8,128)(2,1)}), bf16[512,768]{1,0:T(8,128)(2,1)}) %reduce-scatter.6.cloned.1.call-update) | async-done | bytes 786448 | tf_op jit(solution)/shard_map/reduce_scatter | solution.py:72
  197.0 63.2 %reduce-scatter.4.cloned.1.call-done = bf16[512,768]{1,0:T(8,128)(2,1)} async-done(((bf16[2048,768]{1,0:T(8,128)(2,1)}), bf16[512,768]{1,0:T(8,128)(2,1)}) %reduce-scatter.4.cloned.1.call-update) | async-done | bytes 786448 | tf_op jit(solution)/shard_map/reduce_scatter | solution.py:71
  (29 shorter events, 0.1 us)
Async XLA Ops:
  7.2 49.7 %copy-start = (bf16[1,2048,768]{2,1,0:T(8,128)(2,1)S(1)}, bf16[1,2048,768]{2,1,0:T(8,128)(2,1)}, u32[]{:S(2)}) copy-start(bf16[1,2048,768]{2,1,0:T(8,128)(2,1)} %param.11) | copy-start | bytes 9437188
  7.2 41.1 %copy-start.6 = (f32[192,2]{0,1:T(2,128)S(1)}, f32[192,2]{0,1:T(2,128)}, u32[]{:S(2)}) copy-start(f32[192,2]{0,1:T(2,128)} %param.9) | copy-start | bytes 4612
  7.2 126.6 %reduce-scatter.8.cloned.1.call-start = ((), (), s32[]{:S(2)}) async-start(), calls=%async_computation.5 | async-start | bytes 3932160 | tf_op jit(solution)/shard_map/reduce_scatter | solution.py:70
  7.2 41.8 %collective-permute-start.6 = (bf16[192,2048]{1,0:T(8,128)(2,1)}, bf16[192,2048]{1,0:T(8,128)(2,1)}, u32[]{:S(2)}, u32[]{:S(2)}) collective-permute-start(bf16[192,2048]{1,0:T(8,128)(2,1)} %param.7), channel_id=1, source_target_pairs={{0,4},{4,0},{8,12},{12,8},{1,5},{5,1},{9,13},{13,9},{2,6},{6,2},{1... | collective-permute-start | bytes 2359304 | tf_op jit(solution)/shard_map/ppermute | solution.py:15
  7.8 40.7 %collective-permute-start.7 = (bf16[192,2048]{1,0:T(8,128)(2,1)}, bf16[192,2048]{1,0:T(8,128)(2,1)}, u32[]{:S(2)}, u32[]{:S(2)}) collective-permute-start(bf16[192,2048]{1,0:T(8,128)(2,1)} %param.7), channel_id=1, source_target_pairs={{8,0},{12,4},{0,8},{4,12},{9,1},{13,5},{1,9},{5,13},{10,2},{14,6},... | collective-permute-start | bytes 2359304 | tf_op jit(solution)/shard_map/ppermute | solution.py:19
  10.4 38.2 %collective-permute-start.1 = (bf16[192,2048]{1,0:T(8,128)(2,1)}, bf16[192,2048]{1,0:T(8,128)(2,1)}, u32[]{:S(2)}, u32[]{:S(2)}) collective-permute-start(bf16[192,2048]{1,0:T(8,128)(2,1)} %param.10), channel_id=1, source_target_pairs={{8,0},{12,4},{0,8},{4,12},{9,1},{13,5},{1,9},{5,13},{10,2},{14,6},... | collective-permute-start | bytes 2359304 | tf_op jit(solution)/shard_map/ppermute | solution.py:19
  11.8 33.9 %collective-permute-start.4 = (f32[192,4]{0,1:T(4,128)S(1)}, f32[192,4]{0,1:T(4,128)S(1)}, u32[]{:S(2)}, u32[]{:S(2)}) collective-permute-start(f32[192,4]{0,1:T(4,128)S(1)} %pad_maximum_fusion.1), channel_id=1, source_target_pairs={{8,0},{12,4},{0,8},{4,12},{9,1},{13,5},{1,9},{5,13},{10,2},{14,6},... | collective-permute-start | bytes 9224 | tf_op jit(solution)/shard_map/ppermute | solution.py:19
  13.8 32.0 %collective-permute-start.3 = (f32[192,4]{0,1:T(4,128)S(1)}, f32[192,4]{0,1:T(4,128)S(1)}, u32[]{:S(2)}, u32[]{:S(2)}) collective-permute-start(f32[192,4]{0,1:T(4,128)S(1)} %pad_maximum_fusion.1), channel_id=1, source_target_pairs={{0,4},{4,0},{8,12},{12,8},{1,5},{5,1},{9,13},{13,9},{2,6},{6,2},{1... | collective-permute-start | bytes 9224 | tf_op jit(solution)/shard_map/ppermute | solution.py:15
  45.7 7.7 %collective-permute-start = (bf16[192,2048]{1,0:T(8,128)(2,1)}, bf16[192,2048]{1,0:T(8,128)(2,1)}, u32[]{:S(2)}, u32[]{:S(2)}) collective-permute-start(bf16[192,2048]{1,0:T(8,128)(2,1)} %param.10), channel_id=1, source_target_pairs={{0,4},{4,0},{8,12},{12,8},{1,5},{5,1},{9,13},{13,9},{2,6},{6,2},{1... | collective-permute-start | bytes 2359304 | tf_op jit(solution)/shard_map/ppermute | solution.py:15
  45.7 2.6 collective-permute-start.5
  48.3 5.1 %copy-start.4 = (bf16[768,2048]{1,0:T(8,128)(2,1)S(1)}, bf16[768,2048]{1,0:T(8,128)(2,1)}, u32[]{:S(2)}) copy-start(bf16[768,2048]{1,0:T(8,128)(2,1)} %constant_dynamic-update-slice_fusion.3) | copy-start | bytes 9437188
  48.4 7.4 %collective-permute-start.8 = (bf16[192,2048]{1,0:T(8,128)(2,1)}, bf16[192,2048]{1,0:T(8,128)(2,1)S(1)}, u32[]{:S(2)}, u32[]{:S(2)}) collective-permute-start(bf16[192,2048]{1,0:T(8,128)(2,1)} %collective-permute-done.7), channel_id=1, source_target_pairs={{0,4},{4,0},{8,12},{12,8},{1,5},{5,1},{9,13},{13,9},{2,6},{6,2},{1... | collective-permute-start | bytes 2359304 | tf_op jit(solution)/shard_map/ppermute | solution.py:15
  48.5 16.1 %collective-permute-start.2 = (bf16[192,2048]{1,0:T(8,128)(2,1)}, bf16[192,2048]{1,0:T(8,128)(2,1)S(1)}, u32[]{:S(2)}, u32[]{:S(2)}) collective-permute-start(bf16[192,2048]{1,0:T(8,128)(2,1)} %collective-permute-done.1), channel_id=1, source_target_pairs={{0,4},{4,0},{8,12},{12,8},{1,5},{5,1},{9,13},{13,9},{2,6},{6,2},{1... | collective-permute-start | bytes 2359304 | tf_op jit(solution)/shard_map/ppermute | solution.py:15
  56.8 4.8 %copy-start.2 = (bf16[768,2048]{1,0:T(8,128)(2,1)S(1)}, bf16[768,2048]{1,0:T(8,128)(2,1)}, u32[]{:S(2)}) copy-start(bf16[768,2048]{1,0:T(8,128)(2,1)} %constant_dynamic-update-slice_fusion.4) | copy-start | bytes 9437188
  56.8 4.8 %copy-start.7 = (bf16[1,2048,768]{2,1,0:T(8,128)(2,1)S(1)}, bf16[1,2048,768]{2,1,0:T(8,128)(2,1)}, u32[]{:S(2)}) copy-start(bf16[1,2048,768]{2,1,0:T(8,128)(2,1)} %param.12) | copy-start | bytes 9437188
  61.7 3.0 %copy-start.9 = (f32[768,768]{0,1:T(8,128)}, f32[768,768]{0,1:T(8,128)S(1)}, u32[]{:S(2)}) copy-start(f32[768,768]{0,1:T(8,128)S(1)} %fusion.3) | copy-start | bytes 7077892
  64.6 1.5 copy-start.10
  66.1 1.7 copy-start.5
  71.9 125.1 %reduce-scatter.6.cloned.1.call-start = ((), (), s32[]{:S(2)}) async-start(), calls=%async_computation.4 | async-start | bytes 3932160 | tf_op jit(solution)/shard_map/reduce_scatter | solution.py:72
  72.1 10.0 %copy-start.3 = (bf16[768,2048]{1,0:T(8,128)(2,1)S(1)}, bf16[768,2048]{1,0:T(8,128)(2,1)}, u32[]{:S(2)}) copy-start(bf16[768,2048]{1,0:T(8,128)(2,1)} %constant_dynamic-update-slice_fusion.4) | copy-start | bytes 9437188
  81.0 1.1 copy-start.11
  86.2 173.9 %reduce-scatter.4.cloned.1.call-start = ((), (), s32[]{:S(2)}) async-start(), calls=%async_computation.3 | async-start | bytes 3932160 | tf_op jit(solution)/shard_map/reduce_scatter | solution.py:71
  93.0 4.1 %copy-start.8 = (bf16[1,2048,768]{2,1,0:T(8,128)(2,1)S(1)}, bf16[1,2048,768]{2,1,0:T(8,128)(2,1)}, u32[]{:S(2)}) copy-start(bf16[1,2048,768]{2,1,0:T(8,128)(2,1)} %param.12) | copy-start | bytes 9437188
  93.0 4.1 %copy-start.12 = (bf16[768,768]{0,1:T(8,128)(2,1)S(1)}, bf16[768,768]{0,1:T(8,128)(2,1)}, u32[]{:S(2)}) copy-start(bf16[768,768]{0,1:T(8,128)(2,1)} %copy-done.11) | copy-start | bytes 3538948
  100.0 1.7 copy-start.1
  103.0 3.8 %collective-permute-start.9 = (bf16[2,192,2048]{2,1,0:T(8,128)(2,1)}, bf16[2,192,2048]{2,1,0:T(8,128)(2,1)}, u32[]{:S(2)}, u32[]{:S(2)}) collective-permute-start(bf16[2,192,2048]{2,1,0:T(8,128)(2,1)} %slice_bitcast_fusion), channel_id=1, source_target_pairs={{0,4},{4,0},{8,12},{12,8},{1,5},{5,1},{9,13},{13,9},{2,6},{6,2},{1... | collective-permute-start | bytes 4718600 | tf_op jit(solution)/shard_map/ppermute | solution.py:15
  109.3 20.3 %collective-permute-start.10 = (bf16[192,2048]{1,0:T(8,128)(2,1)S(1)}, bf16[192,2048]{1,0:T(8,128)(2,1)S(1)}, u32[]{:S(2)}, u32[]{:S(2)}) collective-permute-start(bf16[192,2048]{1,0:T(8,128)(2,1)S(1)} %slice_bitcast_fusion.2), channel_id=1, source_target_pairs={{8,0},{12,4},{0,8},{4,12},{9,1},{13,5},{1,9},{5,13},{10,2},{14,6},... | collective-permute-start | bytes 2359304 | tf_op jit(solution)/shard_map/ppermute | solution.py:19
  111.1 1.2 collective-permute-start.11
  112.4 16.6 %collective-permute-start.12 = (f32[192,2]{0,1:T(2,128)S(1)}, f32[192,2]{0,1:T(2,128)S(1)}, u32[]{:S(2)}, u32[]{:S(2)}) collective-permute-start(f32[192,2]{0,1:T(2,128)S(1)} %bitcast.66), channel_id=1, source_target_pairs={{8,0},{12,4},{0,8},{4,12},{9,1},{13,5},{1,9},{5,13},{10,2},{14,6},... | collective-permute-start | bytes 4616 | tf_op jit(solution)/shard_map/ppermute | solution.py:19
Sparse Core Ops, SparseCore 0:
  72.0 61.7 reduce-scatter.7
  136.6 60.2 reduce-scatter.5
  199.8 60.2 reduce-scatter.3

commit v2 on v1

v2 whole, which is shorter than its diff:
```python
import functools

import jax
import jax.numpy as jnp
from jax import lax
from jax.experimental import pallas as pl
from jax.experimental.pallas import tpu as pltpu
from jax.sharding import PartitionSpec as P

BF = jnp.bfloat16
F32 = jnp.float32
VMEM_SMALL = 28 * 1024 * 1024
VMEM_LARGE = 28 * 1024 * 1024
COST = pl.CostEstimate(flops=1000, bytes_accessed=1000, transcendentals=0)


def dot(a, b, ca, cb):
    return lax.dot_general(a, b, (((ca,), (cb,)), ((), ())), preferred_element_type=F32)


def send(x, axis, pairs, what):
    with jax.named_scope(what):
        return lax.ppermute(x, axis, pairs)


def core_swap(x, experts, what):
    return send(x, "expert", [(i, i ^ 1) for i in range(experts)], what + "_core")


def chip_shift(x, experts, k, what):
    return send(x, "expert", [((i + 2 * k) % experts, i) for i in range(experts)], what + "_chip")


def gather_pairs(x, experts, what):
    pairs = []
    for k in range(experts // 2):
        mine = x if k == 0 else chip_shift(x, experts, k, what)
        pairs.append((mine, core_swap(mine, experts, what)))
    return pairs


def flat(pairs):
    return [b for pair in pairs for b in pair]


def return_sums(pairs, experts, what):
    return [add(own, core_swap(other, experts, what)) for own, other in pairs]


def return_shift(sums, experts, what):
    chips = experts // 2
    return add(sums[0], *(chip_shift(sums[k], experts, chips - k, what) for k in range(1, chips)))


def add(*terms):
    total = terms[0].astype(F32)
    for t in terms[1:]:
        total = total + t.astype(F32)
    return total.astype(terms[0].dtype)


def line_step(x, step, size, towards, what):
    if towards > 0:
        pairs = [(i, i + 1) for i in range(size - 1) if i >= step]
    else:
        pairs = [(i, i - 1) for i in range(1, size) if size - 1 - i >= step]
    return send(x, "dp", pairs, what + ("_right" if towards > 0 else "_left"))


def rotate(x, k, size, what):
    return send(x, "dp", [(i, (i + k) % size) for i in range(size)], what + "_rotated")


def inward(x, size, what):
    return send(x, "dp", [(0, 1), (size - 1, size - 2)], what + "_inward")


def outward(x, size, what):
    return send(x, "dp", [(1, 0), (size - 2, size - 1)], what + "_outward")


def across(x, what):
    return send(x, "dp", [(1, 2), (2, 1)], what + "_across")


def call(body, name, grid, inputs, outputs, scratch=(), deps=(), limit=VMEM_SMALL):
    def spec(entry):
        if len(entry) == 2:
            return pl.BlockSpec(memory_space=entry[1])
        return pl.BlockSpec(entry[1], entry[2])

    n = len(inputs)

    def kernel(*refs):
        body(*refs[:n], *refs[n + len(deps) :])

    return pl.pallas_call(
        kernel,
        grid=grid,
        in_specs=[spec(e) for e in inputs] + [pl.BlockSpec(memory_space=pl.ANY)] * len(deps),
        out_specs=[pl.BlockSpec(o[2], o[3]) for o in outputs],
        out_shape=[jax.ShapeDtypeStruct(o[0], o[1]) for o in outputs],
        scratch_shapes=list(scratch),
        compiler_params=pltpu.CompilerParams(vmem_limit_bytes=limit),
        cost_estimate=COST,
        name=name,
    )(*[e[0] for e in inputs], *deps)


def whole(a):
    return (a, a.shape, lambda *i: (0,) * a.ndim)


def copies(blocks, target, sem, first=0):
    rows = blocks[0].shape[0]
    return [
        pltpu.make_async_copy(b, target.at[pl.ds(i * rows, rows)], sem.at[first + i])
        for i, b in enumerate(blocks)
    ]


def fetch(*args):
    moves = copies(*args)
    for m in moves:
        m.start()
    for m in moves:
        m.wait()


def turned(a, b):
    rows, cols = a.shape
    tile = 512

    def body(a, b, at, bt):
        at[...] = a[...].T
        bt[...] = b[...].T

    inputs = [(x, (tile, cols), lambda i: (i, 0)) for x in (a, b)]
    outputs = [((cols, rows), a.dtype, (cols, tile), lambda i: (0, i))] * 2
    return call(body, "turned", (rows // tile,), inputs, outputs)


def forward(pair, gate_wt, up_wt, deps=()):
    rows, width = 2 * pair[0].shape[0], pair[0].shape[1]
    units = gate_wt.shape[0]
    tile = 256

    def body(a, b, gate_wt, up_wt, hidden, gate_factor, up_factor, x, sem):
        @pl.when(pl.program_id(0) == 0)
        def _():
            fetch((a, b), x, sem)

        gate_pre = dot(gate_wt[...], x[...], 1, 1)
        up_pre = dot(up_wt[...], x[...], 1, 1)
        sigmoid = jax.nn.sigmoid(gate_pre)
        activated = gate_pre * sigmoid
        hidden[...] = (activated * up_pre).astype(BF)
        gate_factor[...] = up_pre * (sigmoid * (1.0 + gate_pre * (1.0 - sigmoid)))
        up_factor[...] = activated

    at = lambda i: (i, 0)
    return call(
        body,
        "forward",
        (units // tile,),
        [(b, pl.ANY) for b in pair] + [(w, (tile, width), at) for w in (gate_wt, up_wt)],
        [((units, rows), t, (tile, rows), at) for t in (BF, F32, F32)],
        [pltpu.VMEM((rows, width), BF), pltpu.SemaphoreType.DMA((2,))],
        deps,
    )


def backward(pair, down_w, weight, hidden, gate_factor, up_factor, deps=()):
    rows, width = 2 * pair[0].shape[0], pair[0].shape[1]
    units = down_w.shape[0]
    tile = 256

    def body(
        a, b, down_w, weight, hidden, gate_factor, up_factor, gate_grad, up_grad, gate_sum, og, sem
    ):
        step = pl.program_id(0)

        @pl.when(step == 0)
        def _():
            fetch((a, b), og, sem)
            gate_sum[...] = jnp.zeros_like(gate_sum)

        raw = dot(down_w[...], og[...], 1, 1)
        scaled = raw * weight[...]
        gate_grad[...] = (scaled * gate_factor[...]).astype(BF)
        up_grad[...] = (scaled * up_factor[...]).astype(BF)
        gate_sum[...] += jnp.sum(raw * hidden[...].astype(F32), axis=0, keepdims=True)

    at = lambda i: (i, 0)
    tall = (tile, rows)
    return call(
        body,
        "backward",
        (units // tile,),
        [(b, pl.ANY) for b in pair]
        + [(down_w, (tile, width), at), whole(weight)]
        + [(a, tall, at) for a in (hidden, gate_factor, up_factor)],
        [((units, rows), BF, tall, at)] * 2 + [((1, rows), F32, (1, rows), lambda i: (0, 0))],
        [pltpu.VMEM((rows, width), BF), pltpu.SemaphoreType.DMA((2,))],
        deps,
        VMEM_LARGE,
    )


def slots(info, me, count):
    pairs, height, rows = info.shape
    width = height // 2

    def body(me, info, table, weight):
        chosen = info[0, :width] == me[0]
        weight[0] = jnp.sum(jnp.where(chosen, info[0, width:], 0.0), axis=0, keepdims=True)
        picked = jnp.sum(jnp.where(chosen, 1.0, 0.0), axis=0, keepdims=True)
        rank = jnp.broadcast_to(picked, (8, rows))
        lane = lax.broadcasted_iota(jnp.int32, (8, rows), 1)
        step = 1
        while step < rows:
            rank = rank + jnp.where(lane >= step, pltpu.roll(rank, step, 1), 0.0)
            step *= 2
        slot = jnp.where(picked > 0.0, rank[:1] - 1.0, float(count)).astype(jnp.int32)
        row = lax.broadcasted_iota(jnp.int32, (count, rows), 0)
        table[0] = jnp.where(row == slot, 1.0, 0.0).astype(BF)

    at = lambda i: (i, 0, 0)
    return call(
        body,
        "slots",
        (pairs,),
        [(me, pltpu.SMEM), (info, (1, height, rows), at)],
        [
            ((pairs, count, rows), BF, (1, count, rows), at),
            ((pairs, 1, rows), F32, (1, 1, rows), at),
        ],
    )


TAGS = 16


def pack(groups, tables, pairs, weight=None, deps=()):
    units, rows = groups[0][0].shape
    count = tables.shape[1]
    n = len(pairs)
    step = 256 if units % 256 == 0 else units
    inputs = [p for g in groups for p in g] + ([] if weight is None else [weight]) + [tables]

    def body(*refs):
        refs, out = refs[:-1], refs[-1]
        for i, c in enumerate(pairs):
            table = refs[-1][c]
            cols = slice(i * count, (i + 1) * count)
            for j in range(len(groups)):
                for start in range(0, units, step):
                    here = refs[j * n + i][start : start + step]
                    if weight is not None:
                        here = (here.astype(F32) * refs[-2][c]).astype(BF)
                    at = j * units + start
                    out[at : at + step, cols] = dot(here, table, 1, 1).astype(BF)
            token = lax.broadcasted_iota(jnp.int32, (TAGS, rows), 1) + c * rows
            row = lax.broadcasted_iota(jnp.int32, (TAGS, rows), 0)
            token = jnp.where(row == 0, token // 256, jnp.where(row == 1, token % 256, 0))
            tags = dot(token.astype(F32).astype(BF), table, 1, 1)
            out[len(groups) * units :, cols] = tags.astype(BF)

    shape = (len(groups) * units + TAGS, n * count)
    return call(
        body,
        "pack",
        (1,),
        [whole(a) for a in inputs],
        [(shape, BF, shape, lambda i: (0, 0))],
        (),
        deps,
        VMEM_LARGE,
    )[0]


def spread(packed, tags, rows, first=0):
    tags = tags.astype(F32)
    token = (tags[:1] * 256.0 + tags[1:2]).astype(jnp.int32) - first
    row = lax.broadcasted_iota(jnp.int32, (rows, packed.shape[1]), 0)
    table = jnp.where(row == token, 1.0, 0.0).astype(BF)
    return dot(packed, table, 1, 1).astype(BF)


def sum_products(packed, valid, blocks, order, parts, deps=()):
    height, width = blocks[0].shape
    rows, share = height * len(blocks), width // parts
    units = packed[0].shape[0] - TAGS
    m, n = len(packed), len(blocks)

    def body(valid, *refs):
        blocks, packed, (out, total, whole_rows, sem) = refs[:n], refs[n : n + m], refs[n + m :]
        fetch(blocks, whole_rows, sem)
        total[...] = jnp.zeros_like(total)
        for i in range(m):

            @pl.when(valid[i] > 0)
            def _():
                left = spread(packed[i][:units], packed[i][units:], rows)
                cols = slice(order[i] * share, (order[i] + 1) * share)
                total[...] += dot(left, whole_rows[:, cols], 1, 0)

        out[...] = total[...].astype(BF)

    return call(
        body,
        "sum_products",
        (1,),
        [(valid, pltpu.SMEM)] + [(b, pl.ANY) for b in blocks] + [whole(a) for a in packed],
        [((units, share), BF, (units, share), lambda i: (0, 0))],
        [
            pltpu.VMEM((units, share), F32),
            pltpu.VMEM((rows, width), BF),
            pltpu.SemaphoreType.DMA((n,)),
        ],
        deps,
        VMEM_LARGE,
    )[0]


def input_grad(gate_grad, up_grad, gate_wt, up_wt, sums, deps=()):
    units, rows = gate_grad.shape
    width = gate_wt.shape[1]
    tile = 512
    half = rows // 2
    picks = sums.shape[0]

    def body(gate_grad, up_grad, gate_wt, up_wt, sums, own, other, g, u):
        @pl.when(pl.program_id(0) == 0)
        def _():
            g[...] = gate_grad[...].T
            u[...] = up_grad[...].T

        total = dot(g[...], gate_wt[...], 1, 0) + dot(u[...], up_wt[...], 1, 0)
        for i, out in enumerate((own, other)):
            out[:half] = total[i * half : (i + 1) * half].astype(BF)
            out[half:] = jnp.zeros((TAGS, tile), BF)

            @pl.when(pl.program_id(0) == 0)
            def _():
                left = sums[:, i * half : (i + 1) * half]
                parts = []
                for _ in range(3):
                    parts.append(left.astype(BF).astype(F32))
                    left = left - parts[-1]
                parts.append(jnp.zeros((TAGS - 3 * picks, half), F32))
                out[half:, :half] = jnp.concatenate(parts, axis=0).astype(BF)

    at = lambda i: (0, i)
    return call(
        body,
        "input_grad",
        (width // tile,),
        [whole(gate_grad), whole(up_grad)]
        + [(w, (units, tile), at) for w in (gate_wt, up_wt)]
        + [whole(sums)],
        [((half + TAGS, width), BF, (half + TAGS, tile), at)] * 2,
        [pltpu.VMEM((rows, units), BF)] * 2,
        deps,
        VMEM_LARGE,
    )


def weight_grad(x_pairs, grads, shares, replicas, fold=None, deps=()):
    chips = len(x_pairs)
    blocks = flat(x_pairs)
    small = list(grads)
    units, rows = grads[0].shape
    width = blocks[0].shape[1]
    if fold is not None:
        blocks = blocks + flat(fold[0])
        small = small + [fold[1]]
    total = len(blocks) * blocks[0].shape[0]
    share = width // replicas

    def body(shares, *refs):
        blocks_in, refs = refs[: len(blocks)], refs[len(blocks) :]
        small_in, (out, x, g, sem) = refs[: len(small)], refs[len(small) :]
        step = pl.program_id(0)

        @pl.when(step == 0)
        def _():
            moves = copies(blocks_in, x, sem)
            for m in moves:
                m.start()
            for i in range(chips):
                g[:, i * rows : (i + 1) * rows] = small_in[i][...]
            if fold is not None:
                packed = small_in[chips]
                for i in range(chips):
                    part = slice(i * packed.shape[1] // chips, (i + 1) * packed.shape[1] // chips)
                    at = (chips + i) * rows
                    g[:, at : at + rows] = spread(
                        packed[:units, part], packed[units:, part], rows, i * rows
                    )
            for m in moves:
                m.wait()

        cols = pl.ds(pl.multiple_of(shares[step] * share, share), share)
        out[0] = dot(g[...], x[:, cols], 1, 0).astype(BF)

    n = shares.shape[0]
    return call(
        body,
        "weight_grad",
        (n,),
        [(shares, pltpu.SMEM)] + [(b, pl.ANY) for b in blocks] + [whole(a) for a in small],
        [((n, units, share), BF, (1, units, share), lambda i: (i, 0, 0))],
        [
            pltpu.VMEM((total, width), BF),
            pltpu.VMEM((units, total), BF),
            pltpu.SemaphoreType.DMA((len(blocks),)),
        ],
        deps,
        VMEM_LARGE,
    )[0]


def on_device(tokens, expert_ids, gate_weights, out_grad, w_gate, w_up, w_down):
    tok_count, pick_width = expert_ids.shape
    experts, replicas = lax.axis_size("expert"), lax.axis_size("dp")
    chips = experts // 2
    me, z = lax.axis_index("expert").astype(F32).reshape(1), lax.axis_index("dp")
    down_w = w_down[0]
    width = tokens.shape[1]
    share = width // replicas
    capacity = 4 * tok_count * pick_width // (3 * experts)
    count = experts * capacity
    pair_rows = 2 * tok_count
    folding = replicas == 4
    pairs = list(range(chips))
    meet = lax.optimization_barrier

    x_core = core_swap(tokens, experts, "tokens")
    x_fold = inward(tokens, replicas, "tokens") if folding else tokens
    x_far = [chip_shift(tokens, experts, k, "tokens") for k in range(1, chips)]
    info = jnp.concatenate([expert_ids.T.astype(F32), gate_weights.T], axis=0)
    info_far = [chip_shift(info, experts, k, "routing") for k in range(1, chips)]
    og_shares = []
    for k in range(replicas):
        part = lax.dynamic_slice_in_dim(out_grad, (z + k) % replicas * share, share, 1)
        og_shares.append(rotate(part, k, replicas, "out_grad_share") if k else part)
    gate_wt, up_wt = turned(w_gate[0], w_up[0])
    fwd = [forward((tokens, x_core), gate_wt, up_wt)]
    x_far, info, info_far, x_fold, out_grad, gate_wt, up_wt, fwd = meet(
        (x_far, info, info_far, x_fold, out_grad, gate_wt, up_wt, fwd)
    )

    og_core = core_swap(out_grad, experts, "out_grad")
    og_far = [chip_shift(out_grad, experts, k, "out_grad") for k in range(1, chips)]
    x = [(tokens, x_core)] + [(b, core_swap(b, experts, "tokens")) for b in x_far]
    info = [(b, core_swap(b, experts, "routing")) for b in (info, *info_far)]
    info = jnp.stack([jnp.concatenate(pair, axis=1) for pair in info])
    fwd += [forward(pair, gate_wt, up_wt) for pair in x[1:]]
    tables, weights = slots(info, me, count // chips)
    packed = pack([[f[0] for f in fwd]], tables, pairs, weights)
    right = [line_step(packed, 0, replicas, 1, "hidden")]
    left = [line_step(packed, 0, replicas, -1, "hidden")]
    og_far, og_core, og_shares, fwd, tables, weights, x, x_fold, info = meet(
        (og_far, og_core, og_shares, fwd, tables, weights, x, x_fold, info)
    )

    def onward(t):
        right.append(line_step(right[-1], t, replicas, 1, "hidden"))
        left.append(line_step(left[-1], t, replicas, -1, "hidden"))

    bwd = [backward((out_grad, og_core), down_w, weights[0], *fwd[0])]
    for c in range(1, chips):
        pair = (og_far[c - 1], core_swap(og_far[c - 1], experts, "out_grad"))
        bwd.append(backward(pair, down_w, weights[c], *fwd[c]))
    gate_grad, up_grad = [b[0] for b in bwd], [b[1] for b in bwd]
    og_rows = jnp.concatenate(og_shares, axis=1)

    def input_grads(deps=()):
        halves = []
        for c, (gate, up, sums) in enumerate(bwd):
            sums = jnp.where(info[c, :pick_width] == me, sums, 0.0)
            halves.append(input_grad(gate, up, gate_wt, up_wt, sums, deps))
        return halves

    def grad_down(og_rows):
        gathered, blocks, valid = [packed], [0], [z >= 0]
        for t in range(replicas - 1):
            gathered += [right[t], left[t]]
            blocks += [t + 1, replicas - 1 - t]
            valid += [z - 1 - t >= 0, z + 1 + t < replicas]
        valid = jnp.stack(valid).astype(jnp.int32)
        return sum_products(gathered, valid, flat(og_rows), blocks, replicas)

    if folding:
        x_there = [chip_shift(x_fold, experts, k, "tokens_fold") for k in range(1, chips)]
        gate_packed = pack([gate_grad], tables, pairs)
        up_packed = pack([up_grad], tables, pairs, None, [gate_packed])
        gate_there = inward(gate_packed, replicas, "gate_grad")
        up_there = inward(up_packed, replicas, "up_grad")
        right, left, bwd, gate_grad, up_grad, og_rows, x_there = meet(
            (right, left, bwd, gate_grad, up_grad, og_rows, x_there)
        )

        onward(1)
        x_there = [(b, core_swap(b, experts, "tokens_fold")) for b in [x_fold, *x_there]]
        og_rows = [og_rows, *(chip_shift(og_rows, experts, k, "out_grad_share") for k in range(1, chips))]
        gate_there, x_there, gate_grad = meet((gate_there, x_there, gate_grad))

        order = jnp.where(z < 2, jnp.arange(3, -1, -1), jnp.arange(4)).astype(jnp.int32)
        gate_sent = weight_grad(x, gate_grad, order[:2], replicas, (x_there, gate_there))
        gate_met = across(gate_sent, "gate_sums")
        og_rows = [(b, core_swap(b, experts, "out_grad_share")) for b in og_rows]
        up_there, gate_sent, gate_there, x_there, gate_grad, up_grad, right, left = meet(
            (up_there, gate_sent, gate_there, x_there, gate_grad, up_grad, right, left)
        )

        up_sent = weight_grad(x, up_grad, order[:2], replicas, (x_there, up_there))
        up_met = [across(up_sent[0], "up_far_sums"), across(up_sent[1], "up_sums")]
        gate_kept = weight_grad(x, gate_grad, order[2:], replicas, (x_there, gate_there), [up_sent])
        up_kept = weight_grad(x, up_grad, order[2:], replicas, (x_there, up_there), [gate_kept])
        onward(2)
        halves = input_grads([up_kept])
        gate_met, gate_kept, up_kept, halves, og_rows, right, left = meet(
            (gate_met, gate_kept, up_kept, halves, og_rows, right, left)
        )

        gate_far = outward(add(gate_kept[1], gate_met[0]).T, replicas, "gate_sums")
        gate_own = add(gate_kept[0], gate_met[1]).T
        sums = return_sums(halves, experts, "token_grads")
        down = grad_down(og_rows)
        up_met[0], up_kept, gate_own, sums, down = meet(
            (up_met[0], up_kept, gate_own, sums, down)
        )

        outer = (z == 0) | (z == replicas - 1)
        up_far = outward(add(up_kept[1], up_met[0]).T, replicas, "up_sums")
        grads = return_shift(sums, experts, "token_grads")
        gate_share = jnp.where(outer, gate_far, gate_own)
        up_share = jnp.where(outer, up_far, add(up_kept[0], up_met[1]).T)
    else:
        every = jnp.arange(replicas, dtype=jnp.int32)

        def scatter(grads):
            total = weight_grad(x, grads, every, replicas)
            return lax.psum_scatter(total, "dp", scatter_dimension=0, tiled=True)[0].T

        gate_share, up_share = scatter(gate_grad), scatter(up_grad)
        for t in range(1, replicas - 1):
            onward(t)
        grads = return_shift(return_sums(input_grads(), experts, "token_grads"), experts, "token_grads")
        down = grad_down(gather_pairs(og_rows, experts, "out_grad_share"))
    token_grads = grads[:tok_count]
    sums = grads[tok_count:, :tok_count].astype(F32)
    gate_grads = sum(sums[i * pick_width : (i + 1) * pick_width] for i in range(3)).T
    return (
        token_grads,
        gate_grads,
        gate_share[None],
        up_share[None],
        down[None],
    )


def solution(mesh):
    rows = P(("groups", "expert", "dp"), None)
    weights = P("expert", None, None)
    return jax.shard_map(
        on_device,
        mesh=mesh,
        in_specs=(rows, rows, rows, rows, weights, weights, weights),
        out_specs=(
            rows,
            rows,
            P(("groups", "expert"), "dp", None),
            P(("groups", "expert"), "dp", None),
            P(("groups", "expert"), None, "dp"),
        ),
        check_vma=False,
    )
```

time: 267 us -> 210 us (0.79)
  waiting for transfers between devices: 180 us -> 37.7 us
  Pallas kernels: 0 us -> 70.9 us
  starting transfers between devices: 8.75 us -> 52 us
  matrix products: 38.5 us -> 0 us
  between operations: 14 us -> 1.35 us
  local copies, waits for them, and re-layouts: 19.3 us -> 30.6 us
  other arithmetic: 5.7 us -> 16.3 us
    reduce_scatter x3 -> x0, waiting for transfers between devices: 129 us -> none  [the longest x1 63.2 us: on_device(): gate_share = lax.psum_scatter(grad_g, 'dp', scatter_dimension=0, tiled=True)]
    pallas_call x0 -> x16, Pallas kernels: none -> 70.9 us  [call(): pl.pallas_call(kernel, grid=grid, in_specs=[spec(e) for e in inputs] + [p...]
    ppermute x13 -> x35, starting transfers between devices: 8.44 us -> 52 us  [send(): return lax.ppermute(x, axis, pairs)]
    dot_general x8 -> x0, matrix products: 38.5 us -> none  [dot(): lax.dot_general(a, b, (((ca,), (cb,)), ((), ())), preferred_element_type=...]
    ppermute x13 -> x35, waiting for transfers between devices: 51 us -> 37.7 us  [send(): return lax.ppermute(x, axis, pairs)]
    unnamed x34 -> x114, local copies, waits for them, and re-layouts: 16.8 us -> 25 us
    transpose x0 -> x3, other arithmetic: none -> 4.66 us  [the longest x1 2.96 us: on_device(): gate_far = outward(add(gate_kept[1], gate_met[0]).T, replicas, 'gate_sums')]
    broadcast_in_dim x0 -> x2, other arithmetic: none -> 2.9 us  [the longest x1 1.68 us: on_device(): up_share[None]]
  transfers between devices with their start and end apart: 16 -> 35, of which waited for: 7 -> 10; matrix products, arithmetic and copies ran while one was open for 20% -> 10% of each run, Pallas kernels for 0% -> 34%
where the time goes in v2:
time: 210 us; the launch traced here: 209 us
  Pallas kernels  70.9 us (34%)
  starting transfers between devices  52 us (25%)
  waiting for transfers between devices  37.7 us (18%)
  local copies, waits for them, and re-layouts  30.6 us (15%)
  other arithmetic  16.3 us (8%)
    pallas_call x16, Pallas kernels, call(): pl.pallas_call(kernel, grid=grid, in_specs=[spec(e) for e in inputs] + [p...  70.9 us
    ppermute x35, starting transfers between devices, send(): return lax.ppermute(x, axis, pairs)  52 us
    ppermute x35, waiting for transfers between devices, send(): return lax.ppermute(x, axis, pairs)  37.7 us
    unnamed x114, local copies, waits for them, and re-layouts  25 us
    convert_element_type x3, other arithmetic, add(): return total.astype(terms[0].dtype)  5.2 us
  transfers between devices with their start and end apart: 35, of which 10 were waited for; matrix products, arithmetic and copies ran while one was open for 10% of the time, Pallas kernels for 34%

profile of v2, /device:TPU:0, one launch (start us, length us, event | category | flops | bytes accessed | tf_op | source)
XLA Modules:
  0.0 208.9 jit_solution(10588819505660489313)
XLA Ops:
  1.1 2.6 %collective-permute-start = (bf16[192,2048]{1,0:T(8,128)(2,1)}, bf16[192,2048]{1,0:T(8,128)(2,1)}, u32[]{:S(2)}, u32[]{:S(2)}) collective-permute-start(bf16[192,2048]{1,0:T(8,128)(2,1)} %refs_1_.3), channel_id=1, source_target_pairs={{8,0},{12,4},{0,8},{4,12},{9,1},{13,5},{1,9},{5,13},{10,2},{14,6},... | collective-permute-start | bytes 2359304 | tf_op jit(solution)/shard_map/tokens_chip/ppermute | solution.py:23
  3.7 4.4 %collective-permute-start.2 = (bf16[192,2048]{1,0:T(8,128)(2,1)}, bf16[192,2048]{1,0:T(8,128)(2,1)}, u32[]{:S(2)}, u32[]{:S(2)}) collective-permute-start(bf16[192,2048]{1,0:T(8,128)(2,1)} %refs_1_.3), channel_id=1, source_target_pairs={{0,1},{3,2},{4,5},{7,6},{8,9},{11,10},{12,13},{15,14},{16,17},{19,... | collective-permute-start | bytes 2359304 | tf_op jit(solution)/shard_map/tokens_inward/ppermute | solution.py:23
  10.0 1.9 copy-done.34
  11.9 1.9 copy-done.35
  13.8 2.3 %turned.1 = (bf16[768,2048]{1,0:T(8,128)(2,1)S(1)}, bf16[768,2048]{1,0:T(8,128)(2,1)S(1)}) custom-call(bf16[2048,768]{1,0:T(8,128)(2,1)S(1)} %bitcast.61, bf16[2048,768]{1,0:T(8,128)(2,1)S(1)} %bitcast.62), custom_call_target="tpu_custom_call" | custom-call | flops 1000 | bytes 1000 | tf_op jit(solution)/shard_map/turned/pallas_call | solution.py:97
  16.1 4.0 %forward.2 = (bf16[768,384]{1,0:T(8,128)(2,1)S(1)}, f32[768,384]{1,0:T(8,128)S(1)}, f32[768,384]{1,0:T(8,128)S(1)}) custom-call(bf16[192,2048]{1,0:T(8,128)(2,1)S(1)} %copy-done.5, bf16[192,2048]{1,0:T(8,128)(2,1)S(1)} %collective-permute-done.3.refs_1_.refs_2_, bf16[768,2048]{1,0:T(8,128)(2,1)S(1)} %get-tuple-element.123.refs_2_, ...), custom_call_target="tpu_custom_call" | custom-call | flops 1000 | bytes 1000 | tf_op jit(solution)/shard_map/forward/pallas_call | solution.py:97
  21.0 1.1 copy-done.38
  22.0 1.1 copy-done.40
  23.1 1.5 collective-permute-done.2.refs_5_
  25.7 2.1 %constant_dynamic-slice_fusion = (bf16[192,512]{1,0:T(8,128)(2,1)}, bf16[192,512]{1,0:T(8,128)(2,1)}, bf16[192,512]{1,0:T(8,128)(2,1)}, bf16[192,512]{1,0:T(8,128)(2,1)}) fusion(bf16[192,2048]{1,0:T(8,128)(2,1)} %refs_0_.2, s32[]{:T(128)S(6)} %select_n.67, s32[]{:T(128)S(6)} %select_n.63, s32[]{:T(128)S(6)} %select_n.61, s32[]{:T(128)S(6)} %select_n.65), kind=kLoop, calls=%fused_computation.32 | loop fusion | bytes 1572880 | tf_op jit(solution)/shard_map/dynamic_slice | solution.py:446
  27.8 2.5 %collective-permute-start.6 = (bf16[192,512]{1,0:T(8,128)(2,1)}, bf16[192,512]{1,0:T(8,128)(2,1)}, u32[]{:S(2)}, u32[]{:S(2)}) collective-permute-start(bf16[192,512]{1,0:T(8,128)(2,1)} %get-tuple-element.231), channel_id=1, source_target_pairs={{0,1},{1,2},{2,3},{3,0},{4,5},{5,6},{6,7},{7,4},{8,9},{9,10},{10,1... | collective-permute-start | bytes 589832 | tf_op jit(solution)/shard_map/out_grad_share_rotated/ppermute | solution.py:23
  30.3 1.1 collective-permute-done.11
  31.4 1.1 collective-permute-start.7
  32.5 2.9 %collective-permute-start.8 = (bf16[192,512]{1,0:T(8,128)(2,1)}, bf16[192,512]{1,0:T(8,128)(2,1)S(1)}, u32[]{:S(2)}, u32[]{:S(2)}) collective-permute-start(bf16[192,512]{1,0:T(8,128)(2,1)} %get-tuple-element.230), channel_id=1, source_target_pairs={{0,3},{1,0},{2,1},{3,2},{4,7},{5,4},{6,5},{7,6},{8,11},{9,8},{10,9... | collective-permute-start | bytes 589832 | tf_op jit(solution)/shard_map/out_grad_share_rotated/ppermute | solution.py:23
  35.5 1.2 slots.1
  36.7 1.9 copy-done.1
  38.5 5.4 %forward.3 = (bf16[768,384]{1,0:T(8,128)(2,1)S(1)}, f32[768,384]{1,0:T(8,128)S(1)}, f32[768,384]{1,0:T(8,128)S(1)}) custom-call(bf16[192,2048]{1,0:T(8,128)(2,1)} %collective-permute-done.refs_0_.refs_3_, bf16[192,2048]{1,0:T(8,128)(2,1)} %collective-permute-done.9.refs_1_.refs_4_, bf16[768,2048]{1,0:T(8,128)(2,1)S(1)} %get-tuple-element.123.refs_2_, ...), custom_call_target="tpu_custom_call" | custom-call | flops 1000 | bytes 1000 | tf_op jit(solution)/shard_map/forward/pallas_call | solution.py:97
  44.0 1.4 collective-permute-done.7
  46.2 6.6 %collective-permute-start.16 = (bf16[784,512]{1,0:T(8,128)(2,1)S(1)}, bf16[784,512]{1,0:T(8,128)(2,1)S(1)}, u32[]{:S(2)}, u32[]{:S(2)}) collective-permute-start(bf16[784,512]{1,0:T(8,128)(2,1)S(1)} %pack.5.refs_5_), channel_id=1, source_target_pairs={{0,1},{1,2},{2,3},{4,5},{5,6},{6,7},{8,9},{9,10},{10,11},{12,13},{... | collective-permute-start | bytes 2408456 | tf_op jit(solution)/shard_map/hidden_right/ppermute | solution.py:23
  52.8 1.3 collective-permute-start.17
  54.1 1.6 collective-permute-start.18
  55.7 3.7 %backward.2 = (bf16[768,384]{1,0:T(8,128)(2,1)S(1)}, bf16[768,384]{1,0:T(8,128)(2,1)S(1)}, f32[1,384]{1,0:T(1,128)S(1)}) custom-call(bf16[192,2048]{1,0:T(8,128)(2,1)} %refs_0_.2, bf16[192,2048]{1,0:T(8,128)(2,1)} %collective-permute-done.5.refs_1_, bf16[768,2048]{1,0:T(8,128)(2,1)S(1)} %bitcast.59, f32[1,384]{1,0:T(1,128)S(1)} %get-tuple-element.237.refs_3_, ...), custom_call_target="tpu_custom_call" | custom-call | flops 1000 | bytes 1000 | tf_op jit(solution)/shard_map/backward/pallas_call | solution.py:97
  59.4 3.8 %backward.3 = (bf16[768,384]{1,0:T(8,128)(2,1)S(1)}, bf16[768,384]{1,0:T(8,128)(2,1)S(1)}, f32[1,384]{1,0:T(1,128)S(1)}) custom-call(bf16[192,2048]{1,0:T(8,128)(2,1)} %collective-permute-done.4.refs_0_, bf16[192,2048]{1,0:T(8,128)(2,1)S(1)} %collective-permute-done.12.refs_1_, bf16[768,2048]{1,0:T(8,128)(2,1)S(1)} %bitcast.60, ...), custom_call_target="tpu_custom_call" | custom-call | flops 1000 | bytes 1000 | tf_op jit(solution)/shard_map/backward/pallas_call | solution.py:97
  64.1 1.6 pack.3.refs_3_
  65.8 5.4 %collective-permute-start.14 = (bf16[784,512]{1,0:T(8,128)(2,1)}, bf16[784,512]{1,0:T(8,128)(2,1)}, u32[]{:S(2)}, u32[]{:S(2)}) collective-permute-start(bf16[784,512]{1,0:T(8,128)(2,1)} %pack.3.refs_3_), channel_id=1, source_target_pairs={{0,1},{3,2},{4,5},{7,6},{8,9},{11,10},{12,13},{15,14},{16,17},{19,... | collective-permute-start | bytes 2408456 | tf_op jit(solution)/shard_map/gate_grad_inward/ppermute | solution.py:23
  71.2 1.9 pad_maximum_fusion.refs_1_
  76.1 1.1 copy-done.19
  77.1 1.1 copy-done.26
  78.9 4.5 %collective-permute-start.13 = (bf16[784,512]{1,0:T(8,128)(2,1)S(1)}, bf16[784,512]{1,0:T(8,128)(2,1)S(1)}, u32[]{:S(2)}, u32[]{:S(2)}) collective-permute-start(bf16[784,512]{1,0:T(8,128)(2,1)S(1)} %pack.4), channel_id=1, source_target_pairs={{0,1},{3,2},{4,5},{7,6},{8,9},{11,10},{12,13},{15,14},{16,17},{19,... | collective-permute-start | bytes 2408456 | tf_op jit(solution)/shard_map/up_grad_inward/ppermute | solution.py:23
  83.4 1.6 collective-permute-start.20
  85.0 1.3 collective-permute-start.21
  86.3 1.5 collective-permute-start.25
  88.8 7.5 %weight_grad.4 = bf16[2,768,512]{2,1,0:T(8,128)(2,1)} custom-call(s32[2]{0:T(128)S(1)} %get-tuple-element.239.refs_0_, bf16[192,2048]{1,0:T(8,128)(2,1)S(1)} %copy-done.6, bf16[192,2048]{1,0:T(8,128)(2,1)S(1)} %copy-done.9, bf16[192,2048]{1,0:T(8,128)(2,1)} %collective-permute-done.refs_0_.refs_3_, bf16[192,2048]{1,0:T(8,128)(2,1)} %collective-permute-done.9.refs_1_.refs_4_, ...), custom_call_target="tpu_custom_call" | custom-call | flops 1000 | bytes 1000 | tf_op jit(solution)/shard_map/weight_grad/pallas_call | solution.py:97
  96.4 1.8 collective-permute-start.23
  98.2 7.3 %collective-permute-done.13.refs_11_ = bf16[784,512]{1,0:T(8,128)(2,1)S(1)} collective-permute-done((bf16[784,512]{1,0:T(8,128)(2,1)S(1)}, bf16[784,512]{1,0:T(8,128)(2,1)S(1)}, u32[]{:S(2)}, u32[]{:S(2)}) %collective-permute-start.13) | collective-permute-done | bytes 802848 | tf_op jit(solution)/shard_map/up_grad_inward/ppermute | solution.py:23
  107.5 1.6 collective-permute-start.27
  109.1 1.5 collective-permute-start.28
  111.2 1.1 copy-done.7
  112.3 1.1 copy-done.10
  113.5 1.1 copy-done.20
  114.5 1.1 copy-done.27
  115.6 1.1 copy-done.32
  116.7 6.0 %weight_grad.5.refs_12_ = bf16[2,768,512]{2,1,0:T(8,128)(2,1)S(1)} custom-call(s32[2]{0:T(128)S(1)} %get-tuple-element.239.refs_0_, bf16[192,2048]{1,0:T(8,128)(2,1)S(1)} %copy-done.7, bf16[192,2048]{1,0:T(8,128)(2,1)S(1)} %copy-done.10, bf16[192,2048]{1,0:T(8,128)(2,1)} %collective-permute-done.refs_0_.refs_3_, ...), custom_call_target="tpu_custom_call" | custom-call | flops 1000 | bytes 1000 | tf_op jit(solution)/shard_map/weight_grad/pallas_call | solution.py:97
  122.8 7.2 %weight_grad.6.refs_12_ = bf16[2,768,512]{2,1,0:T(8,128)(2,1)S(1)} custom-call(s32[2]{0:T(128)S(1)} %get-tuple-element.238.refs_0_, bf16[192,2048]{1,0:T(8,128)(2,1)S(1)} %copy-done.7, bf16[192,2048]{1,0:T(8,128)(2,1)S(1)} %copy-done.10, bf16[192,2048]{1,0:T(8,128)(2,1)} %collective-permute-done.refs_0_.refs_3_, ...), custom_call_target="tpu_custom_call" | custom-call | flops 1000 | bytes 1000 | tf_op jit(solution)/shard_map/weight_grad/pallas_call | solution.py:97
  130.1 6.6 %weight_grad.7.refs_5_ = bf16[2,768,512]{2,1,0:T(8,128)(2,1)S(1)} custom-call(s32[2]{0:T(128)S(1)} %get-tuple-element.238.refs_0_, bf16[192,2048]{1,0:T(8,128)(2,1)S(1)} %copy-done.7, bf16[192,2048]{1,0:T(8,128)(2,1)S(1)} %copy-done.10, bf16[192,2048]{1,0:T(8,128)(2,1)} %collective-permute-done.refs_0_.refs_3_, ...), custom_call_target="tpu_custom_call" | custom-call | flops 1000 | bytes 1000 | tf_op jit(solution)/shard_map/weight_grad/pallas_call | solution.py:97
  136.8 5.0 %input_grad.3 = (bf16[208,2048]{1,0:T(8,128)(2,1)S(1)}, bf16[208,2048]{1,0:T(8,128)(2,1)}) custom-call(bf16[768,384]{1,0:T(8,128)(2,1)S(1)} %copy-done.24, bf16[768,384]{1,0:T(8,128)(2,1)S(1)} %copy-done.28, bf16[768,2048]{1,0:T(8,128)(2,1)S(1)} %get-tuple-element.123.refs_2_, bf16[768,2048]{1,0:T(8,128)(2,1)S(1)} %copy-done.2, ...), custom_call_target="tpu_custom_call" | custom-call | flops 1000 | bytes 1000 | tf_op jit(solution)/shard_map/input_grad/pallas_call | solution.py:97
  142.7 4.3 %input_grad.2 = (bf16[208,2048]{1,0:T(8,128)(2,1)S(1)}, bf16[208,2048]{1,0:T(8,128)(2,1)S(1)}) custom-call(bf16[768,384]{1,0:T(8,128)(2,1)S(1)} %copy-done.17, bf16[768,384]{1,0:T(8,128)(2,1)S(1)} %copy-done.21, bf16[768,2048]{1,0:T(8,128)(2,1)S(1)} %get-tuple-element.123.refs_2_, bf16[768,2048]{1,0:T(8,128)(2,1)S(1)} %copy-done.2, ...), custom_call_target="tpu_custom_call" | custom-call | flops 1000 | bytes 1000 | tf_op jit(solution)/shard_map/input_grad/pallas_call | solution.py:97
  149.6 2.4 %slice_bitcast_fusion = (bf16[768,512]{1,0:T(8,128)(2,1)}, bf16[768,512]{1,0:T(8,128)(2,1)S(1)}) fusion(bf16[2,768,512]{2,1,0:T(8,128)(2,1)} %copy-done.11), kind=kLoop, calls=%fused_computation.15 | loop fusion | bytes 3145728 | tf_op jit(solution)/shard_map/squeeze | solution.py:519
  152.7 1.7 collective-permute-start.34
  154.4 3.0 %fusion.3 = (bf16[512,768]{0,1:T(8,128)(2,1)}, bf16[512,768]{0,1:T(8,128)(2,1)}) fusion(bf16[2,768,512]{2,1,0:T(8,128)(2,1)} %collective-permute-done.23, bf16[2,768,512]{2,1,0:T(8,128)(2,1)S(1)} %copy-done.13), kind=kLoop, calls=%fused_computation.10 | loop fusion | flops 3145728 | bytes 4718592 | tf_op jit(solution)/shard_map/transpose | solution.py:528
  157.4 1.4 collective-permute-start.32
  158.8 10.8 %sum_products.1 = bf16[768,512]{1,0:T(8,128)(2,1)} custom-call(s32[7]{0:T(128)S(1)} %convert_element_type.107.refs_0_, bf16[192,2048]{1,0:T(8,128)(2,1)} %pad_maximum_fusion.refs_1_, bf16[192,2048]{1,0:T(8,128)(2,1)} %collective-permute-done.24.refs_2_, bf16[192,2048]{1,0:T(8,128)(2,1)} %collective-permute-done.25.refs_3_, ...), custom_call_target="tpu_custom_call" | custom-call | flops 1000 | bytes 1000 | tf_op jit(solution)/shard_map/sum_products/pallas_call | solution.py:97
  169.6 2.5 %add_convert_fusion.1 = bf16[208,2048]{1,0:T(8,128)(2,1)} fusion(bf16[208,2048]{1,0:T(8,128)(2,1)} %collective-permute-done.30, bf16[208,2048]{1,0:T(8,128)(2,1)S(1)} %copy-done.43), kind=kLoop, calls=%fused_computation.1 | loop fusion | flops 1703936 | bytes 2555904 | tf_op jit(solution)/shard_map/convert_element_type | solution.py:59
  172.1 1.3 add_convert_fusion.2
  173.8 1.1 fusion.4
  174.9 1.3 collective-permute-start.33
  176.2 1.6 collective-permute-start.31
  177.8 7.0 %collective-permute-done.32 = bf16[512,768]{0,1:T(8,128)(2,1)} collective-permute-done((bf16[512,768]{0,1:T(8,128)(2,1)}, bf16[512,768]{0,1:T(8,128)(2,1)}, u32[]{:S(2)}, u32[]{:S(2)}) %collective-permute-start.32) | collective-permute-done | bytes 786464 | tf_op jit(solution)/shard_map/gate_sums_outward/ppermute | solution.py:23
  184.7 1.2 select_bitcast_fusion
  186.0 1.2 copy.12
  187.1 15.9 %collective-permute-done.33 = bf16[512,768]{0,1:T(8,128)(2,1)} collective-permute-done((bf16[512,768]{0,1:T(8,128)(2,1)}, bf16[512,768]{0,1:T(8,128)(2,1)}, u32[]{:S(2)}, u32[]{:S(2)}) %collective-permute-start.33) | collective-permute-done | bytes 786464 | tf_op jit(solution)/shard_map/up_sums_outward/ppermute | solution.py:23
  203.0 1.7 fusion.7
  204.7 1.2 copy.13
  205.8 1.5 add_convert_fusion
  (162 shorter events, 19.6 us)
Async XLA Ops:
  0.6 15.5 %collective-permute-start.3 = (bf16[192,2048]{1,0:T(8,128)(2,1)}, bf16[192,2048]{1,0:T(8,128)(2,1)S(1)}, u32[]{:S(2)}, u32[]{:S(2)}) collective-permute-start(bf16[192,2048]{1,0:T(8,128)(2,1)} %refs_1_.3), channel_id=1, source_target_pairs={{0,4},{4,0},{8,12},{12,8},{1,5},{5,1},{9,13},{13,9},{2,6},{6,2},{1... | collective-permute-start | bytes 2359304 | tf_op jit(solution)/shard_map/tokens_core/ppermute | solution.py:23
  1.1 22.0 %collective-permute-start = (bf16[192,2048]{1,0:T(8,128)(2,1)}, bf16[192,2048]{1,0:T(8,128)(2,1)}, u32[]{:S(2)}, u32[]{:S(2)}) collective-permute-start(bf16[192,2048]{1,0:T(8,128)(2,1)} %refs_1_.3), channel_id=1, source_target_pairs={{8,0},{12,4},{0,8},{4,12},{9,1},{13,5},{1,9},{5,13},{10,2},{14,6},... | collective-permute-start | bytes 2359304 | tf_op jit(solution)/shard_map/tokens_chip/ppermute | solution.py:23
  3.7 20.9 %collective-permute-start.2 = (bf16[192,2048]{1,0:T(8,128)(2,1)}, bf16[192,2048]{1,0:T(8,128)(2,1)}, u32[]{:S(2)}, u32[]{:S(2)}) collective-permute-start(bf16[192,2048]{1,0:T(8,128)(2,1)} %refs_1_.3), channel_id=1, source_target_pairs={{0,1},{3,2},{4,5},{7,6},{8,9},{11,10},{12,13},{15,14},{16,17},{19,... | collective-permute-start | bytes 2359304 | tf_op jit(solution)/shard_map/tokens_inward/ppermute | solution.py:23
  9.5 13.6 %collective-permute-start.1 = (f32[4,192]{1,0:T(4,128)S(1)}, f32[4,192]{1,0:T(4,128)S(1)}, u32[]{:S(2)}, u32[]{:S(2)}) collective-permute-start(f32[4,192]{1,0:T(4,128)S(1)} %pad_maximum_fusion.2), channel_id=1, source_target_pairs={{8,0},{12,4},{0,8},{4,12},{9,1},{13,5},{1,9},{5,13},{10,2},{14,6},... | collective-permute-start | bytes 9224 | tf_op jit(solution)/shard_map/routing_chip/ppermute | solution.py:23
  24.7 7.9 %collective-permute-start.9 = (bf16[192,2048]{1,0:T(8,128)(2,1)}, bf16[192,2048]{1,0:T(8,128)(2,1)}, u32[]{:S(2)}, u32[]{:S(2)}) collective-permute-start(bf16[192,2048]{1,0:T(8,128)(2,1)} %collective-permute-done.refs_0_.refs_3_), channel_id=1, source_target_pairs={{0,4},{4,0},{8,12},{12,8},{1,5},{5,1},{9,13},{13,9},{2,6},{6,2},{1... | collective-permute-start | bytes 2359304 | tf_op jit(solution)/shard_map/tokens_core/ppermute | solution.py:23
  24.7 20.7 %collective-permute-start.4 = (bf16[192,2048]{1,0:T(8,128)(2,1)}, bf16[192,2048]{1,0:T(8,128)(2,1)}, u32[]{:S(2)}, u32[]{:S(2)}) collective-permute-start(bf16[192,2048]{1,0:T(8,128)(2,1)} %refs_0_.2), channel_id=1, source_target_pairs={{8,0},{12,4},{0,8},{4,12},{9,1},{13,5},{1,9},{5,13},{10,2},{14,6},... | collective-permute-start | bytes 2359304 | tf_op jit(solution)/shard_map/out_grad_chip/ppermute | solution.py:23
  25.2 20.2 %collective-permute-start.5 = (bf16[192,2048]{1,0:T(8,128)(2,1)}, bf16[192,2048]{1,0:T(8,128)(2,1)}, u32[]{:S(2)}, u32[]{:S(2)}) collective-permute-start(bf16[192,2048]{1,0:T(8,128)(2,1)} %refs_0_.2), channel_id=1, source_target_pairs={{0,4},{4,0},{8,12},{12,8},{1,5},{5,1},{9,13},{13,9},{2,6},{6,2},{1... | collective-permute-start | bytes 2359304 | tf_op jit(solution)/shard_map/out_grad_core/ppermute | solution.py:23
  25.4 4.9 %collective-permute-start.10 = (f32[4,192]{1,0:T(4,128)S(1)}, f32[4,192]{1,0:T(4,128)S(1)}, u32[]{:S(2)}, u32[]{:S(2)}) collective-permute-start(f32[4,192]{1,0:T(4,128)S(1)} %pad_maximum_fusion.2), channel_id=1, source_target_pairs={{0,4},{4,0},{8,12},{12,8},{1,5},{5,1},{9,13},{13,9},{2,6},{6,2},{1... | collective-permute-start | bytes 9224 | tf_op jit(solution)/shard_map/routing_core/ppermute | solution.py:23
  27.8 16.2 %collective-permute-start.6 = (bf16[192,512]{1,0:T(8,128)(2,1)}, bf16[192,512]{1,0:T(8,128)(2,1)}, u32[]{:S(2)}, u32[]{:S(2)}) collective-permute-start(bf16[192,512]{1,0:T(8,128)(2,1)} %get-tuple-element.231), channel_id=1, source_target_pairs={{0,1},{1,2},{2,3},{3,0},{4,5},{5,6},{6,7},{7,4},{8,9},{9,10},{10,1... | collective-permute-start | bytes 589832 | tf_op jit(solution)/shard_map/out_grad_share_rotated/ppermute | solution.py:23
  30.3 1.2 collective-permute-start.11
  31.4 13.9 %collective-permute-start.7 = (bf16[192,512]{1,0:T(8,128)(2,1)}, bf16[192,512]{1,0:T(8,128)(2,1)S(1)}, u32[]{:S(2)}, u32[]{:S(2)}) collective-permute-start(bf16[192,512]{1,0:T(8,128)(2,1)} %get-tuple-element.233), channel_id=1, source_target_pairs={{0,2},{1,3},{2,0},{3,1},{4,6},{5,7},{6,4},{7,5},{8,10},{9,11},{10,... | collective-permute-start | bytes 589832 | tf_op jit(solution)/shard_map/out_grad_share_rotated/ppermute | solution.py:23
  32.5 12.8 %collective-permute-start.8 = (bf16[192,512]{1,0:T(8,128)(2,1)}, bf16[192,512]{1,0:T(8,128)(2,1)S(1)}, u32[]{:S(2)}, u32[]{:S(2)}) collective-permute-start(bf16[192,512]{1,0:T(8,128)(2,1)} %get-tuple-element.230), channel_id=1, source_target_pairs={{0,3},{1,0},{2,1},{3,2},{4,7},{5,4},{6,5},{7,6},{8,11},{9,8},{10,9... | collective-permute-start | bytes 589832 | tf_op jit(solution)/shard_map/out_grad_share_rotated/ppermute | solution.py:23
  38.5 6.9 %copy-start.37 = (bf16[768,384]{1,0:T(8,128)(2,1)S(1)}, bf16[768,384]{1,0:T(8,128)(2,1)}, u32[]{:S(2)}) copy-start(bf16[768,384]{1,0:T(8,128)(2,1)} %copy-done.36) | copy-start | bytes 1769476
  38.5 17.1 %copy-start.14 = (bf16[1,768,2048]{2,1,0:T(8,128)(2,1)S(1)}, bf16[1,768,2048]{2,1,0:T(8,128)(2,1)}, u32[]{:S(2)}) copy-start(bf16[1,768,2048]{2,1,0:T(8,128)(2,1)} %param.13) | copy-start | bytes 9437188
  43.9 11.8 %copy-start.39 = (f32[768,384]{1,0:T(8,128)S(1)}, f32[768,384]{1,0:T(8,128)}, u32[]{:S(2)}) copy-start(f32[768,384]{1,0:T(8,128)} %copy-done.38) | copy-start | bytes 3538948
  43.9 11.8 %copy-start.41 = (f32[768,384]{1,0:T(8,128)S(1)}, f32[768,384]{1,0:T(8,128)}, u32[]{:S(2)}) copy-start(f32[768,384]{1,0:T(8,128)} %copy-done.40) | copy-start | bytes 3538948
  45.3 14.1 %collective-permute-start.12 = (bf16[192,2048]{1,0:T(8,128)(2,1)}, bf16[192,2048]{1,0:T(8,128)(2,1)S(1)}, u32[]{:S(2)}, u32[]{:S(2)}) collective-permute-start(bf16[192,2048]{1,0:T(8,128)(2,1)} %collective-permute-done.4.refs_0_), channel_id=1, source_target_pairs={{0,4},{4,0},{8,12},{12,8},{1,5},{5,1},{9,13},{13,9},{2,6},{6,2},{1... | collective-permute-start | bytes 2359304 | tf_op jit(solution)/shard_map/out_grad_core/ppermute | solution.py:23
  46.2 13.2 %copy-start.29 = (bf16[784,512]{1,0:T(8,128)(2,1)}, bf16[784,512]{1,0:T(8,128)(2,1)S(1)}, u32[]{:S(2)}) copy-start(bf16[784,512]{1,0:T(8,128)(2,1)S(1)} %pack.5.refs_5_) | copy-start | bytes 2408452
  46.2 27.9 %collective-permute-start.16 = (bf16[784,512]{1,0:T(8,128)(2,1)S(1)}, bf16[784,512]{1,0:T(8,128)(2,1)S(1)}, u32[]{:S(2)}, u32[]{:S(2)}) collective-permute-start(bf16[784,512]{1,0:T(8,128)(2,1)S(1)} %pack.5.refs_5_), channel_id=1, source_target_pairs={{0,1},{1,2},{2,3},{4,5},{5,6},{6,7},{8,9},{9,10},{10,11},{12,13},{... | collective-permute-start | bytes 2408456 | tf_op jit(solution)/shard_map/hidden_right/ppermute | solution.py:23
  52.8 21.9 %collective-permute-start.17 = (bf16[784,512]{1,0:T(8,128)(2,1)S(1)}, bf16[784,512]{1,0:T(8,128)(2,1)S(1)}, u32[]{:S(2)}, u32[]{:S(2)}) collective-permute-start(bf16[784,512]{1,0:T(8,128)(2,1)S(1)} %pack.5.refs_5_), channel_id=1, source_target_pairs={{1,0},{2,1},{3,2},{5,4},{6,5},{7,6},{9,8},{10,9},{11,10},{13,12},{... | collective-permute-start | bytes 2408456 | tf_op jit(solution)/shard_map/hidden_left/ppermute | solution.py:23
  54.1 20.0 %collective-permute-start.18 = (bf16[192,2048]{1,0:T(8,128)(2,1)}, bf16[192,2048]{1,0:T(8,128)(2,1)}, u32[]{:S(2)}, u32[]{:S(2)}) collective-permute-start(bf16[192,2048]{1,0:T(8,128)(2,1)} %collective-permute-done.2.refs_5_), channel_id=1, source_target_pairs={{8,0},{12,4},{0,8},{4,12},{9,1},{13,5},{1,9},{5,13},{10,2},{14,6},... | collective-permute-start | bytes 2359304 | tf_op jit(solution)/shard_map/tokens_fold_chip/ppermute | solution.py:23
  55.7 29.3 %collective-permute-start.15 = (bf16[192,2048]{1,0:T(8,128)(2,1)}, bf16[192,2048]{1,0:T(8,128)(2,1)}, u32[]{:S(2)}, u32[]{:S(2)}) collective-permute-start(bf16[192,2048]{1,0:T(8,128)(2,1)} %collective-permute-done.2.refs_5_), channel_id=1, source_target_pairs={{0,4},{4,0},{8,12},{12,8},{1,5},{5,1},{9,13},{13,9},{2,6},{6,2},{1... | collective-permute-start | bytes 2359304 | tf_op jit(solution)/shard_map/tokens_fold_core/ppermute | solution.py:23
  59.4 4.7 %copy-start.15 = (bf16[768,384]{1,0:T(8,128)(2,1)}, bf16[768,384]{1,0:T(8,128)(2,1)S(1)}, u32[]{:S(2)}) copy-start(bf16[768,384]{1,0:T(8,128)(2,1)S(1)} %get-tuple-element.182.refs_0_.refs_9_) | copy-start | bytes 1769476
  64.1 9.0 %copy-start.22 = (bf16[768,384]{1,0:T(8,128)(2,1)}, bf16[768,384]{1,0:T(8,128)(2,1)S(1)}, u32[]{:S(2)}) copy-start(bf16[768,384]{1,0:T(8,128)(2,1)S(1)} %get-tuple-element.188.refs_1_.refs_10_.refs_0_) | copy-start | bytes 1769476
  64.1 9.0 %copy-start.50 = (f32[1,384]{1,0:T(1,128)}, f32[1,384]{1,0:T(1,128)S(1)}, u32[]{:S(2)}) copy-start(f32[1,384]{1,0:T(1,128)S(1)} %get-tuple-element.190) | copy-start | bytes 4612
  64.1 7.1 %copy-start.55 = (bf16[192,512]{1,0:T(8,128)(2,1)S(1)}, bf16[192,512]{1,0:T(8,128)(2,1)}, u32[]{:S(2)}) copy-start(bf16[192,512]{1,0:T(8,128)(2,1)} %get-tuple-element.154) | copy-start | bytes 589828
  65.8 23.0 %collective-permute-start.14 = (bf16[784,512]{1,0:T(8,128)(2,1)}, bf16[784,512]{1,0:T(8,128)(2,1)}, u32[]{:S(2)}, u32[]{:S(2)}) collective-permute-start(bf16[784,512]{1,0:T(8,128)(2,1)} %pack.3.refs_3_), channel_id=1, source_target_pairs={{0,1},{3,2},{4,5},{7,6},{8,9},{11,10},{12,13},{15,14},{16,17},{19,... | collective-permute-start | bytes 2408456 | tf_op jit(solution)/shard_map/gate_grad_inward/ppermute | solution.py:23
  76.1 10.2 %collective-permute-start.19 = (bf16[192,2048]{1,0:T(8,128)(2,1)}, bf16[192,2048]{1,0:T(8,128)(2,1)}, u32[]{:S(2)}, u32[]{:S(2)}) collective-permute-start(bf16[192,2048]{1,0:T(8,128)(2,1)} %collective-permute-done.18.refs_7_), channel_id=1, source_target_pairs={{0,4},{4,0},{8,12},{12,8},{1,5},{5,1},{9,13},{13,9},{2,6},{6,2},{1... | collective-permute-start | bytes 2359304 | tf_op jit(solution)/shard_map/tokens_fold_core/ppermute | solution.py:23
  78.2 10.6 %copy-start.6 = (bf16[192,2048]{1,0:T(8,128)(2,1)S(1)}, bf16[192,2048]{1,0:T(8,128)(2,1)}, u32[]{:S(2)}) copy-start(bf16[192,2048]{1,0:T(8,128)(2,1)} %refs_1_.3) | copy-start | bytes 2359300
  78.2 10.6 %copy-start.9 = (bf16[192,2048]{1,0:T(8,128)(2,1)S(1)}, bf16[192,2048]{1,0:T(8,128)(2,1)}, u32[]{:S(2)}) copy-start(bf16[192,2048]{1,0:T(8,128)(2,1)} %copy-done.8) | copy-start | bytes 2359300
  78.2 10.6 %copy-start.16 = (bf16[768,384]{1,0:T(8,128)(2,1)S(1)}, bf16[768,384]{1,0:T(8,128)(2,1)}, u32[]{:S(2)}) copy-start(bf16[768,384]{1,0:T(8,128)(2,1)} %copy-done.15) | copy-start | bytes 1769476
  78.2 10.6 %copy-start.23 = (bf16[768,384]{1,0:T(8,128)(2,1)S(1)}, bf16[768,384]{1,0:T(8,128)(2,1)}, u32[]{:S(2)}) copy-start(bf16[768,384]{1,0:T(8,128)(2,1)} %copy-done.22) | copy-start | bytes 1769476
  78.9 26.6 %collective-permute-start.13 = (bf16[784,512]{1,0:T(8,128)(2,1)S(1)}, bf16[784,512]{1,0:T(8,128)(2,1)S(1)}, u32[]{:S(2)}, u32[]{:S(2)}) collective-permute-start(bf16[784,512]{1,0:T(8,128)(2,1)S(1)} %pack.4), channel_id=1, source_target_pairs={{0,1},{3,2},{4,5},{7,6},{8,9},{11,10},{12,13},{15,14},{16,17},{19,... | collective-permute-start | bytes 2408456 | tf_op jit(solution)/shard_map/up_grad_inward/ppermute | solution.py:23
  83.4 23.0 %collective-permute-start.20 = (bf16[784,512]{1,0:T(8,128)(2,1)}, bf16[784,512]{1,0:T(8,128)(2,1)}, u32[]{:S(2)}, u32[]{:S(2)}) collective-permute-start(bf16[784,512]{1,0:T(8,128)(2,1)} %copy-done.46), channel_id=1, source_target_pairs={{1,2},{2,3},{5,6},{6,7},{9,10},{10,11},{13,14},{14,15},{17,18},{18... | collective-permute-start | bytes 2408456 | tf_op jit(solution)/shard_map/hidden_right/ppermute | solution.py:23
  85.0 22.5 %collective-permute-start.21 = (bf16[784,512]{1,0:T(8,128)(2,1)}, bf16[784,512]{1,0:T(8,128)(2,1)}, u32[]{:S(2)}, u32[]{:S(2)}) collective-permute-start(bf16[784,512]{1,0:T(8,128)(2,1)} %copy-done.48), channel_id=1, source_target_pairs={{1,0},{2,1},{5,4},{6,5},{9,8},{10,9},{13,12},{14,13},{17,16},{18,1... | collective-permute-start | bytes 2408456 | tf_op jit(solution)/shard_map/hidden_left/ppermute | solution.py:23
  86.3 24.3 %collective-permute-start.25 = (bf16[192,2048]{1,0:T(8,128)(2,1)}, bf16[192,2048]{1,0:T(8,128)(2,1)}, u32[]{:S(2)}, u32[]{:S(2)}) collective-permute-start(bf16[192,2048]{1,0:T(8,128)(2,1)} %pad_maximum_fusion.refs_1_), channel_id=1, source_target_pairs={{8,0},{12,4},{0,8},{4,12},{9,1},{13,5},{1,9},{5,13},{10,2},{14,6},... | collective-permute-start | bytes 2359304 | tf_op jit(solution)/shard_map/out_grad_share_chip/ppermute | solution.py:23
  88.8 22.3 %copy-start.51 = (f32[1,384]{1,0:T(1,128)S(1)}, f32[1,384]{1,0:T(1,128)}, u32[]{:S(2)}) copy-start(f32[1,384]{1,0:T(1,128)} %copy-done.50) | copy-start | bytes 4612
  96.4 52.5 %collective-permute-start.23 = (bf16[2,768,512]{2,1,0:T(8,128)(2,1)}, bf16[2,768,512]{2,1,0:T(8,128)(2,1)}, u32[]{:S(2)}, u32[]{:S(2)}) collective-permute-start(bf16[2,768,512]{2,1,0:T(8,128)(2,1)} %weight_grad.4), channel_id=1, source_target_pairs={{1,2},{2,1},{5,6},{6,5},{9,10},{10,9},{13,14},{14,13},{17,18},{18,... | collective-permute-start | bytes 4718600 | tf_op jit(solution)/shard_map/gate_sums_across/ppermute | solution.py:23
  107.5 41.4 %collective-permute-start.27 = (bf16[784,512]{1,0:T(8,128)(2,1)}, bf16[784,512]{1,0:T(8,128)(2,1)}, u32[]{:S(2)}, u32[]{:S(2)}) collective-permute-start(bf16[784,512]{1,0:T(8,128)(2,1)} %collective-permute-done.20.refs_8_), channel_id=1, source_target_pairs={{2,3},{6,7},{10,11},{14,15},{18,19},{22,23},{26,27},{30,31}} | collective-permute-start | bytes 2408456 | tf_op jit(solution)/shard_map/hidden_right/ppermute | solution.py:23
  109.1 39.8 %collective-permute-start.28 = (bf16[784,512]{1,0:T(8,128)(2,1)}, bf16[784,512]{1,0:T(8,128)(2,1)}, u32[]{:S(2)}, u32[]{:S(2)}) collective-permute-start(bf16[784,512]{1,0:T(8,128)(2,1)} %collective-permute-done.21.refs_9_), channel_id=1, source_target_pairs={{1,0},{5,4},{9,8},{13,12},{17,16},{21,20},{25,24},{29,28}} | collective-permute-start | bytes 2408456 | tf_op jit(solution)/shard_map/hidden_left/ppermute | solution.py:23
  110.6 38.3 %collective-permute-start.24 = (bf16[192,2048]{1,0:T(8,128)(2,1)}, bf16[192,2048]{1,0:T(8,128)(2,1)}, u32[]{:S(2)}, u32[]{:S(2)}) collective-permute-start(bf16[192,2048]{1,0:T(8,128)(2,1)} %pad_maximum_fusion.refs_1_), channel_id=1, source_target_pairs={{0,4},{4,0},{8,12},{12,8},{1,5},{5,1},{9,13},{13,9},{2,6},{6,2},{1... | collective-permute-start | bytes 2359304 | tf_op jit(solution)/shard_map/out_grad_share_core/ppermute | solution.py:23
  110.7 38.2 %collective-permute-start.26 = (bf16[192,2048]{1,0:T(8,128)(2,1)}, bf16[192,2048]{1,0:T(8,128)(2,1)}, u32[]{:S(2)}, u32[]{:S(2)}) collective-permute-start(bf16[192,2048]{1,0:T(8,128)(2,1)} %collective-permute-done.25.refs_3_), channel_id=1, source_target_pairs={{0,4},{4,0},{8,12},{12,8},{1,5},{5,1},{9,13},{13,9},{2,6},{6,2},{1... | collective-permute-start | bytes 2359304 | tf_op jit(solution)/shard_map/out_grad_share_core/ppermute | solution.py:23
  116.7 6.0 %copy-start.17 = (bf16[768,384]{1,0:T(8,128)(2,1)S(1)}, bf16[768,384]{1,0:T(8,128)(2,1)}, u32[]{:S(2)}) copy-start(bf16[768,384]{1,0:T(8,128)(2,1)} %copy-done.15) | copy-start | bytes 1769476
  116.7 6.0 %copy-start.24 = (bf16[768,384]{1,0:T(8,128)(2,1)S(1)}, bf16[768,384]{1,0:T(8,128)(2,1)}, u32[]{:S(2)}) copy-start(bf16[768,384]{1,0:T(8,128)(2,1)} %copy-done.22) | copy-start | bytes 1769476
  122.7 7.3 %copy-start.11 = (bf16[2,768,512]{2,1,0:T(8,128)(2,1)}, bf16[2,768,512]{2,1,0:T(8,128)(2,1)S(1)}, u32[]{:S(2)}) copy-start(bf16[2,768,512]{2,1,0:T(8,128)(2,1)S(1)} %weight_grad.5.refs_12_) | copy-start | bytes 4718596
  122.8 7.3 %copy-start.21 = (bf16[768,384]{1,0:T(8,128)(2,1)S(1)}, bf16[768,384]{1,0:T(8,128)(2,1)}, u32[]{:S(2)}) copy-start(bf16[768,384]{1,0:T(8,128)(2,1)} %copy-done.18) | copy-start | bytes 1769476
  122.8 7.3 %copy-start.28 = (bf16[768,384]{1,0:T(8,128)(2,1)S(1)}, bf16[768,384]{1,0:T(8,128)(2,1)}, u32[]{:S(2)}) copy-start(bf16[768,384]{1,0:T(8,128)(2,1)} %copy-done.25) | copy-start | bytes 1769476
  122.8 7.3 %copy-start.33 = (bf16[784,512]{1,0:T(8,128)(2,1)S(1)}, bf16[784,512]{1,0:T(8,128)(2,1)}, u32[]{:S(2)}) copy-start(bf16[784,512]{1,0:T(8,128)(2,1)} %copy-done.31) | copy-start | bytes 2408452
  130.0 6.7 %copy-start.12 = (bf16[2,768,512]{2,1,0:T(8,128)(2,1)}, bf16[2,768,512]{2,1,0:T(8,128)(2,1)S(1)}, u32[]{:S(2)}) copy-start(bf16[2,768,512]{2,1,0:T(8,128)(2,1)S(1)} %weight_grad.6.refs_12_) | copy-start | bytes 4718596
  130.1 6.7 %copy-start.2 = (bf16[768,2048]{1,0:T(8,128)(2,1)S(1)}, bf16[768,2048]{1,0:T(8,128)(2,1)}, u32[]{:S(2)}) copy-start(bf16[768,2048]{1,0:T(8,128)(2,1)} %copy-done) | copy-start | bytes 9437188
  136.7 5.9 %copy-start.3 = (bf16[2,768,512]{2,1,0:T(8,128)(2,1)}, bf16[2,768,512]{2,1,0:T(8,128)(2,1)S(1)}, u32[]{:S(2)}) copy-start(bf16[2,768,512]{2,1,0:T(8,128)(2,1)S(1)} %weight_grad.7.refs_5_) | copy-start | bytes 4718596
  148.9 20.7 %collective-permute-start.30 = (bf16[208,2048]{1,0:T(8,128)(2,1)}, bf16[208,2048]{1,0:T(8,128)(2,1)}, u32[]{:S(2)}, u32[]{:S(2)}) collective-permute-start(bf16[208,2048]{1,0:T(8,128)(2,1)} %get-tuple-element.204), channel_id=1, source_target_pairs={{0,4},{4,0},{8,12},{12,8},{1,5},{5,1},{9,13},{13,9},{2,6},{6,2},{1... | collective-permute-start | bytes 2555912 | tf_op jit(solution)/shard_map/token_grads_core/ppermute | solution.py:23
  149.1 5.3 %copy-start.13 = (bf16[2,768,512]{2,1,0:T(8,128)(2,1)S(1)}, bf16[2,768,512]{2,1,0:T(8,128)(2,1)}, u32[]{:S(2)}) copy-start(bf16[2,768,512]{2,1,0:T(8,128)(2,1)} %copy-done.12) | copy-start | bytes 4718596
  149.1 23.0 %collective-permute-start.29 = (bf16[208,2048]{1,0:T(8,128)(2,1)}, bf16[208,2048]{1,0:T(8,128)(2,1)S(1)}, u32[]{:S(2)}, u32[]{:S(2)}) collective-permute-start(bf16[208,2048]{1,0:T(8,128)(2,1)} %copy-done.52), channel_id=1, source_target_pairs={{0,4},{4,0},{8,12},{12,8},{1,5},{5,1},{9,13},{13,9},{2,6},{6,2},{1... | collective-permute-start | bytes 2555912 | tf_op jit(solution)/shard_map/token_grads_core/ppermute | solution.py:23
  152.0 21.4 %collective-permute-start.22 = (bf16[768,512]{1,0:T(8,128)(2,1)S(1)}, bf16[768,512]{1,0:T(8,128)(2,1)S(1)}, u32[]{:S(2)}, u32[]{:S(2)}) collective-permute-start(bf16[768,512]{1,0:T(8,128)(2,1)S(1)} %get-tuple-element.229), channel_id=1, source_target_pairs={{1,2},{2,1},{5,6},{6,5},{9,10},{10,9},{13,14},{14,13},{17,18},{18,... | collective-permute-start | bytes 2359304 | tf_op jit(solution)/shard_map/up_far_sums_across/ppermute | solution.py:23
  152.7 6.1 %copy-start.30 = (bf16[784,512]{1,0:T(8,128)(2,1)S(1)}, bf16[784,512]{1,0:T(8,128)(2,1)}, u32[]{:S(2)}) copy-start(bf16[784,512]{1,0:T(8,128)(2,1)} %copy-done.29) | copy-start | bytes 2408452
  152.7 6.1 %copy-start.47 = (bf16[784,512]{1,0:T(8,128)(2,1)S(1)}, bf16[784,512]{1,0:T(8,128)(2,1)}, u32[]{:S(2)}) copy-start(bf16[784,512]{1,0:T(8,128)(2,1)} %copy-done.46) | copy-start | bytes 2408452
  152.7 6.1 %copy-start.49 = (bf16[784,512]{1,0:T(8,128)(2,1)S(1)}, bf16[784,512]{1,0:T(8,128)(2,1)}, u32[]{:S(2)}) copy-start(bf16[784,512]{1,0:T(8,128)(2,1)} %copy-done.48) | copy-start | bytes 2408452
  152.7 34.4 %collective-permute-start.34 = (bf16[768,512]{1,0:T(8,128)(2,1)}, bf16[768,512]{1,0:T(8,128)(2,1)}, u32[]{:S(2)}, u32[]{:S(2)}) collective-permute-start(bf16[768,512]{1,0:T(8,128)(2,1)} %get-tuple-element.228), channel_id=1, source_target_pairs={{1,2},{2,1},{5,6},{6,5},{9,10},{10,9},{13,14},{14,13},{17,18},{18,... | collective-permute-start | bytes 2359304 | tf_op jit(solution)/shard_map/up_sums_across/ppermute | solution.py:23
  157.4 12.2 %copy-start.43 = (bf16[208,2048]{1,0:T(8,128)(2,1)S(1)}, bf16[208,2048]{1,0:T(8,128)(2,1)}, u32[]{:S(2)}) copy-start(bf16[208,2048]{1,0:T(8,128)(2,1)} %copy-done.42) | copy-start | bytes 2555908
  157.4 27.4 %collective-permute-start.32 = (bf16[512,768]{0,1:T(8,128)(2,1)}, bf16[512,768]{0,1:T(8,128)(2,1)}, u32[]{:S(2)}, u32[]{:S(2)}) collective-permute-start(bf16[512,768]{0,1:T(8,128)(2,1)} %get-tuple-element.226), channel_id=1, source_target_pairs={{1,0},{2,3},{5,4},{6,7},{9,8},{10,11},{13,12},{14,15},{17,16},{18,... | collective-permute-start | bytes 2359304 | tf_op jit(solution)/shard_map/gate_sums_outward/ppermute | solution.py:23
  173.4 11.4 %copy-start.54 = (bf16[512,768]{0,1:T(8,128)(2,1)S(1)}, bf16[512,768]{0,1:T(8,128)(2,1)}, u32[]{:S(2)}) copy-start(bf16[512,768]{0,1:T(8,128)(2,1)} %get-tuple-element.217) | copy-start | bytes 2359300
  174.9 28.1 %collective-permute-start.33 = (bf16[512,768]{0,1:T(8,128)(2,1)}, bf16[512,768]{0,1:T(8,128)(2,1)}, u32[]{:S(2)}, u32[]{:S(2)}) collective-permute-start(bf16[512,768]{0,1:T(8,128)(2,1)} %fusion.4), channel_id=1, source_target_pairs={{1,0},{2,3},{5,4},{6,7},{9,8},{10,11},{13,12},{14,15},{17,16},{18,... | collective-permute-start | bytes 2359304 | tf_op jit(solution)/shard_map/up_sums_outward/ppermute | solution.py:23
  176.2 29.7 %collective-permute-start.31 = (bf16[208,2048]{1,0:T(8,128)(2,1)}, bf16[208,2048]{1,0:T(8,128)(2,1)}, u32[]{:S(2)}, u32[]{:S(2)}) collective-permute-start(bf16[208,2048]{1,0:T(8,128)(2,1)} %add_convert_fusion.1), channel_id=1, source_target_pairs={{8,0},{12,4},{0,8},{4,12},{9,1},{13,5},{1,9},{5,13},{10,2},{14,6},... | collective-permute-start | bytes 2555912 | tf_op jit(solution)/shard_map/token_grads_chip/ppermute | solution.py:23
  (27 other events, 42.5 us)

commit v3 on v2

--- a/solution.py
+++ b/solution.py
@@ -10,7 +10,7 @@
 BF = jnp.bfloat16
 F32 = jnp.float32
 VMEM_SMALL = 28 * 1024 * 1024
-VMEM_LARGE = 28 * 1024 * 1024
+VMEM_LARGE = 60 * 1024 * 1024
 COST = pl.CostEstimate(flops=1000, bytes_accessed=1000, transcendentals=0)
 
 
@@ -45,11 +45,6 @@
 
 def return_sums(pairs, experts, what):
     return [add(own, core_swap(other, experts, what)) for own, other in pairs]
-
-
-def return_shift(sums, experts, what):
-    chips = experts // 2
-    return add(sums[0], *(chip_shift(sums[k], experts, chips - k, what) for k in range(1, chips)))
 
 
 def add(*terms):
@@ -111,12 +106,14 @@
     return (a, a.shape, lambda *i: (0,) * a.ndim)
 
 
-def copies(blocks, target, sem, first=0):
-    rows = blocks[0].shape[0]
-    return [
-        pltpu.make_async_copy(b, target.at[pl.ds(i * rows, rows)], sem.at[first + i])
-        for i, b in enumerate(blocks)
-    ]
+def copies(blocks, target, sem, first=0, axis=0):
+    size = blocks[0].shape[axis]
+    moves = []
+    for i, b in enumerate(blocks):
+        at = pl.ds(i * size, size)
+        part = target.at[at] if axis == 0 else target.at[:, at]
+        moves.append(pltpu.make_async_copy(b, part, sem.at[first + i]))
+    return moves
 
 
 def fetch(*args):
@@ -155,16 +152,16 @@
         sigmoid = jax.nn.sigmoid(gate_pre)
         activated = gate_pre * sigmoid
         hidden[...] = (activated * up_pre).astype(BF)
-        gate_factor[...] = up_pre * (sigmoid * (1.0 + gate_pre * (1.0 - sigmoid)))
-        up_factor[...] = activated
+        gate_factor[...] = (up_pre * (sigmoid * (1.0 + gate_pre * (1.0 - sigmoid)))).astype(BF)
+        up_factor[...] = activated.astype(BF)
 
     at = lambda i: (i, 0)
     return call(
         body,
         "forward",
         (units // tile,),
-        [(b, pl.ANY) for b in pair] + [(w, (tile, width), at) for w in (gate_wt, up_wt)],
-        [((units, rows), t, (tile, rows), at) for t in (BF, F32, F32)],
+        [(b, pltpu.HBM) for b in pair] + [(w, (tile, width), at) for w in (gate_wt, up_wt)],
+        [((units, rows), t, (tile, rows), at) for t in (BF, BF, BF)],
         [pltpu.VMEM((rows, width), BF), pltpu.SemaphoreType.DMA((2,))],
         deps,
     )
@@ -187,8 +184,8 @@
 
         raw = dot(down_w[...], og[...], 1, 1)
         scaled = raw * weight[...]
-        gate_grad[...] = (scaled * gate_factor[...]).astype(BF)
-        up_grad[...] = (scaled * up_factor[...]).astype(BF)
+        gate_grad[...] = (scaled * gate_factor[...].astype(F32)).astype(BF)
+        up_grad[...] = (scaled * up_factor[...].astype(F32)).astype(BF)
         gate_sum[...] += jnp.sum(raw * hidden[...].astype(F32), axis=0, keepdims=True)
 
     at = lambda i: (i, 0)
@@ -197,13 +194,12 @@
         body,
         "backward",
         (units // tile,),
-        [(b, pl.ANY) for b in pair]
+        [(b, pltpu.HBM) for b in pair]
         + [(down_w, (tile, width), at), whole(weight)]
         + [(a, tall, at) for a in (hidden, gate_factor, up_factor)],
         [((units, rows), BF, tall, at)] * 2 + [((1, rows), F32, (1, rows), lambda i: (0, 0))],
         [pltpu.VMEM((rows, width), BF), pltpu.SemaphoreType.DMA((2,))],
         deps,
-        VMEM_LARGE,
     )
 
 
@@ -249,7 +245,7 @@
     inputs = [p for g in groups for p in g] + ([] if weight is None else [weight]) + [tables]
 
     def body(*refs):
-        refs, out = refs[:-1], refs[-1]
+        refs, outs = refs[: len(inputs)], refs[len(inputs) :]
         for i, c in enumerate(pairs):
             table = refs[-1][c]
             cols = slice(i * count, (i + 1) * count)
@@ -258,25 +254,24 @@
                     here = refs[j * n + i][start : start + step]
                     if weight is not None:
                         here = (here.astype(F32) * refs[-2][c]).astype(BF)
-                    at = j * units + start
-                    out[at : at + step, cols] = dot(here, table, 1, 1).astype(BF)
+                    outs[j][start : start + step, cols] = dot(here, table, 1, 1).astype(BF)
             token = lax.broadcasted_iota(jnp.int32, (TAGS, rows), 1) + c * rows
             row = lax.broadcasted_iota(jnp.int32, (TAGS, rows), 0)
             token = jnp.where(row == 0, token // 256, jnp.where(row == 1, token % 256, 0))
             tags = dot(token.astype(F32).astype(BF), table, 1, 1)
-            out[len(groups) * units :, cols] = tags.astype(BF)
-
-    shape = (len(groups) * units + TAGS, n * count)
+            for out in outs:
+                out[units:, cols] = tags.astype(BF)
+
+    shape = (units + TAGS, n * count)
     return call(
         body,
         "pack",
         (1,),
         [whole(a) for a in inputs],
-        [(shape, BF, shape, lambda i: (0, 0))],
+        [(shape, BF, shape, lambda i: (0, 0))] * len(groups),
         (),
         deps,
-        VMEM_LARGE,
-    )[0]
+    )
 
 
 def spread(packed, tags, rows, first=0):
@@ -294,14 +289,24 @@
     m, n = len(packed), len(blocks)
 
     def body(valid, *refs):
-        blocks, packed, (out, total, whole_rows, sem) = refs[:n], refs[n : n + m], refs[n + m :]
-        fetch(blocks, whole_rows, sem)
+        blocks, packed, (out, total, whole_rows, held, sem) = refs[:n], refs[n : n + m], refs[n + m :]
+        moves = copies(blocks, whole_rows, sem)
+        for move in moves:
+            move.start()
+        arrivals = [
+            pltpu.make_async_copy(packed[i], held.at[i], sem.at[n + i]) for i in range(m)
+        ]
+        for move in arrivals:
+            move.start()
         total[...] = jnp.zeros_like(total)
+        for move in moves:
+            move.wait()
         for i in range(m):
+            arrivals[i].wait()
 
             @pl.when(valid[i] > 0)
             def _():
-                left = spread(packed[i][:units], packed[i][units:], rows)
+                left = spread(held[i, :units], held[i, units:], rows)
                 cols = slice(order[i] * share, (order[i] + 1) * share)
                 total[...] += dot(left, whole_rows[:, cols], 1, 0)
 
@@ -311,87 +316,143 @@
         body,
         "sum_products",
         (1,),
-        [(valid, pltpu.SMEM)] + [(b, pl.ANY) for b in blocks] + [whole(a) for a in packed],
+        [(valid, pltpu.SMEM)] + [(a, pltpu.HBM) for a in (*blocks, *packed)],
         [((units, share), BF, (units, share), lambda i: (0, 0))],
         [
             pltpu.VMEM((units, share), F32),
             pltpu.VMEM((rows, width), BF),
-            pltpu.SemaphoreType.DMA((n,)),
+            pltpu.VMEM((m, *packed[0].shape), BF),
+            pltpu.SemaphoreType.DMA((n + m,)),
         ],
         deps,
         VMEM_LARGE,
     )[0]
 
 
-def input_grad(gate_grad, up_grad, gate_wt, up_wt, sums, deps=()):
-    units, rows = gate_grad.shape
+def input_grad(gate_grads, up_grads, gate_wt, up_wt, sums, deps=()):
+    units, rows = gate_grads[0].shape
     width = gate_wt.shape[1]
     tile = 512
     half = rows // 2
-    picks = sums.shape[0]
-
-    def body(gate_grad, up_grad, gate_wt, up_wt, sums, own, other, g, u):
-        @pl.when(pl.program_id(0) == 0)
+    chips = len(gate_grads)
+    picks = sums[0].shape[0]
+
+    def body(*refs):
+        grads, (gate_wt, up_wt), refs = refs[: 2 * chips], refs[2 * chips : 2 * chips + 2], refs[2 * chips + 2 :]
+        sums, outs, turned = refs[:chips], refs[chips : 3 * chips], refs[3 * chips :]
+        step = pl.program_id(0)
+
+        @pl.when(step == 0)
         def _():
-            g[...] = gate_grad[...].T
-            u[...] = up_grad[...].T
-
-        total = dot(g[...], gate_wt[...], 1, 0) + dot(u[...], up_wt[...], 1, 0)
-        for i, out in enumerate((own, other)):
-            out[:half] = total[i * half : (i + 1) * half].astype(BF)
-            out[half:] = jnp.zeros((TAGS, tile), BF)
-
-            @pl.when(pl.program_id(0) == 0)
-            def _():
-                left = sums[:, i * half : (i + 1) * half]
-                parts = []
-                for _ in range(3):
-                    parts.append(left.astype(BF).astype(F32))
-                    left = left - parts[-1]
-                parts.append(jnp.zeros((TAGS - 3 * picks, half), F32))
-                out[half:, :half] = jnp.concatenate(parts, axis=0).astype(BF)
+            for a, b in zip(grads, turned):
+                b[...] = a[...].T
+
+        for c in range(chips):
+            total = dot(turned[c][...], gate_wt[...], 1, 0)
+            total = total + dot(turned[chips + c][...], up_wt[...], 1, 0)
+            for i in range(2):
+                out = outs[2 * c + i]
+                out[:half] = total[i * half : (i + 1) * half].astype(BF)
+                out[half:] = jnp.zeros((TAGS, tile), BF)
+
+                @pl.when(step == 0)
+                def _():
+                    left = sums[c][:, i * half : (i + 1) * half]
+                    parts = []
+                    for _ in range(3):
+                        parts.append(left.astype(BF).astype(F32))
+                        left = left - parts[-1]
+                    parts.append(jnp.zeros((TAGS - 3 * picks, half), F32))
+                    out[half:, :half] = jnp.concatenate(parts, axis=0).astype(BF)
 
     at = lambda i: (0, i)
-    return call(
+    outs = call(
         body,
         "input_grad",
         (width // tile,),
-        [whole(gate_grad), whole(up_grad)]
+        [whole(a) for a in (*gate_grads, *up_grads)]
         + [(w, (units, tile), at) for w in (gate_wt, up_wt)]
-        + [whole(sums)],
-        [((half + TAGS, width), BF, (half + TAGS, tile), at)] * 2,
-        [pltpu.VMEM((rows, units), BF)] * 2,
+        + [whole(a) for a in sums],
+        [((half + TAGS, width), BF, (half + TAGS, tile), at)] * (2 * chips),
+        [pltpu.VMEM((rows, units), BF)] * (2 * chips),
         deps,
         VMEM_LARGE,
     )
-
-
-def weight_grad(x_pairs, grads, shares, replicas, fold=None, deps=()):
-    chips = len(x_pairs)
+    return [(outs[2 * c], outs[2 * c + 1]) for c in range(chips)]
+
+
+def finish_tokens(sums, experts, tok_count, picks, deps=()):
+    chips = experts // 2
+    moved = [chip_shift(sums[k], experts, chips - k, "token_grads") for k in range(1, chips)]
+    width = sums[0].shape[1]
+
+    def body(*refs):
+        refs, (grads, out) = refs[:chips], refs[chips:]
+        total = refs[0][...].astype(F32)
+        for ref in refs[1:]:
+            total = total + ref[...].astype(F32)
+        grads[...] = total[:tok_count].astype(BF)
+        parts = total[tok_count:, :tok_count]
+        out[...] = parts[:picks] + parts[picks : 2 * picks] + parts[2 * picks : 3 * picks]
+
+    at = lambda i: (0, 0)
+    grads, sums = call(
+        body,
+        "finish_tokens",
+        (1,),
+        [whole(a) for a in (sums[0], *moved)],
+        [((tok_count, width), BF, (tok_count, width), at), ((picks, tok_count), F32, (picks, tok_count), at)],
+        (),
+        deps,
+    )
+    return grads, sums.T
+
+
+def choose(flag, a, b, deps=()):
+    def body(flag, a, b, out):
+        out[0] = jnp.where(flag[0] > 0, a[...], b[...])
+
+    return call(
+        body,
+        "choose",
+        (1,),
+        [(flag, pltpu.SMEM), whole(a), whole(b)],
+        [((1, *a.shape), BF, (1, *a.shape), lambda i: (0, 0, 0))],
+        (),
+        deps,
+    )[0]
+
+
+def weight_grad(x_pairs, grads, shares, replicas, fold=None, deps=(), joined=False, space=pltpu.HBM):
+    chips, n = len(x_pairs), shares.shape[0]
     blocks = flat(x_pairs)
-    small = list(grads)
     units, rows = grads[0].shape
     width = blocks[0].shape[1]
+    packed = []
     if fold is not None:
         blocks = blocks + flat(fold[0])
-        small = small + [fold[1]]
+        packed = [fold[1]]
     total = len(blocks) * blocks[0].shape[0]
     share = width // replicas
 
     def body(shares, *refs):
         blocks_in, refs = refs[: len(blocks)], refs[len(blocks) :]
-        small_in, (out, x, g, sem) = refs[: len(small)], refs[len(small) :]
+        grads_in, refs = refs[:chips], refs[chips:]
+        packed_in, refs = refs[: len(packed)], refs[len(packed) :]
+        outs, (x, g, sem) = refs[:-3], refs[-3:]
         step = pl.program_id(0)
 
         @pl.when(step == 0)
         def _():
-            moves = copies(blocks_in, x, sem)
+            moves = copies(blocks_in, x, sem, chips)
+            if not joined:
+                moves = copies(grads_in, g, sem, 0, 1) + moves
             for m in moves:
                 m.start()
-            for i in range(chips):
-                g[:, i * rows : (i + 1) * rows] = small_in[i][...]
-            if fold is not None:
-                packed = small_in[chips]
+            if joined:
+                for i in range(chips):
+                    g[:, i * rows : (i + 1) * rows] = grads_in[i][...]
+            for packed in packed_in:
                 for i in range(chips):
                     part = slice(i * packed.shape[1] // chips, (i + 1) * packed.shape[1] // chips)
                     at = (chips + i) * rows
@@ -402,22 +463,52 @@
                 m.wait()
 
         cols = pl.ds(pl.multiple_of(shares[step] * share, share), share)
-        out[0] = dot(g[...], x[:, cols], 1, 0).astype(BF)
-
-    n = shares.shape[0]
+        value = dot(g[...], x[:, cols], 1, 0).astype(BF)
+        if joined:
+            outs[0][0] = value
+        else:
+            for i, out in enumerate(outs):
+
+                @pl.when(step == i)
+                def _():
+                    out[...] = value
+
+    if joined:
+        outputs = [((n, units, share), BF, (1, units, share), lambda i: (i, 0, 0))]
+    else:
+        outputs = [((units, share), BF, (units, share), lambda i: (0, 0))] * n
     return call(
         body,
         "weight_grad",
         (n,),
-        [(shares, pltpu.SMEM)] + [(b, pl.ANY) for b in blocks] + [whole(a) for a in small],
-        [((n, units, share), BF, (1, units, share), lambda i: (i, 0, 0))],
+        [(shares, pltpu.SMEM)]
+        + [(b, space) for b in blocks]
+        + [whole(a) if joined else (a, space) for a in grads]
+        + [whole(a) for a in packed],
+        outputs,
         [
             pltpu.VMEM((total, width), BF),
             pltpu.VMEM((units, total), BF),
-            pltpu.SemaphoreType.DMA((len(blocks),)),
+            pltpu.SemaphoreType.DMA((len(blocks) + chips,)),
         ],
         deps,
         VMEM_LARGE,
+    )
+
+
+def turned_sum(a, b, part, deps=()):
+    def body(a, b, out):
+        out[...] = (a[...].astype(F32) + b[0].astype(F32)).T.astype(BF)
+
+    shape = (a.shape[1], a.shape[0])
+    return call(
+        body,
+        "turned_sum",
+        (1,),
+        [whole(a), (b, (1, *a.shape), lambda i: (part, 0, 0))],
+        [(shape, BF, shape, lambda i: (0, 0))],
+        (),
+        deps,
     )[0]
 
 
@@ -458,7 +549,7 @@
     info = jnp.stack([jnp.concatenate(pair, axis=1) for pair in info])
     fwd += [forward(pair, gate_wt, up_wt) for pair in x[1:]]
     tables, weights = slots(info, me, count // chips)
-    packed = pack([[f[0] for f in fwd]], tables, pairs, weights)
+    packed = pack([[f[0] for f in fwd]], tables, pairs, weights)[0]
     right = [line_step(packed, 0, replicas, 1, "hidden")]
     left = [line_step(packed, 0, replicas, -1, "hidden")]
     og_far, og_core, og_shares, fwd, tables, weights, x, x_fold, info = meet(
@@ -477,25 +568,21 @@
     og_rows = jnp.concatenate(og_shares, axis=1)
 
     def input_grads(deps=()):
-        halves = []
-        for c, (gate, up, sums) in enumerate(bwd):
-            sums = jnp.where(info[c, :pick_width] == me, sums, 0.0)
-            halves.append(input_grad(gate, up, gate_wt, up_wt, sums, deps))
-        return halves
-
-    def grad_down(og_rows):
+        sums = [jnp.where(info[c, :pick_width] == me, b[2], 0.0) for c, b in enumerate(bwd)]
+        return input_grad([b[0] for b in bwd], [b[1] for b in bwd], gate_wt, up_wt, sums, deps)
+
+    def grad_down(og_rows, deps=()):
         gathered, blocks, valid = [packed], [0], [z >= 0]
         for t in range(replicas - 1):
             gathered += [right[t], left[t]]
             blocks += [t + 1, replicas - 1 - t]
             valid += [z - 1 - t >= 0, z + 1 + t < replicas]
         valid = jnp.stack(valid).astype(jnp.int32)
-        return sum_products(gathered, valid, flat(og_rows), blocks, replicas)
+        return sum_products(gathered, valid, flat(og_rows), blocks, replicas, deps)
 
     if folding:
         x_there = [chip_shift(x_fold, experts, k, "tokens_fold") for k in range(1, chips)]
-        gate_packed = pack([gate_grad], tables, pairs)
-        up_packed = pack([up_grad], tables, pairs, None, [gate_packed])
+        gate_packed, up_packed = pack([gate_grad, up_grad], tables, pairs)
         gate_there = inward(gate_packed, replicas, "gate_grad")
         up_there = inward(up_packed, replicas, "up_grad")
         right, left, bwd, gate_grad, up_grad, og_rows, x_there = meet(
@@ -508,7 +595,8 @@
         gate_there, x_there, gate_grad = meet((gate_there, x_there, gate_grad))
 
         order = jnp.where(z < 2, jnp.arange(3, -1, -1), jnp.arange(4)).astype(jnp.int32)
-        gate_sent = weight_grad(x, gate_grad, order[:2], replicas, (x_there, gate_there))
+        fold = (x_there, gate_there)
+        gate_sent = weight_grad(x, gate_grad, order[:2], replicas, fold, (), True, pl.ANY)[0]
         gate_met = across(gate_sent, "gate_sums")
         og_rows = [(b, core_swap(b, experts, "out_grad_share")) for b in og_rows]
         up_there, gate_sent, gate_there, x_there, gate_grad, up_grad, right, left = meet(
@@ -517,47 +605,47 @@
 
         up_sent = weight_grad(x, up_grad, order[:2], replicas, (x_there, up_there))
         up_met = [across(up_sent[0], "up_far_sums"), across(up_sent[1], "up_sums")]
-        gate_kept = weight_grad(x, gate_grad, order[2:], replicas, (x_there, gate_there), [up_sent])
-        up_kept = weight_grad(x, up_grad, order[2:], replicas, (x_there, up_there), [gate_kept])
+        gate_kept = weight_grad(x, gate_grad, order[2:], replicas, (x_there, gate_there), up_sent)
         onward(2)
-        halves = input_grads([up_kept])
-        gate_met, gate_kept, up_kept, halves, og_rows, right, left = meet(
-            (gate_met, gate_kept, up_kept, halves, og_rows, right, left)
+        halves = input_grads(gate_kept)
+        gate_met, gate_kept, up_grad, halves, og_rows, right, left = meet(
+            (gate_met, gate_kept, up_grad, halves, og_rows, right, left)
         )
-
-        gate_far = outward(add(gate_kept[1], gate_met[0]).T, replicas, "gate_sums")
-        gate_own = add(gate_kept[0], gate_met[1]).T
+        up_kept = weight_grad(x, up_grad, order[2:], replicas, (x_there, up_there))
+
+        gate_far = outward(turned_sum(gate_kept[1], gate_met, 0), replicas, "gate_sums")
         sums = return_sums(halves, experts, "token_grads")
-        down = grad_down(og_rows)
-        up_met[0], up_kept, gate_own, sums, down = meet(
-            (up_met[0], up_kept, gate_own, sums, down)
+        gate_own = turned_sum(gate_kept[0], gate_met, 1, up_kept)
+        up_met[0], up_kept, sums, gate_own, gate_far = meet(
+            (up_met[0], up_kept, sums, gate_own, gate_far)
         )
 
-        outer = (z == 0) | (z == replicas - 1)
-        up_far = outward(add(up_kept[1], up_met[0]).T, replicas, "up_sums")
-        grads = return_shift(sums, experts, "token_grads")
-        gate_share = jnp.where(outer, gate_far, gate_own)
-        up_share = jnp.where(outer, up_far, add(up_kept[0], up_met[1]).T)
+        outer = ((z == 0) | (z == replicas - 1)).astype(jnp.int32).reshape(1)
+        up_far = turned_sum(up_kept[1], up_met[0][None], 0)
+        gate_share = choose(outer, gate_far, gate_own, [up_far])
+        down = grad_down(og_rows, [gate_share])
+        up_far = outward(up_far, replicas, "up_sums")
+        up_own = turned_sum(up_kept[0], up_met[1][None], 0, [down])
+        token_grads, gate_grads = finish_tokens(sums, experts, tok_count, pick_width, [up_own])
+        up_share = choose(outer, up_far, up_own, [token_grads])
     else:
         every = jnp.arange(replicas, dtype=jnp.int32)
 
         def scatter(grads):
-            total = weight_grad(x, grads, every, replicas)
-            return lax.psum_scatter(total, "dp", scatter_dimension=0, tiled=True)[0].T
+            total = jnp.stack(weight_grad(x, grads, every, replicas))
+            return lax.psum_scatter(total, "dp", scatter_dimension=0, tiled=True)[0].T[None]
 
         gate_share, up_share = scatter(gate_grad), scatter(up_grad)
         for t in range(1, replicas - 1):
             onward(t)
-        grads = return_shift(return_sums(input_grads(), experts, "token_grads"), experts, "token_grads")
+        sums = return_sums(input_grads(), experts, "token_grads")
+        token_grads, gate_grads = finish_tokens(sums, experts, tok_count, pick_width)
         down = grad_down(gather_pairs(og_rows, experts, "out_grad_share"))
-    token_grads = grads[:tok_count]
-    sums = grads[tok_count:, :tok_count].astype(F32)
-    gate_grads = sum(sums[i * pick_width : (i + 1) * pick_width] for i in range(3)).T
     return (
         token_grads,
         gate_grads,
-        gate_share[None],
-        up_share[None],
+        gate_share,
+        up_share,
         down[None],
     )
 

time: 210 us -> 197 us (0.938)
  Pallas kernels: 70.9 us -> 88.1 us
  local copies, waits for them, and re-layouts: 30.6 us -> 16.3 us
  other arithmetic: 16.3 us -> 8.53 us
  waiting for transfers between devices: 37.7 us -> 30.1 us
    pallas_call x16 -> x21, Pallas kernels: 70.9 us -> 88.1 us  [call(): pl.pallas_call(kernel, grid=grid, in_specs=[spec(e) for e in inputs] + [p...]
    unnamed x114 -> x64, local copies, waits for them, and re-layouts: 25 us -> 13.5 us
    ppermute x35, waiting for transfers between devices: 37.7 us -> 30.1 us  [send(): return lax.ppermute(x, axis, pairs)]
    transpose x3 -> x0, other arithmetic: 4.66 us -> none  [the longest x1 2.96 us: on_device(): gate_far = outward(add(gate_kept[1], gate_met[0]).T, replicas, 'gate_sums')]
    broadcast_in_dim x2 -> x0, other arithmetic: 2.9 us -> none  [the longest x1 1.68 us: on_device(): up_share[None]]
    squeeze x1 -> x0, local copies, waits for them, and re-layouts: 2.35 us -> none  [on_device(): up_met = [across(up_sent[0], 'up_far_sums'), across(up_sent[1], 'up_sums')]]
    convert_element_type x3 -> x2, other arithmetic: 5.2 us -> 3.94 us  [add(): return total.astype(terms[0].dtype)]
  transfers between devices with their start and end apart: 35 -> 35, of which waited for: 10 -> 9; matrix products, arithmetic and copies ran while one was open for 10% -> 6% of each run, Pallas kernels for 34% -> 44%
where the time goes in v3:
time: 197 us; the launch traced here: 196 us
  Pallas kernels  88.1 us (45%)
  starting transfers between devices  51.7 us (26%)
  waiting for transfers between devices  30.1 us (15%)
  local copies, waits for them, and re-layouts  16.3 us (8%)
  other arithmetic  8.53 us (4%)
    pallas_call x21, Pallas kernels, call(): pl.pallas_call(kernel, grid=grid, in_specs=[spec(e) for e in inputs] + [p...  88.1 us
    ppermute x35, starting transfers between devices, send(): return lax.ppermute(x, axis, pairs)  51.7 us
    ppermute x35, waiting for transfers between devices, send(): return lax.ppermute(x, axis, pairs)  30.1 us
    unnamed x64, local copies, waits for them, and re-layouts  13.5 us
  transfers between devices with their start and end apart: 35, of which 9 were waited for; matrix products, arithmetic and copies ran while one was open for 6% of the time, Pallas kernels for 44%

profile of v3, /device:TPU:0, one launch (start us, length us, event | category | flops | bytes accessed | tf_op | source)
XLA Modules:
  0.0 196.0 jit_solution(16154452658598484775)
XLA Ops:
  1.1 2.6 %collective-permute-start = (bf16[192,2048]{1,0:T(8,128)(2,1)}, bf16[192,2048]{1,0:T(8,128)(2,1)}, u32[]{:S(2)}, u32[]{:S(2)}) collective-permute-start(bf16[192,2048]{1,0:T(8,128)(2,1)} %refs_1_.3), channel_id=1, source_target_pairs={{8,0},{12,4},{0,8},{4,12},{9,1},{13,5},{1,9},{5,13},{10,2},{14,6},... | collective-permute-start | bytes 2359304 | tf_op jit(solution)/shard_map/tokens_chip/ppermute | solution.py:23
  3.7 4.4 %collective-permute-start.2 = (bf16[192,2048]{1,0:T(8,128)(2,1)}, bf16[192,2048]{1,0:T(8,128)(2,1)}, u32[]{:S(2)}, u32[]{:S(2)}) collective-permute-start(bf16[192,2048]{1,0:T(8,128)(2,1)} %refs_1_.3), channel_id=1, source_target_pairs={{0,1},{3,2},{4,5},{7,6},{8,9},{11,10},{12,13},{15,14},{16,17},{19,... | collective-permute-start | bytes 2359304 | tf_op jit(solution)/shard_map/tokens_inward/ppermute | solution.py:23
  10.0 1.9 copy-done.11
  11.9 1.9 copy-done.12
  13.8 2.3 %turned.1 = (bf16[768,2048]{1,0:T(8,128)(2,1)S(1)}, bf16[768,2048]{1,0:T(8,128)(2,1)S(1)}) custom-call(bf16[2048,768]{1,0:T(8,128)(2,1)S(1)} %bitcast.33, bf16[2048,768]{1,0:T(8,128)(2,1)S(1)} %bitcast.34), custom_call_target="tpu_custom_call" | custom-call | flops 1000 | bytes 1000 | tf_op jit(solution)/shard_map/turned/pallas_call | solution.py:92
  16.2 4.0 %forward.2 = (bf16[768,384]{1,0:T(8,128)(2,1)S(1)}, bf16[768,384]{1,0:T(8,128)(2,1)S(1)}, bf16[768,384]{1,0:T(8,128)(2,1)S(1)}) custom-call(bf16[192,2048]{1,0:T(8,128)(2,1)S(1)} %copy-done.3, bf16[192,2048]{1,0:T(8,128)(2,1)S(1)} %collective-permute-done.3.refs_1_.refs_2_, bf16[768,2048]{1,0:T(8,128)(2,1)S(1)} %get-tuple-element.136.refs_2_.refs_4_, ...), custom_call_target="tpu_custom_call" | custom-call | flops 1000 | bytes 1000 | tf_op jit(solution)/shard_map/forward/pallas_call | solution.py:92
  20.2 0.8 copy-done.20
  21.0 0.8 copy-done.23
  21.8 0.8 copy-done.25
  22.6 2.0 %collective-permute-done.2.refs_5_ = bf16[192,2048]{1,0:T(8,128)(2,1)} collective-permute-done((bf16[192,2048]{1,0:T(8,128)(2,1)}, bf16[192,2048]{1,0:T(8,128)(2,1)}, u32[]{:S(2)}, u32[]{:S(2)}) %collective-permute-start.2) | collective-permute-done | bytes 786464 | tf_op jit(solution)/shard_map/tokens_inward/ppermute | solution.py:23
  25.7 2.0 %constant_dynamic-slice_fusion = (bf16[192,512]{1,0:T(8,128)(2,1)}, bf16[192,512]{1,0:T(8,128)(2,1)}, bf16[192,512]{1,0:T(8,128)(2,1)S(1)}, bf16[192,512]{1,0:T(8,128)(2,1)}) fusion(bf16[192,2048]{1,0:T(8,128)(2,1)} %refs_0_.2, s32[]{:T(128)S(6)} %select_n.55, s32[]{:T(128)S(6)} %select_n.51, s32[]{:T(128)S(6)} %select_n.49, s32[]{:T(128)S(6)} %select_n.53), kind=kLoop, calls=%fused_computation.12 | loop fusion | bytes 1572880 | tf_op jit(solution)/shard_map/dynamic_slice | solution.py:537
  27.7 2.5 %collective-permute-start.6 = (bf16[192,512]{1,0:T(8,128)(2,1)}, bf16[192,512]{1,0:T(8,128)(2,1)}, u32[]{:S(2)}, u32[]{:S(2)}) collective-permute-start(bf16[192,512]{1,0:T(8,128)(2,1)} %get-tuple-element.248), channel_id=1, source_target_pairs={{0,1},{1,2},{2,3},{3,0},{4,5},{5,6},{6,7},{7,4},{8,9},{9,10},{10,1... | collective-permute-start | bytes 589832 | tf_op jit(solution)/shard_map/out_grad_share_rotated/ppermute | solution.py:23
  30.3 1.1 collective-permute-done.11
  31.4 1.1 collective-permute-start.7
  32.5 2.9 %collective-permute-start.8 = (bf16[192,512]{1,0:T(8,128)(2,1)}, bf16[192,512]{1,0:T(8,128)(2,1)S(1)}, u32[]{:S(2)}, u32[]{:S(2)}) collective-permute-start(bf16[192,512]{1,0:T(8,128)(2,1)} %get-tuple-element.247), channel_id=1, source_target_pairs={{0,3},{1,0},{2,1},{3,2},{4,7},{5,4},{6,5},{7,6},{8,11},{9,8},{10,9... | collective-permute-start | bytes 589832 | tf_op jit(solution)/shard_map/out_grad_share_rotated/ppermute | solution.py:23
  35.4 1.2 slots.1
  36.6 1.9 copy-done.2
  38.5 5.4 %forward.3 = (bf16[768,384]{1,0:T(8,128)(2,1)S(1)}, bf16[768,384]{1,0:T(8,128)(2,1)S(1)}, bf16[768,384]{1,0:T(8,128)(2,1)S(1)}) custom-call(bf16[192,2048]{1,0:T(8,128)(2,1)} %collective-permute-done.refs_0_.refs_3_, bf16[192,2048]{1,0:T(8,128)(2,1)} %collective-permute-done.9.refs_1_.refs_4_, bf16[768,2048]{1,0:T(8,128)(2,1)S(1)} %get-tuple-element.136.refs_2_.refs_4_, ...), custom_call_target="tpu_custom_call" | custom-call | flops 1000 | bytes 1000 | tf_op jit(solution)/shard_map/forward/pallas_call | solution.py:92
  43.9 1.3 collective-permute-done.7
  45.4 0.7 pack.3.refs_5_
  46.1 7.5 %collective-permute-start.16 = (bf16[784,512]{1,0:T(8,128)(2,1)S(1)}, bf16[784,512]{1,0:T(8,128)(2,1)}, u32[]{:S(2)}, u32[]{:S(2)}) collective-permute-start(bf16[784,512]{1,0:T(8,128)(2,1)S(1)} %pack.3.refs_5_), channel_id=1, source_target_pairs={{0,1},{1,2},{2,3},{4,5},{5,6},{6,7},{8,9},{9,10},{10,11},{12,13},{... | collective-permute-start | bytes 2408456 | tf_op jit(solution)/shard_map/hidden_right/ppermute | solution.py:23
  53.6 1.3 collective-permute-start.17
  54.9 1.6 collective-permute-start.18
  56.5 3.7 %backward.2 = (bf16[768,384]{1,0:T(8,128)(2,1)S(1)}, bf16[768,384]{1,0:T(8,128)(2,1)S(1)}, f32[1,384]{1,0:T(1,128)S(1)}) custom-call(bf16[192,2048]{1,0:T(8,128)(2,1)} %refs_0_.2, bf16[192,2048]{1,0:T(8,128)(2,1)} %collective-permute-done.5.refs_1_, bf16[768,2048]{1,0:T(8,128)(2,1)S(1)} %bitcast.31, f32[1,384]{1,0:T(1,128)S(1)} %get-tuple-element.254.refs_3_, ...), custom_call_target="tpu_custom_call" | custom-call | flops 1000 | bytes 1000 | tf_op jit(solution)/shard_map/backward/pallas_call | solution.py:92
  60.3 3.9 %backward.3 = (bf16[768,384]{1,0:T(8,128)(2,1)S(1)}, bf16[768,384]{1,0:T(8,128)(2,1)S(1)}, f32[1,384]{1,0:T(1,128)S(1)}) custom-call(bf16[192,2048]{1,0:T(8,128)(2,1)} %collective-permute-done.4.refs_0_, bf16[192,2048]{1,0:T(8,128)(2,1)S(1)} %collective-permute-done.12.refs_1_, bf16[768,2048]{1,0:T(8,128)(2,1)S(1)} %bitcast.32, ...), custom_call_target="tpu_custom_call" | custom-call | flops 1000 | bytes 1000 | tf_op jit(solution)/shard_map/backward/pallas_call | solution.py:92
  64.2 1.9 pack.2
  66.2 5.4 %collective-permute-start.14 = (bf16[784,512]{1,0:T(8,128)(2,1)}, bf16[784,512]{1,0:T(8,128)(2,1)}, u32[]{:S(2)}, u32[]{:S(2)}) collective-permute-start(bf16[784,512]{1,0:T(8,128)(2,1)} %get-tuple-element.165), channel_id=1, source_target_pairs={{0,1},{3,2},{4,5},{7,6},{8,9},{11,10},{12,13},{15,14},{16,17},{19,... | collective-permute-start | bytes 2408456 | tf_op jit(solution)/shard_map/gate_grad_inward/ppermute | solution.py:23
  71.6 1.9 pad_maximum_fusion.refs_1_
  73.5 1.4 collective-permute-done.18.refs_7_
  75.6 3.7 %collective-permute-start.13 = (bf16[784,512]{1,0:T(8,128)(2,1)}, bf16[784,512]{1,0:T(8,128)(2,1)S(1)}, u32[]{:S(2)}, u32[]{:S(2)}) collective-permute-start(bf16[784,512]{1,0:T(8,128)(2,1)} %copy-done.27), channel_id=1, source_target_pairs={{0,1},{3,2},{4,5},{7,6},{8,9},{11,10},{12,13},{15,14},{16,17},{19,... | collective-permute-start | bytes 2408456 | tf_op jit(solution)/shard_map/up_grad_inward/ppermute | solution.py:23
  79.3 1.6 collective-permute-start.20
  80.9 1.3 collective-permute-start.21
  82.8 1.5 collective-permute-start.25
  84.3 4.9 %collective-permute-done.14.refs_11_ = bf16[784,512]{1,0:T(8,128)(2,1)} collective-permute-done((bf16[784,512]{1,0:T(8,128)(2,1)}, bf16[784,512]{1,0:T(8,128)(2,1)}, u32[]{:S(2)}, u32[]{:S(2)}) %collective-permute-start.14) | collective-permute-done | bytes 802848 | tf_op jit(solution)/shard_map/gate_grad_inward/ppermute | solution.py:23
  89.2 8.3 %weight_grad.4 = bf16[2,768,512]{2,1,0:T(8,128)(2,1)} custom-call(s32[2]{0:T(128)} %get-tuple-element.256.refs_0_, bf16[192,2048]{1,0:T(8,128)(2,1)} %refs_1_.3, bf16[192,2048]{1,0:T(8,128)(2,1)} %copy-done.4, bf16[192,2048]{1,0:T(8,128)(2,1)} %collective-permute-done.refs_0_.refs_3_, bf16[192,2048]{1,0:T(8,128)(2,1)} %collective-permute-done.9.refs_1_.refs_4_, ...), custom_call_target="tpu_custom_call" | custom-call | flops 1000 | bytes 1000 | tf_op jit(solution)/shard_map/weight_grad/pallas_call | solution.py:92
  97.5 0.8 collective-permute-start.23
  98.3 7.7 %collective-permute-done.13.refs_11_ = bf16[784,512]{1,0:T(8,128)(2,1)S(1)} collective-permute-done((bf16[784,512]{1,0:T(8,128)(2,1)}, bf16[784,512]{1,0:T(8,128)(2,1)S(1)}, u32[]{:S(2)}, u32[]{:S(2)}) %collective-permute-start.13) | collective-permute-done | bytes 802848 | tf_op jit(solution)/shard_map/up_grad_inward/ppermute | solution.py:23
  106.0 1.6 collective-permute-start.27
  107.6 1.5 collective-permute-start.28
  110.3 8.5 %weight_grad.5 = (bf16[768,512]{1,0:T(8,128)(2,1)}, bf16[768,512]{1,0:T(8,128)(2,1)}) custom-call(s32[2]{0:T(128)} %get-tuple-element.256.refs_0_, bf16[192,2048]{1,0:T(8,128)(2,1)} %refs_1_.3, bf16[192,2048]{1,0:T(8,128)(2,1)} %copy-done.4, bf16[192,2048]{1,0:T(8,128)(2,1)} %collective-permute-done.refs_0_.refs_3_, ...), custom_call_target="tpu_custom_call" | custom-call | flops 1000 | bytes 1000 | tf_op jit(solution)/shard_map/weight_grad/pallas_call | solution.py:92
  118.8 8.5 %weight_grad.6 = (bf16[768,512]{1,0:T(8,128)(2,1)}, bf16[768,512]{1,0:T(8,128)(2,1)}) custom-call(s32[2]{0:T(128)} %get-tuple-element.255.refs_0_, bf16[192,2048]{1,0:T(8,128)(2,1)} %refs_1_.3, bf16[192,2048]{1,0:T(8,128)(2,1)} %copy-done.4, bf16[192,2048]{1,0:T(8,128)(2,1)} %collective-permute-done.refs_0_.refs_3_, ...), custom_call_target="tpu_custom_call" | custom-call | flops 1000 | bytes 1000 | tf_op jit(solution)/shard_map/weight_grad/pallas_call | solution.py:92
  127.3 10.5 %input_grad.1 = (bf16[208,2048]{1,0:T(8,128)(2,1)}, bf16[208,2048]{1,0:T(8,128)(2,1)}, bf16[208,2048]{1,0:T(8,128)(2,1)}, bf16[208,2048]{1,0:T(8,128)(2,1)}) custom-call(bf16[768,384]{1,0:T(8,128)(2,1)} %copy-done.8, bf16[768,384]{1,0:T(8,128)(2,1)} %copy-done.9, bf16[768,384]{1,0:T(8,128)(2,1)} %copy-done.6, bf16[768,384]{1,0:T(8,128)(2,1)} %copy-done.7, ...), custom_call_target="tpu_custom_call" | custom-call | flops 1000 | bytes 1000 | tf_op jit(solution)/shard_map/input_grad/pallas_call | solution.py:92
  138.4 1.6 collective-permute-start.22
  140.0 1.2 turned_sum.5
  141.2 1.4 collective-permute-start.31
  142.6 8.5 %weight_grad.7 = (bf16[768,512]{1,0:T(8,128)(2,1)}, bf16[768,512]{1,0:T(8,128)(2,1)}) custom-call(s32[2]{0:T(128)} %get-tuple-element.255.refs_0_, bf16[192,2048]{1,0:T(8,128)(2,1)} %refs_1_.3, bf16[192,2048]{1,0:T(8,128)(2,1)} %copy-done.4, bf16[192,2048]{1,0:T(8,128)(2,1)} %collective-permute-done.refs_0_.refs_3_, ...), custom_call_target="tpu_custom_call" | custom-call | flops 1000 | bytes 1000 | tf_op jit(solution)/shard_map/weight_grad/pallas_call | solution.py:92
  151.1 1.1 copy-done.13
  152.2 1.1 copy-done.15
  153.7 0.8 copy-done.31
  154.5 2.4 %add_convert_fusion = bf16[208,2048]{1,0:T(8,128)(2,1)} fusion(bf16[208,2048]{1,0:T(8,128)(2,1)} %collective-permute-done.30, bf16[208,2048]{1,0:T(8,128)(2,1)S(1)} %copy-done.31), kind=kLoop, calls=%fused_computation | loop fusion | flops 1703936 | bytes 2555904 | tf_op jit(solution)/shard_map/convert_element_type | solution.py:54
  156.9 1.5 add_convert_fusion.1.refs_0_
  158.5 9.4 %collective-permute-done.31.refs_1_ = bf16[512,768]{1,0:T(8,128)(2,1)} collective-permute-done((bf16[512,768]{1,0:T(8,128)(2,1)}, bf16[512,768]{1,0:T(8,128)(2,1)}, u32[]{:S(2)}, u32[]{:S(2)}) %collective-permute-start.31) | collective-permute-done | bytes 786464 | tf_op jit(solution)/shard_map/gate_sums_outward/ppermute | solution.py:23
  167.8 1.5 collective-permute-start.32
  169.3 1.6 collective-permute-start.33
  170.9 1.4 turned_sum.6.refs_3_
  172.3 1.3 collective-permute-start.34
  174.3 2.1 %choose.2.refs_12_ = bf16[1,512,768]{2,1,0:T(8,128)(2,1)} custom-call(s32[1]{0:T(128)} %bitcast.20.refs_0_, bf16[512,768]{1,0:T(8,128)(2,1)} %collective-permute-done.31.refs_1_, bf16[512,768]{1,0:T(8,128)(2,1)S(1)} %turned_sum.4.refs_2_, bf16[512,768]{1,0:T(8,128)(2,1)S(1)} %turned_sum.6.refs_3_), custom_call_target="tpu_custom_call" | custom-call | flops 1000 | bytes 1000 | tf_op jit(solution)/shard_map/choose/pallas_call | solution.py:92
  176.4 9.9 %sum_products.1.refs_2_ = bf16[768,512]{1,0:T(8,128)(2,1)} custom-call(s32[7]{0:T(128)} %convert_element_type.40.refs_0_, bf16[192,2048]{1,0:T(8,128)(2,1)} %pad_maximum_fusion.refs_1_, bf16[192,2048]{1,0:T(8,128)(2,1)} %collective-permute-done.24.refs_2_, bf16[192,2048]{1,0:T(8,128)(2,1)} %collective-permute-done.25.refs_3_, ...), custom_call_target="tpu_custom_call" | custom-call | flops 1000 | bytes 1000 | tf_op jit(solution)/shard_map/sum_products/pallas_call | solution.py:92
  186.3 1.1 copy-done.18
  187.4 1.4 turned_sum.7.refs_2_
  188.9 2.2 %finish_tokens.1 = (bf16[192,2048]{1,0:T(8,128)(2,1)}, f32[2,192]{1,0:T(2,128)}) custom-call(bf16[208,2048]{1,0:T(8,128)(2,1)S(1)} %add_convert_fusion.1.refs_0_, bf16[208,2048]{1,0:T(8,128)(2,1)} %collective-permute-done.32.refs_1_, bf16[512,768]{1,0:T(8,128)(2,1)S(1)} %turned_sum.7.refs_2_), custom_call_target="tpu_custom_call" | custom-call | flops 1000 | bytes 1000 | tf_op jit(solution)/shard_map/finish_tokens/pallas_call | solution.py:92
  191.1 1.6 collective-permute-done.34.refs_1_
  192.7 1.1 copy-done.22
  193.9 2.1 %choose.3 = bf16[1,512,768]{2,1,0:T(8,128)(2,1)} custom-call(s32[1]{0:T(128)} %bitcast.20.refs_0_, bf16[512,768]{1,0:T(8,128)(2,1)} %collective-permute-done.34.refs_1_, bf16[512,768]{1,0:T(8,128)(2,1)S(1)} %turned_sum.7.refs_2_, bf16[192,2048]{1,0:T(8,128)(2,1)S(1)} %copy-done.22), custom_call_target="tpu_custom_call" | custom-call | flops 1000 | bytes 1000 | tf_op jit(solution)/shard_map/choose/pallas_call | solution.py:92
  (108 shorter events, 7.8 us)
Async XLA Ops:
  0.6 15.5 %collective-permute-start.3 = (bf16[192,2048]{1,0:T(8,128)(2,1)}, bf16[192,2048]{1,0:T(8,128)(2,1)S(1)}, u32[]{:S(2)}, u32[]{:S(2)}) collective-permute-start(bf16[192,2048]{1,0:T(8,128)(2,1)} %refs_1_.3), channel_id=1, source_target_pairs={{0,4},{4,0},{8,12},{12,8},{1,5},{5,1},{9,13},{13,9},{2,6},{6,2},{1... | collective-permute-start | bytes 2359304 | tf_op jit(solution)/shard_map/tokens_core/ppermute | solution.py:23
  1.1 21.5 %collective-permute-start = (bf16[192,2048]{1,0:T(8,128)(2,1)}, bf16[192,2048]{1,0:T(8,128)(2,1)}, u32[]{:S(2)}, u32[]{:S(2)}) collective-permute-start(bf16[192,2048]{1,0:T(8,128)(2,1)} %refs_1_.3), channel_id=1, source_target_pairs={{8,0},{12,4},{0,8},{4,12},{9,1},{13,5},{1,9},{5,13},{10,2},{14,6},... | collective-permute-start | bytes 2359304 | tf_op jit(solution)/shard_map/tokens_chip/ppermute | solution.py:23
  3.7 20.9 %collective-permute-start.2 = (bf16[192,2048]{1,0:T(8,128)(2,1)}, bf16[192,2048]{1,0:T(8,128)(2,1)}, u32[]{:S(2)}, u32[]{:S(2)}) collective-permute-start(bf16[192,2048]{1,0:T(8,128)(2,1)} %refs_1_.3), channel_id=1, source_target_pairs={{0,1},{3,2},{4,5},{7,6},{8,9},{11,10},{12,13},{15,14},{16,17},{19,... | collective-permute-start | bytes 2359304 | tf_op jit(solution)/shard_map/tokens_inward/ppermute | solution.py:23
  9.5 13.1 %collective-permute-start.1 = (f32[4,192]{1,0:T(4,128)S(1)}, f32[4,192]{1,0:T(4,128)S(1)}, u32[]{:S(2)}, u32[]{:S(2)}) collective-permute-start(f32[4,192]{1,0:T(4,128)S(1)} %pad_maximum_fusion.2), channel_id=1, source_target_pairs={{8,0},{12,4},{0,8},{4,12},{9,1},{13,5},{1,9},{5,13},{10,2},{14,6},... | collective-permute-start | bytes 9224 | tf_op jit(solution)/shard_map/routing_chip/ppermute | solution.py:23
  10.0 1.9 copy-start.11
  11.9 1.9 copy-start.12
  13.8 2.4 %copy-start.3 = (bf16[192,2048]{1,0:T(8,128)(2,1)S(1)}, bf16[192,2048]{1,0:T(8,128)(2,1)}, u32[]{:S(2)}) copy-start(bf16[192,2048]{1,0:T(8,128)(2,1)} %refs_1_.3) | copy-start | bytes 2359300
  16.1 4.1 %copy-start.1 = (bf16[768,2048]{1,0:T(8,128)(2,1)}, bf16[768,2048]{1,0:T(8,128)(2,1)S(1)}, u32[]{:S(2)}) copy-start(bf16[768,2048]{1,0:T(8,128)(2,1)S(1)} %get-tuple-element.137.refs_3_.refs_5_) | copy-start | bytes 9437188
  16.1 20.5 %copy-start = (bf16[768,2048]{1,0:T(8,128)(2,1)}, bf16[768,2048]{1,0:T(8,128)(2,1)S(1)}, u32[]{:S(2)}) copy-start(bf16[768,2048]{1,0:T(8,128)(2,1)S(1)} %get-tuple-element.136.refs_2_.refs_4_) | copy-start | bytes 9437188
  16.1 4.0 %copy-start.4 = (bf16[192,2048]{1,0:T(8,128)(2,1)}, bf16[192,2048]{1,0:T(8,128)(2,1)S(1)}, u32[]{:S(2)}) copy-start(bf16[192,2048]{1,0:T(8,128)(2,1)S(1)} %collective-permute-done.3.refs_1_.refs_2_) | copy-start | bytes 2359300
  24.7 7.8 %collective-permute-start.9 = (bf16[192,2048]{1,0:T(8,128)(2,1)}, bf16[192,2048]{1,0:T(8,128)(2,1)}, u32[]{:S(2)}, u32[]{:S(2)}) collective-permute-start(bf16[192,2048]{1,0:T(8,128)(2,1)} %collective-permute-done.refs_0_.refs_3_), channel_id=1, source_target_pairs={{0,4},{4,0},{8,12},{12,8},{1,5},{5,1},{9,13},{13,9},{2,6},{6,2},{1... | collective-permute-start | bytes 2359304 | tf_op jit(solution)/shard_map/tokens_core/ppermute | solution.py:23
  24.7 20.6 %collective-permute-start.4 = (bf16[192,2048]{1,0:T(8,128)(2,1)}, bf16[192,2048]{1,0:T(8,128)(2,1)}, u32[]{:S(2)}, u32[]{:S(2)}) collective-permute-start(bf16[192,2048]{1,0:T(8,128)(2,1)} %refs_0_.2), channel_id=1, source_target_pairs={{8,0},{12,4},{0,8},{4,12},{9,1},{13,5},{1,9},{5,13},{10,2},{14,6},... | collective-permute-start | bytes 2359304 | tf_op jit(solution)/shard_map/out_grad_chip/ppermute | solution.py:23
  25.2 20.1 %collective-permute-start.5 = (bf16[192,2048]{1,0:T(8,128)(2,1)}, bf16[192,2048]{1,0:T(8,128)(2,1)}, u32[]{:S(2)}, u32[]{:S(2)}) collective-permute-start(bf16[192,2048]{1,0:T(8,128)(2,1)} %refs_0_.2), channel_id=1, source_target_pairs={{0,4},{4,0},{8,12},{12,8},{1,5},{5,1},{9,13},{13,9},{2,6},{6,2},{1... | collective-permute-start | bytes 2359304 | tf_op jit(solution)/shard_map/out_grad_core/ppermute | solution.py:23
  25.4 4.8 %collective-permute-start.10 = (f32[4,192]{1,0:T(4,128)S(1)}, f32[4,192]{1,0:T(4,128)S(1)}, u32[]{:S(2)}, u32[]{:S(2)}) collective-permute-start(f32[4,192]{1,0:T(4,128)S(1)} %pad_maximum_fusion.2), channel_id=1, source_target_pairs={{0,4},{4,0},{8,12},{12,8},{1,5},{5,1},{9,13},{13,9},{2,6},{6,2},{1... | collective-permute-start | bytes 9224 | tf_op jit(solution)/shard_map/routing_core/ppermute | solution.py:23
  27.7 16.2 %collective-permute-start.6 = (bf16[192,512]{1,0:T(8,128)(2,1)}, bf16[192,512]{1,0:T(8,128)(2,1)}, u32[]{:S(2)}, u32[]{:S(2)}) collective-permute-start(bf16[192,512]{1,0:T(8,128)(2,1)} %get-tuple-element.248), channel_id=1, source_target_pairs={{0,1},{1,2},{2,3},{3,0},{4,5},{5,6},{6,7},{7,4},{8,9},{9,10},{10,1... | collective-permute-start | bytes 589832 | tf_op jit(solution)/shard_map/out_grad_share_rotated/ppermute | solution.py:23
  30.2 1.2 collective-permute-start.11
  31.4 13.9 %collective-permute-start.7 = (bf16[192,512]{1,0:T(8,128)(2,1)}, bf16[192,512]{1,0:T(8,128)(2,1)S(1)}, u32[]{:S(2)}, u32[]{:S(2)}) collective-permute-start(bf16[192,512]{1,0:T(8,128)(2,1)} %get-tuple-element.250), channel_id=1, source_target_pairs={{0,2},{1,3},{2,0},{3,1},{4,6},{5,7},{6,4},{7,5},{8,10},{9,11},{10,... | collective-permute-start | bytes 589832 | tf_op jit(solution)/shard_map/out_grad_share_rotated/ppermute | solution.py:23
  32.5 12.8 %collective-permute-start.8 = (bf16[192,512]{1,0:T(8,128)(2,1)}, bf16[192,512]{1,0:T(8,128)(2,1)S(1)}, u32[]{:S(2)}, u32[]{:S(2)}) collective-permute-start(bf16[192,512]{1,0:T(8,128)(2,1)} %get-tuple-element.247), channel_id=1, source_target_pairs={{0,3},{1,0},{2,1},{3,2},{4,7},{5,4},{6,5},{7,6},{8,11},{9,8},{10,9... | collective-permute-start | bytes 589832 | tf_op jit(solution)/shard_map/out_grad_share_rotated/ppermute | solution.py:23
  36.6 1.9 copy-start.2
  38.5 6.9 %copy-start.21 = (bf16[768,384]{1,0:T(8,128)(2,1)S(1)}, bf16[768,384]{1,0:T(8,128)(2,1)}, u32[]{:S(2)}) copy-start(bf16[768,384]{1,0:T(8,128)(2,1)} %copy-done.20) | copy-start | bytes 1769476
  38.5 18.0 %copy-start.5 = (bf16[1,768,2048]{2,1,0:T(8,128)(2,1)S(1)}, bf16[1,768,2048]{2,1,0:T(8,128)(2,1)}, u32[]{:S(2)}) copy-start(bf16[1,768,2048]{2,1,0:T(8,128)(2,1)} %param.13) | copy-start | bytes 9437188
  43.9 12.6 %copy-start.24 = (bf16[768,384]{1,0:T(8,128)(2,1)S(1)}, bf16[768,384]{1,0:T(8,128)(2,1)}, u32[]{:S(2)}) copy-start(bf16[768,384]{1,0:T(8,128)(2,1)} %copy-done.23) | copy-start | bytes 1769476
  43.9 12.6 %copy-start.26 = (bf16[768,384]{1,0:T(8,128)(2,1)S(1)}, bf16[768,384]{1,0:T(8,128)(2,1)}, u32[]{:S(2)}) copy-start(bf16[768,384]{1,0:T(8,128)(2,1)} %copy-done.25) | copy-start | bytes 1769476
  45.3 15.0 %collective-permute-start.12 = (bf16[192,2048]{1,0:T(8,128)(2,1)}, bf16[192,2048]{1,0:T(8,128)(2,1)S(1)}, u32[]{:S(2)}, u32[]{:S(2)}) collective-permute-start(bf16[192,2048]{1,0:T(8,128)(2,1)} %collective-permute-done.4.refs_0_), channel_id=1, source_target_pairs={{0,4},{4,0},{8,12},{12,8},{1,5},{5,1},{9,13},{13,9},{2,6},{6,2},{1... | collective-permute-start | bytes 2359304 | tf_op jit(solution)/shard_map/out_grad_core/ppermute | solution.py:23
  46.1 14.1 %copy-start.10 = (bf16[784,512]{1,0:T(8,128)(2,1)}, bf16[784,512]{1,0:T(8,128)(2,1)S(1)}, u32[]{:S(2)}) copy-start(bf16[784,512]{1,0:T(8,128)(2,1)S(1)} %pack.3.refs_5_) | copy-start | bytes 2408452
  46.1 28.8 %collective-permute-start.16 = (bf16[784,512]{1,0:T(8,128)(2,1)S(1)}, bf16[784,512]{1,0:T(8,128)(2,1)}, u32[]{:S(2)}, u32[]{:S(2)}) collective-permute-start(bf16[784,512]{1,0:T(8,128)(2,1)S(1)} %pack.3.refs_5_), channel_id=1, source_target_pairs={{0,1},{1,2},{2,3},{4,5},{5,6},{6,7},{8,9},{9,10},{10,11},{12,13},{... | collective-permute-start | bytes 2408456 | tf_op jit(solution)/shard_map/hidden_right/ppermute | solution.py:23
  53.6 22.0 %collective-permute-start.17 = (bf16[784,512]{1,0:T(8,128)(2,1)S(1)}, bf16[784,512]{1,0:T(8,128)(2,1)}, u32[]{:S(2)}, u32[]{:S(2)}) collective-permute-start(bf16[784,512]{1,0:T(8,128)(2,1)S(1)} %pack.3.refs_5_), channel_id=1, source_target_pairs={{1,0},{2,1},{3,2},{5,4},{6,5},{7,6},{9,8},{10,9},{11,10},{13,12},{... | collective-permute-start | bytes 2408456 | tf_op jit(solution)/shard_map/hidden_left/ppermute | solution.py:23
  54.9 20.0 %collective-permute-start.18 = (bf16[192,2048]{1,0:T(8,128)(2,1)}, bf16[192,2048]{1,0:T(8,128)(2,1)}, u32[]{:S(2)}, u32[]{:S(2)}) collective-permute-start(bf16[192,2048]{1,0:T(8,128)(2,1)} %collective-permute-done.2.refs_5_), channel_id=1, source_target_pairs={{8,0},{12,4},{0,8},{4,12},{9,1},{13,5},{1,9},{5,13},{10,2},{14,6},... | collective-permute-start | bytes 2359304 | tf_op jit(solution)/shard_map/tokens_fold_chip/ppermute | solution.py:23
  56.4 24.5 %collective-permute-start.15 = (bf16[192,2048]{1,0:T(8,128)(2,1)}, bf16[192,2048]{1,0:T(8,128)(2,1)}, u32[]{:S(2)}, u32[]{:S(2)}) collective-permute-start(bf16[192,2048]{1,0:T(8,128)(2,1)} %collective-permute-done.2.refs_5_), channel_id=1, source_target_pairs={{0,4},{4,0},{8,12},{12,8},{1,5},{5,1},{9,13},{13,9},{2,6},{6,2},{1... | collective-permute-start | bytes 2359304 | tf_op jit(solution)/shard_map/tokens_fold_core/ppermute | solution.py:23
  60.2 4.0 %copy-start.6 = (bf16[768,384]{1,0:T(8,128)(2,1)}, bf16[768,384]{1,0:T(8,128)(2,1)S(1)}, u32[]{:S(2)}) copy-start(bf16[768,384]{1,0:T(8,128)(2,1)S(1)} %get-tuple-element.217.refs_2_.refs_9_) | copy-start | bytes 1769476
  60.2 4.0 %copy-start.8 = (bf16[768,384]{1,0:T(8,128)(2,1)}, bf16[768,384]{1,0:T(8,128)(2,1)S(1)}, u32[]{:S(2)}) copy-start(bf16[768,384]{1,0:T(8,128)(2,1)S(1)} %get-tuple-element.201.refs_0_.refs_9_) | copy-start | bytes 1769476
  64.2 9.4 %copy-start.7 = (bf16[768,384]{1,0:T(8,128)(2,1)}, bf16[768,384]{1,0:T(8,128)(2,1)S(1)}, u32[]{:S(2)}) copy-start(bf16[768,384]{1,0:T(8,128)(2,1)S(1)} %get-tuple-element.218.refs_3_.refs_10_) | copy-start | bytes 1769476
  64.2 9.3 %copy-start.9 = (bf16[768,384]{1,0:T(8,128)(2,1)}, bf16[768,384]{1,0:T(8,128)(2,1)S(1)}, u32[]{:S(2)}) copy-start(bf16[768,384]{1,0:T(8,128)(2,1)S(1)} %get-tuple-element.202.refs_1_.refs_10_) | copy-start | bytes 1769476
  66.2 9.4 %copy-start.27 = (bf16[784,512]{1,0:T(8,128)(2,1)}, bf16[784,512]{1,0:T(8,128)(2,1)S(1)}, u32[]{:S(2)}) copy-start(bf16[784,512]{1,0:T(8,128)(2,1)S(1)} %get-tuple-element.164) | copy-start | bytes 2408452
  66.2 23.0 %collective-permute-start.14 = (bf16[784,512]{1,0:T(8,128)(2,1)}, bf16[784,512]{1,0:T(8,128)(2,1)}, u32[]{:S(2)}, u32[]{:S(2)}) collective-permute-start(bf16[784,512]{1,0:T(8,128)(2,1)} %get-tuple-element.165), channel_id=1, source_target_pairs={{0,1},{3,2},{4,5},{7,6},{8,9},{11,10},{12,13},{15,14},{16,17},{19,... | collective-permute-start | bytes 2408456 | tf_op jit(solution)/shard_map/gate_grad_inward/ppermute | solution.py:23
  75.6 7.2 %collective-permute-start.19 = (bf16[192,2048]{1,0:T(8,128)(2,1)}, bf16[192,2048]{1,0:T(8,128)(2,1)S(1)}, u32[]{:S(2)}, u32[]{:S(2)}) collective-permute-start(bf16[192,2048]{1,0:T(8,128)(2,1)} %collective-permute-done.18.refs_7_), channel_id=1, source_target_pairs={{0,4},{4,0},{8,12},{12,8},{1,5},{5,1},{9,13},{13,9},{2,6},{6,2},{1... | collective-permute-start | bytes 2359304 | tf_op jit(solution)/shard_map/tokens_fold_core/ppermute | solution.py:23
  75.6 30.4 %collective-permute-start.13 = (bf16[784,512]{1,0:T(8,128)(2,1)}, bf16[784,512]{1,0:T(8,128)(2,1)S(1)}, u32[]{:S(2)}, u32[]{:S(2)}) collective-permute-start(bf16[784,512]{1,0:T(8,128)(2,1)} %copy-done.27), channel_id=1, source_target_pairs={{0,1},{3,2},{4,5},{7,6},{8,9},{11,10},{12,13},{15,14},{16,17},{19,... | collective-permute-start | bytes 2408456 | tf_op jit(solution)/shard_map/up_grad_inward/ppermute | solution.py:23
  79.3 26.7 %collective-permute-start.20 = (bf16[784,512]{1,0:T(8,128)(2,1)}, bf16[784,512]{1,0:T(8,128)(2,1)}, u32[]{:S(2)}, u32[]{:S(2)}) collective-permute-start(bf16[784,512]{1,0:T(8,128)(2,1)} %collective-permute-done.16.refs_6_), channel_id=1, source_target_pairs={{1,2},{2,3},{5,6},{6,7},{9,10},{10,11},{13,14},{14,15},{17,18},{18... | collective-permute-start | bytes 2408456 | tf_op jit(solution)/shard_map/hidden_right/ppermute | solution.py:23
  80.9 25.1 %collective-permute-start.21 = (bf16[784,512]{1,0:T(8,128)(2,1)}, bf16[784,512]{1,0:T(8,128)(2,1)}, u32[]{:S(2)}, u32[]{:S(2)}) collective-permute-start(bf16[784,512]{1,0:T(8,128)(2,1)} %collective-permute-done.17.refs_7_), channel_id=1, source_target_pairs={{1,0},{2,1},{5,4},{6,5},{9,8},{10,9},{13,12},{14,13},{17,16},{18,1... | collective-permute-start | bytes 2408456 | tf_op jit(solution)/shard_map/hidden_left/ppermute | solution.py:23
  82.8 6.4 %copy-start.28 = (bf16[192,2048]{1,0:T(8,128)(2,1)}, bf16[192,2048]{1,0:T(8,128)(2,1)S(1)}, u32[]{:S(2)}) copy-start(bf16[192,2048]{1,0:T(8,128)(2,1)S(1)} %collective-permute-done.19.refs_8_) | copy-start | bytes 2359300
  82.8 26.3 %collective-permute-start.25 = (bf16[192,2048]{1,0:T(8,128)(2,1)}, bf16[192,2048]{1,0:T(8,128)(2,1)}, u32[]{:S(2)}, u32[]{:S(2)}) collective-permute-start(bf16[192,2048]{1,0:T(8,128)(2,1)} %pad_maximum_fusion.refs_1_), channel_id=1, source_target_pairs={{8,0},{12,4},{0,8},{4,12},{9,1},{13,5},{1,9},{5,13},{10,2},{14,6},... | collective-permute-start | bytes 2359304 | tf_op jit(solution)/shard_map/out_grad_share_chip/ppermute | solution.py:23
  97.5 40.3 %collective-permute-start.23 = (bf16[2,768,512]{2,1,0:T(8,128)(2,1)}, bf16[2,768,512]{2,1,0:T(8,128)(2,1)S(1)}, u32[]{:S(2)}, u32[]{:S(2)}) collective-permute-start(bf16[2,768,512]{2,1,0:T(8,128)(2,1)} %weight_grad.4), channel_id=1, source_target_pairs={{1,2},{2,1},{5,6},{6,5},{9,10},{10,9},{13,14},{14,13},{17,18},{18,... | collective-permute-start | bytes 4718600 | tf_op jit(solution)/shard_map/gate_sums_across/ppermute | solution.py:23
  106.0 4.3 %copy-start.29 = (bf16[784,512]{1,0:T(8,128)(2,1)}, bf16[784,512]{1,0:T(8,128)(2,1)S(1)}, u32[]{:S(2)}) copy-start(bf16[784,512]{1,0:T(8,128)(2,1)S(1)} %collective-permute-done.13.refs_11_) | copy-start | bytes 2408452
  106.0 31.8 %collective-permute-start.27 = (bf16[784,512]{1,0:T(8,128)(2,1)}, bf16[784,512]{1,0:T(8,128)(2,1)}, u32[]{:S(2)}, u32[]{:S(2)}) collective-permute-start(bf16[784,512]{1,0:T(8,128)(2,1)} %collective-permute-done.20.refs_8_), channel_id=1, source_target_pairs={{2,3},{6,7},{10,11},{14,15},{18,19},{22,23},{26,27},{30,31}} | collective-permute-start | bytes 2408456 | tf_op jit(solution)/shard_map/hidden_right/ppermute | solution.py:23
  107.6 30.2 %collective-permute-start.28 = (bf16[784,512]{1,0:T(8,128)(2,1)}, bf16[784,512]{1,0:T(8,128)(2,1)}, u32[]{:S(2)}, u32[]{:S(2)}) collective-permute-start(bf16[784,512]{1,0:T(8,128)(2,1)} %collective-permute-done.21.refs_9_), channel_id=1, source_target_pairs={{1,0},{5,4},{9,8},{13,12},{17,16},{21,20},{25,24},{29,28}} | collective-permute-start | bytes 2408456 | tf_op jit(solution)/shard_map/hidden_left/ppermute | solution.py:23
  109.0 28.7 %collective-permute-start.24 = (bf16[192,2048]{1,0:T(8,128)(2,1)}, bf16[192,2048]{1,0:T(8,128)(2,1)}, u32[]{:S(2)}, u32[]{:S(2)}) collective-permute-start(bf16[192,2048]{1,0:T(8,128)(2,1)} %pad_maximum_fusion.refs_1_), channel_id=1, source_target_pairs={{0,4},{4,0},{8,12},{12,8},{1,5},{5,1},{9,13},{13,9},{2,6},{6,2},{1... | collective-permute-start | bytes 2359304 | tf_op jit(solution)/shard_map/out_grad_share_core/ppermute | solution.py:23
  109.1 28.6 %collective-permute-start.26 = (bf16[192,2048]{1,0:T(8,128)(2,1)}, bf16[192,2048]{1,0:T(8,128)(2,1)}, u32[]{:S(2)}, u32[]{:S(2)}) collective-permute-start(bf16[192,2048]{1,0:T(8,128)(2,1)} %collective-permute-done.25.refs_3_), channel_id=1, source_target_pairs={{0,4},{4,0},{8,12},{12,8},{1,5},{5,1},{9,13},{13,9},{2,6},{6,2},{1... | collective-permute-start | bytes 2359304 | tf_op jit(solution)/shard_map/out_grad_share_core/ppermute | solution.py:23
  127.3 12.7 %copy-start.19 = (bf16[768,512]{1,0:T(8,128)(2,1)S(1)}, bf16[768,512]{1,0:T(8,128)(2,1)}, u32[]{:S(2)}) copy-start(bf16[768,512]{1,0:T(8,128)(2,1)} %get-tuple-element.227.refs_9_.refs_0_) | copy-start | bytes 2359300
  137.8 15.9 %collective-permute-start.30 = (bf16[208,2048]{1,0:T(8,128)(2,1)}, bf16[208,2048]{1,0:T(8,128)(2,1)}, u32[]{:S(2)}, u32[]{:S(2)}) collective-permute-start(bf16[208,2048]{1,0:T(8,128)(2,1)} %get-tuple-element.224), channel_id=1, source_target_pairs={{0,4},{4,0},{8,12},{12,8},{1,5},{5,1},{9,13},{13,9},{2,6},{6,2},{1... | collective-permute-start | bytes 2555912 | tf_op jit(solution)/shard_map/token_grads_core/ppermute | solution.py:23
  138.0 19.0 %collective-permute-start.29 = (bf16[208,2048]{1,0:T(8,128)(2,1)}, bf16[208,2048]{1,0:T(8,128)(2,1)}, u32[]{:S(2)}, u32[]{:S(2)}) collective-permute-start(bf16[208,2048]{1,0:T(8,128)(2,1)} %get-tuple-element.222), channel_id=1, source_target_pairs={{0,4},{4,0},{8,12},{12,8},{1,5},{5,1},{9,13},{13,9},{2,6},{6,2},{1... | collective-permute-start | bytes 2555912 | tf_op jit(solution)/shard_map/token_grads_core/ppermute | solution.py:23
  138.4 20.1 %collective-permute-start.22 = (bf16[768,512]{1,0:T(8,128)(2,1)}, bf16[768,512]{1,0:T(8,128)(2,1)}, u32[]{:S(2)}, u32[]{:S(2)}) collective-permute-start(bf16[768,512]{1,0:T(8,128)(2,1)} %get-tuple-element.194.refs_12_), channel_id=1, source_target_pairs={{1,2},{2,1},{5,6},{6,5},{9,10},{10,9},{13,14},{14,13},{17,18},{18,... | collective-permute-start | bytes 2359304 | tf_op jit(solution)/shard_map/up_far_sums_across/ppermute | solution.py:23
  141.2 9.9 %copy-start.17 = (bf16[768,512]{1,0:T(8,128)(2,1)S(1)}, bf16[768,512]{1,0:T(8,128)(2,1)}, u32[]{:S(2)}) copy-start(bf16[768,512]{1,0:T(8,128)(2,1)} %get-tuple-element.225.refs_8_.refs_0_) | copy-start | bytes 2359300
  141.2 26.7 %collective-permute-start.31 = (bf16[512,768]{1,0:T(8,128)(2,1)}, bf16[512,768]{1,0:T(8,128)(2,1)}, u32[]{:S(2)}, u32[]{:S(2)}) collective-permute-start(bf16[512,768]{1,0:T(8,128)(2,1)} %turned_sum.5), channel_id=1, source_target_pairs={{1,0},{2,3},{5,4},{6,7},{9,8},{10,11},{13,12},{14,15},{17,16},{18,... | collective-permute-start | bytes 2359304 | tf_op jit(solution)/shard_map/gate_sums_outward/ppermute | solution.py:23
  151.1 1.1 copy-start.13
  152.2 1.1 copy-start.15
  153.3 1.2 copy-start.31
  153.7 3.3 %copy-start.30 = (bf16[208,2048]{1,0:T(8,128)(2,1)S(1)}, bf16[208,2048]{1,0:T(8,128)(2,1)}, u32[]{:S(2)}) copy-start(bf16[208,2048]{1,0:T(8,128)(2,1)} %get-tuple-element.221) | copy-start | bytes 2555908
  156.9 14.0 %copy-start.16 = (bf16[768,512]{1,0:T(8,128)(2,1)S(1)}, bf16[768,512]{1,0:T(8,128)(2,1)}, u32[]{:S(2)}) copy-start(bf16[768,512]{1,0:T(8,128)(2,1)} %get-tuple-element.243.refs_3_.refs_0_) | copy-start | bytes 2359300
  167.8 21.1 %collective-permute-start.32 = (bf16[208,2048]{1,0:T(8,128)(2,1)}, bf16[208,2048]{1,0:T(8,128)(2,1)}, u32[]{:S(2)}, u32[]{:S(2)}) collective-permute-start(bf16[208,2048]{1,0:T(8,128)(2,1)} %add_convert_fusion), channel_id=1, source_target_pairs={{8,0},{12,4},{0,8},{4,12},{9,1},{13,5},{1,9},{5,13},{10,2},{14,6},... | collective-permute-start | bytes 2555912 | tf_op jit(solution)/shard_map/token_grads_chip/ppermute | solution.py:23
  169.3 16.9 %collective-permute-start.33 = (bf16[768,512]{1,0:T(8,128)(2,1)}, bf16[768,512]{1,0:T(8,128)(2,1)}, u32[]{:S(2)}, u32[]{:S(2)}) collective-permute-start(bf16[768,512]{1,0:T(8,128)(2,1)} %get-tuple-element.198.refs_13_), channel_id=1, source_target_pairs={{1,2},{2,1},{5,6},{6,5},{9,10},{10,9},{13,14},{14,13},{17,18},{18,... | collective-permute-start | bytes 2359304 | tf_op jit(solution)/shard_map/up_sums_across/ppermute | solution.py:23
  172.3 20.4 %collective-permute-start.34 = (bf16[512,768]{1,0:T(8,128)(2,1)S(1)}, bf16[512,768]{1,0:T(8,128)(2,1)}, u32[]{:S(2)}, u32[]{:S(2)}) collective-permute-start(bf16[512,768]{1,0:T(8,128)(2,1)S(1)} %turned_sum.6.refs_3_), channel_id=1, source_target_pairs={{1,0},{2,3},{5,4},{6,7},{9,8},{10,11},{13,12},{14,15},{17,16},{18,... | collective-permute-start | bytes 2359304 | tf_op jit(solution)/shard_map/up_sums_outward/ppermute | solution.py:23
  176.4 9.9 %copy-start.14 = (bf16[768,512]{1,0:T(8,128)(2,1)S(1)}, bf16[768,512]{1,0:T(8,128)(2,1)}, u32[]{:S(2)}) copy-start(bf16[768,512]{1,0:T(8,128)(2,1)} %get-tuple-element.230.refs_2_.refs_0_) | copy-start | bytes 2359300
  186.3 1.1 copy-start.18
  192.7 1.1 copy-start.22
  (3 other events, 2.4 us)

commit v4 on v3

--- a/solution.py
+++ b/solution.py
@@ -435,43 +435,60 @@
     total = len(blocks) * blocks[0].shape[0]
     share = width // replicas
 
+    own = len(x_pairs) * 2
+    near = chips * rows
+
     def body(shares, *refs):
         blocks_in, refs = refs[: len(blocks)], refs[len(blocks) :]
         grads_in, refs = refs[:chips], refs[chips:]
         packed_in, refs = refs[: len(packed)], refs[len(packed) :]
-        outs, (x, g, sem) = refs[:-3], refs[-3:]
+        outs, (x, g, held, sem) = refs[:-4], refs[-4:]
         step = pl.program_id(0)
+        cols = pl.ds(pl.multiple_of(shares[step] * share, share), share)
+
+        def store(value):
+            value = value.astype(BF)
+            if joined:
+                outs[0][0] = value
+            else:
+                for i, out in enumerate(outs):
+
+                    @pl.when(step == i)
+                    def _():
+                        out[...] = value
 
         @pl.when(step == 0)
         def _():
-            moves = copies(blocks_in, x, sem, chips)
-            if not joined:
-                moves = copies(grads_in, g, sem, 0, 1) + moves
-            for m in moves:
+            first = copies(grads_in, g, sem, 0, 1) + copies(blocks_in[:own], x, sem, chips)
+            there = [
+                pltpu.make_async_copy(p, held, sem.at[chips + len(blocks)]) for p in packed_in
+            ]
+            rest = []
+            if fold is not None:
+                rest = copies(blocks_in[own:], x.at[pl.ds(near, total - near)], sem, chips + own)
+            for m in first + there + rest:
                 m.start()
-            if joined:
+            for m in first:
+                m.wait()
+            value = dot(g[:, :near], x[:near, cols], 1, 0)
+            for m in there:
+                m.wait()
+            if fold is not None:
                 for i in range(chips):
-                    g[:, i * rows : (i + 1) * rows] = grads_in[i][...]
-            for packed in packed_in:
-                for i in range(chips):
-                    part = slice(i * packed.shape[1] // chips, (i + 1) * packed.shape[1] // chips)
-                    at = (chips + i) * rows
+                    part = slice(i * held.shape[1] // chips, (i + 1) * held.shape[1] // chips)
+                    at = near + i * rows
                     g[:, at : at + rows] = spread(
-                        packed[:units, part], packed[units:, part], rows, i * rows
+                        held[:units, part], held[units:, part], rows, i * rows
                     )
-            for m in moves:
+            for m in rest:
                 m.wait()
-
-        cols = pl.ds(pl.multiple_of(shares[step] * share, share), share)
-        value = dot(g[...], x[:, cols], 1, 0).astype(BF)
-        if joined:
-            outs[0][0] = value
-        else:
-            for i, out in enumerate(outs):
-
-                @pl.when(step == i)
-                def _():
-                    out[...] = value
+            if fold is not None:
+                value = value + dot(g[:, near:], x[near:, cols], 1, 0)
+            store(value)
+
+        @pl.when(step > 0)
+        def _():
+            store(dot(g[...], x[:, cols], 1, 0))
 
     if joined:
         outputs = [((n, units, share), BF, (1, units, share), lambda i: (i, 0, 0))]
@@ -482,14 +499,13 @@
         "weight_grad",
         (n,),
         [(shares, pltpu.SMEM)]
-        + [(b, space) for b in blocks]
-        + [whole(a) if joined else (a, space) for a in grads]
-        + [whole(a) for a in packed],
+        + [(a, space) for a in (*blocks, *grads, *packed)],
         outputs,
         [
             pltpu.VMEM((total, width), BF),
             pltpu.VMEM((units, total), BF),
-            pltpu.SemaphoreType.DMA((len(blocks) + chips,)),
+            pltpu.VMEM(packed[0].shape if packed else (16, 128), BF),
+            pltpu.SemaphoreType.DMA((len(blocks) + chips + 1,)),
         ],
         deps,
         VMEM_LARGE,
@@ -552,8 +568,8 @@
     packed = pack([[f[0] for f in fwd]], tables, pairs, weights)[0]
     right = [line_step(packed, 0, replicas, 1, "hidden")]
     left = [line_step(packed, 0, replicas, -1, "hidden")]
-    og_far, og_core, og_shares, fwd, tables, weights, x, x_fold, info = meet(
-        (og_far, og_core, og_shares, fwd, tables, weights, x, x_fold, info)
+    og_far, og_core, og_shares, packed, fwd, tables, weights, x, x_fold, info = meet(
+        (og_far, og_core, og_shares, packed, fwd, tables, weights, x, x_fold, info)
     )
 
     def onward(t):
@@ -616,9 +632,7 @@
         gate_far = outward(turned_sum(gate_kept[1], gate_met, 0), replicas, "gate_sums")
         sums = return_sums(halves, experts, "token_grads")
         gate_own = turned_sum(gate_kept[0], gate_met, 1, up_kept)
-        up_met[0], up_kept, sums, gate_own, gate_far = meet(
-            (up_met[0], up_kept, sums, gate_own, gate_far)
-        )
+        up_met[0], up_kept, gate_own = meet((up_met[0], up_kept, gate_own))
 
         outer = ((z == 0) | (z == replicas - 1)).astype(jnp.int32).reshape(1)
         up_far = turned_sum(up_kept[1], up_met[0][None], 0)

time: 197 us -> 190 us (0.964)
  waiting for transfers between devices: 30.1 us -> 27.5 us
  Pallas kernels: 88.1 us -> 85.5 us
  other arithmetic: 8.53 us -> 6.31 us
    pallas_call x21, Pallas kernels: 88.1 us -> 85.5 us  [call(): pl.pallas_call(kernel, grid=grid, in_specs=[spec(e) for e in inputs] + [p...]
    ppermute x35, waiting for transfers between devices: 30.1 us -> 27.5 us  [send(): return lax.ppermute(x, axis, pairs)]
    unnamed x64 -> x68, local copies, waits for them, and re-layouts: 13.5 us -> 14.4 us
  transfers between devices with their start and end apart: 35 -> 35, of which waited for: 9 -> 8; matrix products, arithmetic and copies ran while one was open for 6% -> 5% of each run, Pallas kernels for 44% -> 45%
where the time goes in v4:
time: 190 us; the launch traced here: 188 us
  Pallas kernels  85.5 us (45%)
  starting transfers between devices  50.7 us (27%)
  waiting for transfers between devices  27.5 us (14%)
  local copies, waits for them, and re-layouts  17.2 us (9%)
  other arithmetic  6.31 us (3%)
    pallas_call x21, Pallas kernels, call(): pl.pallas_call(kernel, grid=grid, in_specs=[spec(e) for e in inputs] + [p...  85.5 us
    ppermute x35, starting transfers between devices, send(): return lax.ppermute(x, axis, pairs)  50.7 us
    ppermute x35, waiting for transfers between devices, send(): return lax.ppermute(x, axis, pairs)  27.5 us
    unnamed x68, local copies, waits for them, and re-layouts  14.4 us
  transfers between devices with their start and end apart: 35, of which 8 were waited for; matrix products, arithmetic and copies ran while one was open for 5% of the time, Pallas kernels for 45%

profile of v4, /device:TPU:0, one launch (start us, length us, event | category | flops | bytes accessed | tf_op | source)
XLA Modules:
  0.0 188.4 jit_solution(8771339077390788733)
XLA Ops:
  1.1 2.6 %collective-permute-start = (bf16[192,2048]{1,0:T(8,128)(2,1)}, bf16[192,2048]{1,0:T(8,128)(2,1)}, u32[]{:S(2)}, u32[]{:S(2)}) collective-permute-start(bf16[192,2048]{1,0:T(8,128)(2,1)} %refs_1_.3), channel_id=1, source_target_pairs={{8,0},{12,4},{0,8},{4,12},{9,1},{13,5},{1,9},{5,13},{10,2},{14,6},... | collective-permute-start | bytes 2359304 | tf_op jit(solution)/shard_map/tokens_chip/ppermute | solution.py:23
  3.7 4.4 %collective-permute-start.2 = (bf16[192,2048]{1,0:T(8,128)(2,1)}, bf16[192,2048]{1,0:T(8,128)(2,1)}, u32[]{:S(2)}, u32[]{:S(2)}) collective-permute-start(bf16[192,2048]{1,0:T(8,128)(2,1)} %refs_1_.3), channel_id=1, source_target_pairs={{0,1},{3,2},{4,5},{7,6},{8,9},{11,10},{12,13},{15,14},{16,17},{19,... | collective-permute-start | bytes 2359304 | tf_op jit(solution)/shard_map/tokens_inward/ppermute | solution.py:23
  8.1 0.7 convert_bitcast_fusion
  8.8 0.7 pad_maximum_fusion.2
  10.0 1.9 %copy-done.11 = bf16[1,2048,768]{2,1,0:T(8,128)(2,1)S(1)} copy-done((bf16[1,2048,768]{2,1,0:T(8,128)(2,1)S(1)}, bf16[1,2048,768]{2,1,0:T(8,128)(2,1)}, u32[]{:S(2)}) %copy-start.11) | copy-done | bytes 3145752
  11.9 1.9 %copy-done.12 = bf16[1,2048,768]{2,1,0:T(8,128)(2,1)S(1)} copy-done((bf16[1,2048,768]{2,1,0:T(8,128)(2,1)S(1)}, bf16[1,2048,768]{2,1,0:T(8,128)(2,1)}, u32[]{:S(2)}) %copy-start.12) | copy-done | bytes 3145752
  13.8 2.3 %turned.1 = (bf16[768,2048]{1,0:T(8,128)(2,1)S(1)}, bf16[768,2048]{1,0:T(8,128)(2,1)S(1)}) custom-call(bf16[2048,768]{1,0:T(8,128)(2,1)S(1)} %bitcast.33, bf16[2048,768]{1,0:T(8,128)(2,1)S(1)} %bitcast.34), custom_call_target="tpu_custom_call" | custom-call | flops 1000 | bytes 1000 | tf_op jit(solution)/shard_map/turned/pallas_call | solution.py:92
  16.2 4.0 %forward.2 = (bf16[768,384]{1,0:T(8,128)(2,1)S(1)}, bf16[768,384]{1,0:T(8,128)(2,1)S(1)}, bf16[768,384]{1,0:T(8,128)(2,1)S(1)}) custom-call(bf16[192,2048]{1,0:T(8,128)(2,1)S(1)} %copy-done.3, bf16[192,2048]{1,0:T(8,128)(2,1)S(1)} %collective-permute-done.3.refs_1_.refs_2_, bf16[768,2048]{1,0:T(8,128)(2,1)S(1)} %get-tuple-element.132.refs_2_.refs_4_, ...), custom_call_target="tpu_custom_call" | custom-call | flops 1000 | bytes 1000 | tf_op jit(solution)/shard_map/forward/pallas_call | solution.py:92
  20.2 0.8 copy-done.20
  21.0 0.8 copy-done.23
  21.8 0.8 copy-done.25
  22.6 2.0 %collective-permute-done.2.refs_5_ = bf16[192,2048]{1,0:T(8,128)(2,1)} collective-permute-done((bf16[192,2048]{1,0:T(8,128)(2,1)}, bf16[192,2048]{1,0:T(8,128)(2,1)}, u32[]{:S(2)}, u32[]{:S(2)}) %collective-permute-start.2) | collective-permute-done | bytes 786464 | tf_op jit(solution)/shard_map/tokens_inward/ppermute | solution.py:23
  25.7 2.1 %constant_dynamic-slice_fusion = (bf16[192,512]{1,0:T(8,128)(2,1)}, bf16[192,512]{1,0:T(8,128)(2,1)}, bf16[192,512]{1,0:T(8,128)(2,1)S(1)}, bf16[192,512]{1,0:T(8,128)(2,1)}) fusion(bf16[192,2048]{1,0:T(8,128)(2,1)} %refs_0_.2, s32[]{:T(128)S(6)} %select_n.55, s32[]{:T(128)S(6)} %select_n.51, s32[]{:T(128)S(6)} %select_n.49, s32[]{:T(128)S(6)} %select_n.53), kind=kLoop, calls=%fused_computation.12 | loop fusion | bytes 1572880 | tf_op jit(solution)/shard_map/dynamic_slice | solution.py:553
  27.7 2.5 %collective-permute-start.6 = (bf16[192,512]{1,0:T(8,128)(2,1)}, bf16[192,512]{1,0:T(8,128)(2,1)S(1)}, u32[]{:S(2)}, u32[]{:S(2)}) collective-permute-start(bf16[192,512]{1,0:T(8,128)(2,1)} %get-tuple-element.244), channel_id=1, source_target_pairs={{0,1},{1,2},{2,3},{3,0},{4,5},{5,6},{6,7},{7,4},{8,9},{9,10},{10,1... | collective-permute-start | bytes 589832 | tf_op jit(solution)/shard_map/out_grad_share_rotated/ppermute | solution.py:23
  30.3 1.1 collective-permute-done.11
  31.4 1.1 collective-permute-start.7
  32.5 2.9 %collective-permute-start.8 = (bf16[192,512]{1,0:T(8,128)(2,1)}, bf16[192,512]{1,0:T(8,128)(2,1)S(1)}, u32[]{:S(2)}, u32[]{:S(2)}) collective-permute-start(bf16[192,512]{1,0:T(8,128)(2,1)} %get-tuple-element.243), channel_id=1, source_target_pairs={{0,3},{1,0},{2,1},{3,2},{4,7},{5,4},{6,5},{7,6},{8,11},{9,8},{10,9... | collective-permute-start | bytes 589832 | tf_op jit(solution)/shard_map/out_grad_share_rotated/ppermute | solution.py:23
  35.4 1.2 slots.1
  36.6 1.9 copy-done.2
  38.5 5.4 %forward.3 = (bf16[768,384]{1,0:T(8,128)(2,1)S(1)}, bf16[768,384]{1,0:T(8,128)(2,1)S(1)}, bf16[768,384]{1,0:T(8,128)(2,1)S(1)}) custom-call(bf16[192,2048]{1,0:T(8,128)(2,1)} %collective-permute-done.refs_0_.refs_3_, bf16[192,2048]{1,0:T(8,128)(2,1)} %collective-permute-done.9.refs_1_.refs_4_, bf16[768,2048]{1,0:T(8,128)(2,1)S(1)} %get-tuple-element.132.refs_2_.refs_4_, ...), custom_call_target="tpu_custom_call" | custom-call | flops 1000 | bytes 1000 | tf_op jit(solution)/shard_map/forward/pallas_call | solution.py:92
  43.9 0.7 pack.2.refs_5_
  45.4 6.6 %collective-permute-start.15 = (bf16[784,512]{1,0:T(8,128)(2,1)S(1)}, bf16[784,512]{1,0:T(8,128)(2,1)S(1)}, u32[]{:S(2)}, u32[]{:S(2)}) collective-permute-start(bf16[784,512]{1,0:T(8,128)(2,1)S(1)} %pack.2.refs_5_), channel_id=1, source_target_pairs={{0,1},{1,2},{2,3},{4,5},{5,6},{6,7},{8,9},{9,10},{10,11},{12,13},{... | collective-permute-start | bytes 2408456 | tf_op jit(solution)/shard_map/hidden_right/ppermute | solution.py:23
  52.0 1.3 collective-permute-start.16
  53.3 1.6 collective-permute-start.17
  54.9 3.8 %backward.2 = (bf16[768,384]{1,0:T(8,128)(2,1)S(1)}, bf16[768,384]{1,0:T(8,128)(2,1)S(1)}, f32[1,384]{1,0:T(1,128)S(1)}) custom-call(bf16[192,2048]{1,0:T(8,128)(2,1)} %refs_0_.2, bf16[192,2048]{1,0:T(8,128)(2,1)} %collective-permute-done.5.refs_1_, bf16[768,2048]{1,0:T(8,128)(2,1)S(1)} %bitcast.31, f32[1,384]{1,0:T(1,128)S(1)} %get-tuple-element.250.refs_3_, ...), custom_call_target="tpu_custom_call" | custom-call | flops 1000 | bytes 1000 | tf_op jit(solution)/shard_map/backward/pallas_call | solution.py:92
  58.7 3.9 %backward.3 = (bf16[768,384]{1,0:T(8,128)(2,1)S(1)}, bf16[768,384]{1,0:T(8,128)(2,1)S(1)}, f32[1,384]{1,0:T(1,128)S(1)}) custom-call(bf16[192,2048]{1,0:T(8,128)(2,1)} %collective-permute-done.4.refs_0_, bf16[192,2048]{1,0:T(8,128)(2,1)S(1)} %collective-permute-done.12.refs_1_, bf16[768,2048]{1,0:T(8,128)(2,1)S(1)} %bitcast.32, ...), custom_call_target="tpu_custom_call" | custom-call | flops 1000 | bytes 1000 | tf_op jit(solution)/shard_map/backward/pallas_call | solution.py:92
  62.6 2.0 %pack.3 = (bf16[784,512]{1,0:T(8,128)(2,1)}, bf16[784,512]{1,0:T(8,128)(2,1)S(1)}) custom-call(bf16[768,384]{1,0:T(8,128)(2,1)S(1)} %get-tuple-element.199.refs_0_.refs_9_, bf16[768,384]{1,0:T(8,128)(2,1)S(1)} %get-tuple-element.200.refs_1_.refs_10_, bf16[768,384]{1,0:T(8,128)(2,1)S(1)} %get-tuple-element.219.refs_2_.refs_9_, ...), custom_call_target="tpu_custom_call" | custom-call | flops 1000 | bytes 1000 | tf_op jit(solution)/shard_map/pack/pallas_call | solution.py:92
  64.6 5.4 %collective-permute-start.13 = (bf16[784,512]{1,0:T(8,128)(2,1)}, bf16[784,512]{1,0:T(8,128)(2,1)}, u32[]{:S(2)}, u32[]{:S(2)}) collective-permute-start(bf16[784,512]{1,0:T(8,128)(2,1)} %get-tuple-element.162), channel_id=1, source_target_pairs={{0,1},{3,2},{4,5},{7,6},{8,9},{11,10},{12,13},{15,14},{16,17},{19,... | collective-permute-start | bytes 2408456 | tf_op jit(solution)/shard_map/gate_grad_inward/ppermute | solution.py:23
  70.1 1.0 pad_maximum_fusion.refs_1_
  71.0 2.3 %collective-permute-done.17.refs_7_ = bf16[192,2048]{1,0:T(8,128)(2,1)} collective-permute-done((bf16[192,2048]{1,0:T(8,128)(2,1)}, bf16[192,2048]{1,0:T(8,128)(2,1)}, u32[]{:S(2)}, u32[]{:S(2)}) %collective-permute-start.17) | collective-permute-done | bytes 786464 | tf_op jit(solution)/shard_map/tokens_fold_chip/ppermute | solution.py:23
  74.8 4.0 %collective-permute-start.20 = (bf16[784,512]{1,0:T(8,128)(2,1)}, bf16[784,512]{1,0:T(8,128)(2,1)S(1)}, u32[]{:S(2)}, u32[]{:S(2)}) collective-permute-start(bf16[784,512]{1,0:T(8,128)(2,1)} %copy-done.27), channel_id=1, source_target_pairs={{0,1},{3,2},{4,5},{7,6},{8,9},{11,10},{12,13},{15,14},{16,17},{19,... | collective-permute-start | bytes 2408456 | tf_op jit(solution)/shard_map/up_grad_inward/ppermute | solution.py:23
  78.8 1.6 collective-permute-start.21
  80.4 1.3 collective-permute-start.22
  82.2 1.5 collective-permute-start.24
  83.8 3.9 %collective-permute-done.13.refs_11_ = bf16[784,512]{1,0:T(8,128)(2,1)} collective-permute-done((bf16[784,512]{1,0:T(8,128)(2,1)}, bf16[784,512]{1,0:T(8,128)(2,1)}, u32[]{:S(2)}, u32[]{:S(2)}) %collective-permute-start.13) | collective-permute-done | bytes 802848 | tf_op jit(solution)/shard_map/gate_grad_inward/ppermute | solution.py:23
  87.7 7.9 %weight_grad.4 = bf16[2,768,512]{2,1,0:T(8,128)(2,1)} custom-call(s32[2]{0:T(128)} %get-tuple-element.252.refs_0_, bf16[192,2048]{1,0:T(8,128)(2,1)} %refs_1_.3, bf16[192,2048]{1,0:T(8,128)(2,1)} %copy-done.4, bf16[192,2048]{1,0:T(8,128)(2,1)} %collective-permute-done.refs_0_.refs_3_, bf16[192,2048]{1,0:T(8,128)(2,1)} %collective-permute-done.9.refs_1_.refs_4_, ...), custom_call_target="tpu_custom_call" | custom-call | flops 1000 | bytes 1000 | tf_op jit(solution)/shard_map/weight_grad/pallas_call | solution.py:92
  95.6 0.8 collective-permute-start.19
  96.3 8.1 %collective-permute-done.20.refs_11_ = bf16[784,512]{1,0:T(8,128)(2,1)S(1)} collective-permute-done((bf16[784,512]{1,0:T(8,128)(2,1)}, bf16[784,512]{1,0:T(8,128)(2,1)S(1)}, u32[]{:S(2)}, u32[]{:S(2)}) %collective-permute-start.20) | collective-permute-done | bytes 802848 | tf_op jit(solution)/shard_map/up_grad_inward/ppermute | solution.py:23
  104.5 1.6 collective-permute-start.26
  106.1 1.5 collective-permute-start.27
  108.8 8.1 %weight_grad.5 = (bf16[768,512]{1,0:T(8,128)(2,1)}, bf16[768,512]{1,0:T(8,128)(2,1)}) custom-call(s32[2]{0:T(128)} %get-tuple-element.252.refs_0_, bf16[192,2048]{1,0:T(8,128)(2,1)} %refs_1_.3, bf16[192,2048]{1,0:T(8,128)(2,1)} %copy-done.4, bf16[192,2048]{1,0:T(8,128)(2,1)} %collective-permute-done.refs_0_.refs_3_, ...), custom_call_target="tpu_custom_call" | custom-call | flops 1000 | bytes 1000 | tf_op jit(solution)/shard_map/weight_grad/pallas_call | solution.py:92
  116.9 8.2 %weight_grad.6 = (bf16[768,512]{1,0:T(8,128)(2,1)}, bf16[768,512]{1,0:T(8,128)(2,1)}) custom-call(s32[2]{0:T(128)} %get-tuple-element.251.refs_0_, bf16[192,2048]{1,0:T(8,128)(2,1)} %refs_1_.3, bf16[192,2048]{1,0:T(8,128)(2,1)} %copy-done.4, bf16[192,2048]{1,0:T(8,128)(2,1)} %collective-permute-done.refs_0_.refs_3_, ...), custom_call_target="tpu_custom_call" | custom-call | flops 1000 | bytes 1000 | tf_op jit(solution)/shard_map/weight_grad/pallas_call | solution.py:92
  125.1 10.5 %input_grad.1 = (bf16[208,2048]{1,0:T(8,128)(2,1)}, bf16[208,2048]{1,0:T(8,128)(2,1)}, bf16[208,2048]{1,0:T(8,128)(2,1)}, bf16[208,2048]{1,0:T(8,128)(2,1)}) custom-call(bf16[768,384]{1,0:T(8,128)(2,1)} %copy-done.8, bf16[768,384]{1,0:T(8,128)(2,1)} %copy-done.9, bf16[768,384]{1,0:T(8,128)(2,1)} %copy-done.6, bf16[768,384]{1,0:T(8,128)(2,1)} %copy-done.7, ...), custom_call_target="tpu_custom_call" | custom-call | flops 1000 | bytes 1000 | tf_op jit(solution)/shard_map/input_grad/pallas_call | solution.py:92
  135.8 1.7 collective-permute-start.31
  137.5 1.5 collective-permute-start.32
  139.0 1.2 turned_sum.5
  140.2 1.3 collective-permute-start.33
  141.9 1.2 add_convert_fusion
  143.1 1.2 collective-permute-start.30
  144.3 8.1 %weight_grad.7 = (bf16[768,512]{1,0:T(8,128)(2,1)}, bf16[768,512]{1,0:T(8,128)(2,1)}) custom-call(s32[2]{0:T(128)} %get-tuple-element.251.refs_0_, bf16[192,2048]{1,0:T(8,128)(2,1)} %refs_1_.3, bf16[192,2048]{1,0:T(8,128)(2,1)} %copy-done.4, bf16[192,2048]{1,0:T(8,128)(2,1)} %collective-permute-done.refs_0_.refs_3_, ...), custom_call_target="tpu_custom_call" | custom-call | flops 1000 | bytes 1000 | tf_op jit(solution)/shard_map/weight_grad/pallas_call | solution.py:92
  152.5 1.1 copy-done.13
  153.6 1.1 copy-done.15
  155.1 0.8 copy-done.16
  155.9 1.4 turned_sum.6.refs_3_
  157.3 1.3 collective-permute-start.34
  159.3 8.9 %collective-permute-done.33.refs_1_ = bf16[512,768]{1,0:T(8,128)(2,1)} collective-permute-done((bf16[512,768]{1,0:T(8,128)(2,1)}, bf16[512,768]{1,0:T(8,128)(2,1)}, u32[]{:S(2)}, u32[]{:S(2)}) %collective-permute-start.33) | collective-permute-done | bytes 786464 | tf_op jit(solution)/shard_map/gate_sums_outward/ppermute | solution.py:23
  168.2 2.1 %choose.2.refs_12_ = bf16[1,512,768]{2,1,0:T(8,128)(2,1)} custom-call(s32[1]{0:T(128)} %bitcast.20.refs_0_, bf16[512,768]{1,0:T(8,128)(2,1)} %collective-permute-done.33.refs_1_, bf16[512,768]{1,0:T(8,128)(2,1)S(1)} %turned_sum.4.refs_2_, bf16[512,768]{1,0:T(8,128)(2,1)S(1)} %turned_sum.6.refs_3_), custom_call_target="tpu_custom_call" | custom-call | flops 1000 | bytes 1000 | tf_op jit(solution)/shard_map/choose/pallas_call | solution.py:92
  170.3 9.7 %sum_products.1.refs_2_ = bf16[768,512]{1,0:T(8,128)(2,1)} custom-call(s32[7]{0:T(128)} %convert_element_type.40.refs_0_, bf16[192,2048]{1,0:T(8,128)(2,1)} %pad_maximum_fusion.refs_1_, bf16[192,2048]{1,0:T(8,128)(2,1)} %collective-permute-done.23.refs_2_, bf16[192,2048]{1,0:T(8,128)(2,1)} %collective-permute-done.24.refs_3_, ...), custom_call_target="tpu_custom_call" | custom-call | flops 1000 | bytes 1000 | tf_op jit(solution)/shard_map/sum_products/pallas_call | solution.py:92
  180.0 1.1 copy-done.18
  181.1 1.4 turned_sum.7.refs_2_
  182.6 1.4 add_convert_fusion.1.refs_0_
  184.1 2.2 %finish_tokens.1 = (bf16[192,2048]{1,0:T(8,128)(2,1)}, f32[2,192]{1,0:T(2,128)}) custom-call(bf16[208,2048]{1,0:T(8,128)(2,1)S(1)} %add_convert_fusion.1.refs_0_, bf16[208,2048]{1,0:T(8,128)(2,1)} %collective-permute-done.30.refs_1_, bf16[512,768]{1,0:T(8,128)(2,1)S(1)} %turned_sum.7.refs_2_), custom_call_target="tpu_custom_call" | custom-call | flops 1000 | bytes 1000 | tf_op jit(solution)/shard_map/finish_tokens/pallas_call | solution.py:92
  186.3 1.1 copy-done.22
  187.4 1.0 choose.3
  (112 shorter events, 7.7 us)
Async XLA Ops:
  0.6 15.5 %collective-permute-start.3 = (bf16[192,2048]{1,0:T(8,128)(2,1)}, bf16[192,2048]{1,0:T(8,128)(2,1)S(1)}, u32[]{:S(2)}, u32[]{:S(2)}) collective-permute-start(bf16[192,2048]{1,0:T(8,128)(2,1)} %refs_1_.3), channel_id=1, source_target_pairs={{0,4},{4,0},{8,12},{12,8},{1,5},{5,1},{9,13},{13,9},{2,6},{6,2},{1... | collective-permute-start | bytes 2359304 | tf_op jit(solution)/shard_map/tokens_core/ppermute | solution.py:23
  1.1 21.5 %collective-permute-start = (bf16[192,2048]{1,0:T(8,128)(2,1)}, bf16[192,2048]{1,0:T(8,128)(2,1)}, u32[]{:S(2)}, u32[]{:S(2)}) collective-permute-start(bf16[192,2048]{1,0:T(8,128)(2,1)} %refs_1_.3), channel_id=1, source_target_pairs={{8,0},{12,4},{0,8},{4,12},{9,1},{13,5},{1,9},{5,13},{10,2},{14,6},... | collective-permute-start | bytes 2359304 | tf_op jit(solution)/shard_map/tokens_chip/ppermute | solution.py:23
  3.7 20.9 %collective-permute-start.2 = (bf16[192,2048]{1,0:T(8,128)(2,1)}, bf16[192,2048]{1,0:T(8,128)(2,1)}, u32[]{:S(2)}, u32[]{:S(2)}) collective-permute-start(bf16[192,2048]{1,0:T(8,128)(2,1)} %refs_1_.3), channel_id=1, source_target_pairs={{0,1},{3,2},{4,5},{7,6},{8,9},{11,10},{12,13},{15,14},{16,17},{19,... | collective-permute-start | bytes 2359304 | tf_op jit(solution)/shard_map/tokens_inward/ppermute | solution.py:23
  9.5 13.1 %collective-permute-start.1 = (f32[4,192]{1,0:T(4,128)S(1)}, f32[4,192]{1,0:T(4,128)S(1)}, u32[]{:S(2)}, u32[]{:S(2)}) collective-permute-start(f32[4,192]{1,0:T(4,128)S(1)} %pad_maximum_fusion.2), channel_id=1, source_target_pairs={{8,0},{12,4},{0,8},{4,12},{9,1},{13,5},{1,9},{5,13},{10,2},{14,6},... | collective-permute-start | bytes 9224 | tf_op jit(solution)/shard_map/routing_chip/ppermute | solution.py:23
  10.0 1.9 %copy-start.11 = (bf16[1,2048,768]{2,1,0:T(8,128)(2,1)S(1)}, bf16[1,2048,768]{2,1,0:T(8,128)(2,1)}, u32[]{:S(2)}) copy-start(bf16[1,2048,768]{2,1,0:T(8,128)(2,1)} %param.11) | copy-start | bytes 9437188
  11.9 1.9 %copy-start.12 = (bf16[1,2048,768]{2,1,0:T(8,128)(2,1)S(1)}, bf16[1,2048,768]{2,1,0:T(8,128)(2,1)}, u32[]{:S(2)}) copy-start(bf16[1,2048,768]{2,1,0:T(8,128)(2,1)} %param.12) | copy-start | bytes 9437188
  13.8 2.4 %copy-start.3 = (bf16[192,2048]{1,0:T(8,128)(2,1)S(1)}, bf16[192,2048]{1,0:T(8,128)(2,1)}, u32[]{:S(2)}) copy-start(bf16[192,2048]{1,0:T(8,128)(2,1)} %refs_1_.3) | copy-start | bytes 2359300
  16.1 4.1 %copy-start.1 = (bf16[768,2048]{1,0:T(8,128)(2,1)}, bf16[768,2048]{1,0:T(8,128)(2,1)S(1)}, u32[]{:S(2)}) copy-start(bf16[768,2048]{1,0:T(8,128)(2,1)S(1)} %get-tuple-element.133.refs_3_.refs_5_) | copy-start | bytes 9437188
  16.1 20.5 %copy-start = (bf16[768,2048]{1,0:T(8,128)(2,1)}, bf16[768,2048]{1,0:T(8,128)(2,1)S(1)}, u32[]{:S(2)}) copy-start(bf16[768,2048]{1,0:T(8,128)(2,1)S(1)} %get-tuple-element.132.refs_2_.refs_4_) | copy-start | bytes 9437188
  16.1 4.0 %copy-start.4 = (bf16[192,2048]{1,0:T(8,128)(2,1)}, bf16[192,2048]{1,0:T(8,128)(2,1)S(1)}, u32[]{:S(2)}) copy-start(bf16[192,2048]{1,0:T(8,128)(2,1)S(1)} %collective-permute-done.3.refs_1_.refs_2_) | copy-start | bytes 2359300
  24.7 7.8 %collective-permute-start.9 = (bf16[192,2048]{1,0:T(8,128)(2,1)}, bf16[192,2048]{1,0:T(8,128)(2,1)}, u32[]{:S(2)}, u32[]{:S(2)}) collective-permute-start(bf16[192,2048]{1,0:T(8,128)(2,1)} %collective-permute-done.refs_0_.refs_3_), channel_id=1, source_target_pairs={{0,4},{4,0},{8,12},{12,8},{1,5},{5,1},{9,13},{13,9},{2,6},{6,2},{1... | collective-permute-start | bytes 2359304 | tf_op jit(solution)/shard_map/tokens_core/ppermute | solution.py:23
  24.7 20.6 %collective-permute-start.4 = (bf16[192,2048]{1,0:T(8,128)(2,1)}, bf16[192,2048]{1,0:T(8,128)(2,1)}, u32[]{:S(2)}, u32[]{:S(2)}) collective-permute-start(bf16[192,2048]{1,0:T(8,128)(2,1)} %refs_0_.2), channel_id=1, source_target_pairs={{8,0},{12,4},{0,8},{4,12},{9,1},{13,5},{1,9},{5,13},{10,2},{14,6},... | collective-permute-start | bytes 2359304 | tf_op jit(solution)/shard_map/out_grad_chip/ppermute | solution.py:23
  25.2 20.1 %collective-permute-start.5 = (bf16[192,2048]{1,0:T(8,128)(2,1)}, bf16[192,2048]{1,0:T(8,128)(2,1)}, u32[]{:S(2)}, u32[]{:S(2)}) collective-permute-start(bf16[192,2048]{1,0:T(8,128)(2,1)} %refs_0_.2), channel_id=1, source_target_pairs={{0,4},{4,0},{8,12},{12,8},{1,5},{5,1},{9,13},{13,9},{2,6},{6,2},{1... | collective-permute-start | bytes 2359304 | tf_op jit(solution)/shard_map/out_grad_core/ppermute | solution.py:23
  25.4 4.8 %collective-permute-start.10 = (f32[4,192]{1,0:T(4,128)S(1)}, f32[4,192]{1,0:T(4,128)S(1)}, u32[]{:S(2)}, u32[]{:S(2)}) collective-permute-start(f32[4,192]{1,0:T(4,128)S(1)} %pad_maximum_fusion.2), channel_id=1, source_target_pairs={{0,4},{4,0},{8,12},{12,8},{1,5},{5,1},{9,13},{13,9},{2,6},{6,2},{1... | collective-permute-start | bytes 9224 | tf_op jit(solution)/shard_map/routing_core/ppermute | solution.py:23
  27.7 17.0 %collective-permute-start.6 = (bf16[192,512]{1,0:T(8,128)(2,1)}, bf16[192,512]{1,0:T(8,128)(2,1)S(1)}, u32[]{:S(2)}, u32[]{:S(2)}) collective-permute-start(bf16[192,512]{1,0:T(8,128)(2,1)} %get-tuple-element.244), channel_id=1, source_target_pairs={{0,1},{1,2},{2,3},{3,0},{4,5},{5,6},{6,7},{7,4},{8,9},{9,10},{10,1... | collective-permute-start | bytes 589832 | tf_op jit(solution)/shard_map/out_grad_share_rotated/ppermute | solution.py:23
  30.2 1.2 collective-permute-start.11
  31.4 13.9 %collective-permute-start.7 = (bf16[192,512]{1,0:T(8,128)(2,1)}, bf16[192,512]{1,0:T(8,128)(2,1)S(1)}, u32[]{:S(2)}, u32[]{:S(2)}) collective-permute-start(bf16[192,512]{1,0:T(8,128)(2,1)} %get-tuple-element.246), channel_id=1, source_target_pairs={{0,2},{1,3},{2,0},{3,1},{4,6},{5,7},{6,4},{7,5},{8,10},{9,11},{10,... | collective-permute-start | bytes 589832 | tf_op jit(solution)/shard_map/out_grad_share_rotated/ppermute | solution.py:23
  32.5 12.8 %collective-permute-start.8 = (bf16[192,512]{1,0:T(8,128)(2,1)}, bf16[192,512]{1,0:T(8,128)(2,1)S(1)}, u32[]{:S(2)}, u32[]{:S(2)}) collective-permute-start(bf16[192,512]{1,0:T(8,128)(2,1)} %get-tuple-element.243), channel_id=1, source_target_pairs={{0,3},{1,0},{2,1},{3,2},{4,7},{5,4},{6,5},{7,6},{8,11},{9,8},{10,9... | collective-permute-start | bytes 589832 | tf_op jit(solution)/shard_map/out_grad_share_rotated/ppermute | solution.py:23
  36.6 1.9 %copy-start.2 = (bf16[768,2048]{1,0:T(8,128)(2,1)S(1)}, bf16[768,2048]{1,0:T(8,128)(2,1)}, u32[]{:S(2)}) copy-start(bf16[768,2048]{1,0:T(8,128)(2,1)} %copy-done.1) | copy-start | bytes 9437188
  38.5 5.4 %copy-start.21 = (bf16[768,384]{1,0:T(8,128)(2,1)S(1)}, bf16[768,384]{1,0:T(8,128)(2,1)}, u32[]{:S(2)}) copy-start(bf16[768,384]{1,0:T(8,128)(2,1)} %copy-done.20) | copy-start | bytes 1769476
  38.5 16.4 %copy-start.5 = (bf16[1,768,2048]{2,1,0:T(8,128)(2,1)S(1)}, bf16[1,768,2048]{2,1,0:T(8,128)(2,1)}, u32[]{:S(2)}) copy-start(bf16[1,768,2048]{2,1,0:T(8,128)(2,1)} %param.13) | copy-start | bytes 9437188
  43.9 11.0 %copy-start.24 = (bf16[768,384]{1,0:T(8,128)(2,1)S(1)}, bf16[768,384]{1,0:T(8,128)(2,1)}, u32[]{:S(2)}) copy-start(bf16[768,384]{1,0:T(8,128)(2,1)} %copy-done.23) | copy-start | bytes 1769476
  43.9 11.0 %copy-start.26 = (bf16[768,384]{1,0:T(8,128)(2,1)S(1)}, bf16[768,384]{1,0:T(8,128)(2,1)}, u32[]{:S(2)}) copy-start(bf16[768,384]{1,0:T(8,128)(2,1)} %copy-done.25) | copy-start | bytes 1769476
  44.7 14.0 %copy-start.10 = (bf16[784,512]{1,0:T(8,128)(2,1)}, bf16[784,512]{1,0:T(8,128)(2,1)S(1)}, u32[]{:S(2)}) copy-start(bf16[784,512]{1,0:T(8,128)(2,1)S(1)} %pack.2.refs_5_) | copy-start | bytes 2408452
  45.3 13.4 %collective-permute-start.12 = (bf16[192,2048]{1,0:T(8,128)(2,1)}, bf16[192,2048]{1,0:T(8,128)(2,1)S(1)}, u32[]{:S(2)}, u32[]{:S(2)}) collective-permute-start(bf16[192,2048]{1,0:T(8,128)(2,1)} %collective-permute-done.4.refs_0_), channel_id=1, source_target_pairs={{0,4},{4,0},{8,12},{12,8},{1,5},{5,1},{9,13},{13,9},{2,6},{6,2},{1... | collective-permute-start | bytes 2359304 | tf_op jit(solution)/shard_map/out_grad_core/ppermute | solution.py:23
  45.4 27.9 %collective-permute-start.15 = (bf16[784,512]{1,0:T(8,128)(2,1)S(1)}, bf16[784,512]{1,0:T(8,128)(2,1)S(1)}, u32[]{:S(2)}, u32[]{:S(2)}) collective-permute-start(bf16[784,512]{1,0:T(8,128)(2,1)S(1)} %pack.2.refs_5_), channel_id=1, source_target_pairs={{0,1},{1,2},{2,3},{4,5},{5,6},{6,7},{8,9},{9,10},{10,11},{12,13},{... | collective-permute-start | bytes 2408456 | tf_op jit(solution)/shard_map/hidden_right/ppermute | solution.py:23
  52.0 21.9 %collective-permute-start.16 = (bf16[784,512]{1,0:T(8,128)(2,1)S(1)}, bf16[784,512]{1,0:T(8,128)(2,1)S(1)}, u32[]{:S(2)}, u32[]{:S(2)}) collective-permute-start(bf16[784,512]{1,0:T(8,128)(2,1)S(1)} %pack.2.refs_5_), channel_id=1, source_target_pairs={{1,0},{2,1},{3,2},{5,4},{6,5},{7,6},{9,8},{10,9},{11,10},{13,12},{... | collective-permute-start | bytes 2408456 | tf_op jit(solution)/shard_map/hidden_left/ppermute | solution.py:23
  53.3 20.0 %collective-permute-start.17 = (bf16[192,2048]{1,0:T(8,128)(2,1)}, bf16[192,2048]{1,0:T(8,128)(2,1)}, u32[]{:S(2)}, u32[]{:S(2)}) collective-permute-start(bf16[192,2048]{1,0:T(8,128)(2,1)} %collective-permute-done.2.refs_5_), channel_id=1, source_target_pairs={{8,0},{12,4},{0,8},{4,12},{9,1},{13,5},{1,9},{5,13},{10,2},{14,6},... | collective-permute-start | bytes 2359304 | tf_op jit(solution)/shard_map/tokens_fold_chip/ppermute | solution.py:23
  54.9 25.5 %collective-permute-start.14 = (bf16[192,2048]{1,0:T(8,128)(2,1)}, bf16[192,2048]{1,0:T(8,128)(2,1)}, u32[]{:S(2)}, u32[]{:S(2)}) collective-permute-start(bf16[192,2048]{1,0:T(8,128)(2,1)} %collective-permute-done.2.refs_5_), channel_id=1, source_target_pairs={{0,4},{4,0},{8,12},{12,8},{1,5},{5,1},{9,13},{13,9},{2,6},{6,2},{1... | collective-permute-start | bytes 2359304 | tf_op jit(solution)/shard_map/tokens_fold_core/ppermute | solution.py:23
  58.7 4.0 %copy-start.6 = (bf16[768,384]{1,0:T(8,128)(2,1)}, bf16[768,384]{1,0:T(8,128)(2,1)S(1)}, u32[]{:S(2)}) copy-start(bf16[768,384]{1,0:T(8,128)(2,1)S(1)} %get-tuple-element.219.refs_2_.refs_9_) | copy-start | bytes 1769476
  58.7 4.0 %copy-start.8 = (bf16[768,384]{1,0:T(8,128)(2,1)}, bf16[768,384]{1,0:T(8,128)(2,1)S(1)}, u32[]{:S(2)}) copy-start(bf16[768,384]{1,0:T(8,128)(2,1)S(1)} %get-tuple-element.199.refs_0_.refs_9_) | copy-start | bytes 1769476
  62.6 8.4 %copy-start.7 = (bf16[768,384]{1,0:T(8,128)(2,1)}, bf16[768,384]{1,0:T(8,128)(2,1)S(1)}, u32[]{:S(2)}) copy-start(bf16[768,384]{1,0:T(8,128)(2,1)S(1)} %get-tuple-element.220.refs_3_.refs_10_) | copy-start | bytes 1769476
  62.6 8.4 %copy-start.9 = (bf16[768,384]{1,0:T(8,128)(2,1)}, bf16[768,384]{1,0:T(8,128)(2,1)S(1)}, u32[]{:S(2)}) copy-start(bf16[768,384]{1,0:T(8,128)(2,1)S(1)} %get-tuple-element.200.refs_1_.refs_10_) | copy-start | bytes 1769476
  64.6 9.2 %copy-start.27 = (bf16[784,512]{1,0:T(8,128)(2,1)}, bf16[784,512]{1,0:T(8,128)(2,1)S(1)}, u32[]{:S(2)}) copy-start(bf16[784,512]{1,0:T(8,128)(2,1)S(1)} %get-tuple-element.180) | copy-start | bytes 2408452
  64.6 23.0 %collective-permute-start.13 = (bf16[784,512]{1,0:T(8,128)(2,1)}, bf16[784,512]{1,0:T(8,128)(2,1)}, u32[]{:S(2)}, u32[]{:S(2)}) collective-permute-start(bf16[784,512]{1,0:T(8,128)(2,1)} %get-tuple-element.162), channel_id=1, source_target_pairs={{0,1},{3,2},{4,5},{7,6},{8,9},{11,10},{12,13},{15,14},{16,17},{19,... | collective-permute-start | bytes 2408456 | tf_op jit(solution)/shard_map/gate_grad_inward/ppermute | solution.py:23
  74.8 7.5 %collective-permute-start.18 = (bf16[192,2048]{1,0:T(8,128)(2,1)}, bf16[192,2048]{1,0:T(8,128)(2,1)S(1)}, u32[]{:S(2)}, u32[]{:S(2)}) collective-permute-start(bf16[192,2048]{1,0:T(8,128)(2,1)} %collective-permute-done.17.refs_7_), channel_id=1, source_target_pairs={{0,4},{4,0},{8,12},{12,8},{1,5},{5,1},{9,13},{13,9},{2,6},{6,2},{1... | collective-permute-start | bytes 2359304 | tf_op jit(solution)/shard_map/tokens_fold_core/ppermute | solution.py:23
  74.8 29.7 %collective-permute-start.20 = (bf16[784,512]{1,0:T(8,128)(2,1)}, bf16[784,512]{1,0:T(8,128)(2,1)S(1)}, u32[]{:S(2)}, u32[]{:S(2)}) collective-permute-start(bf16[784,512]{1,0:T(8,128)(2,1)} %copy-done.27), channel_id=1, source_target_pairs={{0,1},{3,2},{4,5},{7,6},{8,9},{11,10},{12,13},{15,14},{16,17},{19,... | collective-permute-start | bytes 2408456 | tf_op jit(solution)/shard_map/up_grad_inward/ppermute | solution.py:23
  78.8 25.7 %collective-permute-start.21 = (bf16[784,512]{1,0:T(8,128)(2,1)}, bf16[784,512]{1,0:T(8,128)(2,1)}, u32[]{:S(2)}, u32[]{:S(2)}) collective-permute-start(bf16[784,512]{1,0:T(8,128)(2,1)} %copy-done.32), channel_id=1, source_target_pairs={{1,2},{2,3},{5,6},{6,7},{9,10},{10,11},{13,14},{14,15},{17,18},{18... | collective-permute-start | bytes 2408456 | tf_op jit(solution)/shard_map/hidden_right/ppermute | solution.py:23
  80.4 24.1 %collective-permute-start.22 = (bf16[784,512]{1,0:T(8,128)(2,1)}, bf16[784,512]{1,0:T(8,128)(2,1)}, u32[]{:S(2)}, u32[]{:S(2)}) collective-permute-start(bf16[784,512]{1,0:T(8,128)(2,1)} %copy-done.33), channel_id=1, source_target_pairs={{1,0},{2,1},{5,4},{6,5},{9,8},{10,9},{13,12},{14,13},{17,16},{18,1... | collective-permute-start | bytes 2408456 | tf_op jit(solution)/shard_map/hidden_left/ppermute | solution.py:23
  82.2 5.4 %copy-start.28 = (bf16[192,2048]{1,0:T(8,128)(2,1)}, bf16[192,2048]{1,0:T(8,128)(2,1)S(1)}, u32[]{:S(2)}) copy-start(bf16[192,2048]{1,0:T(8,128)(2,1)S(1)} %collective-permute-done.18.refs_8_) | copy-start | bytes 2359300
  82.2 25.4 %collective-permute-start.24 = (bf16[192,2048]{1,0:T(8,128)(2,1)}, bf16[192,2048]{1,0:T(8,128)(2,1)}, u32[]{:S(2)}, u32[]{:S(2)}) collective-permute-start(bf16[192,2048]{1,0:T(8,128)(2,1)} %pad_maximum_fusion.refs_1_), channel_id=1, source_target_pairs={{8,0},{12,4},{0,8},{4,12},{9,1},{13,5},{1,9},{5,13},{10,2},{14,6},... | collective-permute-start | bytes 2359304 | tf_op jit(solution)/shard_map/out_grad_share_chip/ppermute | solution.py:23
  95.6 40.1 %collective-permute-start.19 = (bf16[2,768,512]{2,1,0:T(8,128)(2,1)}, bf16[2,768,512]{2,1,0:T(8,128)(2,1)S(1)}, u32[]{:S(2)}, u32[]{:S(2)}) collective-permute-start(bf16[2,768,512]{2,1,0:T(8,128)(2,1)} %weight_grad.4), channel_id=1, source_target_pairs={{1,2},{2,1},{5,6},{6,5},{9,10},{10,9},{13,14},{14,13},{17,18},{18,... | collective-permute-start | bytes 4718600 | tf_op jit(solution)/shard_map/gate_sums_across/ppermute | solution.py:23
  104.5 4.3 %copy-start.29 = (bf16[784,512]{1,0:T(8,128)(2,1)}, bf16[784,512]{1,0:T(8,128)(2,1)S(1)}, u32[]{:S(2)}) copy-start(bf16[784,512]{1,0:T(8,128)(2,1)S(1)} %collective-permute-done.20.refs_11_) | copy-start | bytes 2408452
  104.5 31.1 %collective-permute-start.26 = (bf16[784,512]{1,0:T(8,128)(2,1)}, bf16[784,512]{1,0:T(8,128)(2,1)}, u32[]{:S(2)}, u32[]{:S(2)}) collective-permute-start(bf16[784,512]{1,0:T(8,128)(2,1)} %collective-permute-done.21.refs_8_), channel_id=1, source_target_pairs={{2,3},{6,7},{10,11},{14,15},{18,19},{22,23},{26,27},{30,31}} | collective-permute-start | bytes 2408456 | tf_op jit(solution)/shard_map/hidden_right/ppermute | solution.py:23
  106.1 29.6 %collective-permute-start.27 = (bf16[784,512]{1,0:T(8,128)(2,1)}, bf16[784,512]{1,0:T(8,128)(2,1)}, u32[]{:S(2)}, u32[]{:S(2)}) collective-permute-start(bf16[784,512]{1,0:T(8,128)(2,1)} %collective-permute-done.22.refs_9_), channel_id=1, source_target_pairs={{1,0},{5,4},{9,8},{13,12},{17,16},{21,20},{25,24},{29,28}} | collective-permute-start | bytes 2408456 | tf_op jit(solution)/shard_map/hidden_left/ppermute | solution.py:23
  107.5 28.1 %collective-permute-start.23 = (bf16[192,2048]{1,0:T(8,128)(2,1)}, bf16[192,2048]{1,0:T(8,128)(2,1)}, u32[]{:S(2)}, u32[]{:S(2)}) collective-permute-start(bf16[192,2048]{1,0:T(8,128)(2,1)} %pad_maximum_fusion.refs_1_), channel_id=1, source_target_pairs={{0,4},{4,0},{8,12},{12,8},{1,5},{5,1},{9,13},{13,9},{2,6},{6,2},{1... | collective-permute-start | bytes 2359304 | tf_op jit(solution)/shard_map/out_grad_share_core/ppermute | solution.py:23
  107.6 28.0 %collective-permute-start.25 = (bf16[192,2048]{1,0:T(8,128)(2,1)}, bf16[192,2048]{1,0:T(8,128)(2,1)}, u32[]{:S(2)}, u32[]{:S(2)}) collective-permute-start(bf16[192,2048]{1,0:T(8,128)(2,1)} %collective-permute-done.24.refs_3_), channel_id=1, source_target_pairs={{0,4},{4,0},{8,12},{12,8},{1,5},{5,1},{9,13},{13,9},{2,6},{6,2},{1... | collective-permute-start | bytes 2359304 | tf_op jit(solution)/shard_map/out_grad_share_core/ppermute | solution.py:23
  125.1 13.9 %copy-start.19 = (bf16[768,512]{1,0:T(8,128)(2,1)S(1)}, bf16[768,512]{1,0:T(8,128)(2,1)}, u32[]{:S(2)}) copy-start(bf16[768,512]{1,0:T(8,128)(2,1)} %get-tuple-element.237.refs_9_.refs_0_) | copy-start | bytes 2359300
  135.6 6.3 %copy-start.31 = (bf16[208,2048]{1,0:T(8,128)(2,1)S(1)}, bf16[208,2048]{1,0:T(8,128)(2,1)}, u32[]{:S(2)}) copy-start(bf16[208,2048]{1,0:T(8,128)(2,1)} %get-tuple-element.217) | copy-start | bytes 2555908
  135.6 6.2 %collective-permute-start.29 = (bf16[208,2048]{1,0:T(8,128)(2,1)}, bf16[208,2048]{1,0:T(8,128)(2,1)S(1)}, u32[]{:S(2)}, u32[]{:S(2)}) collective-permute-start(bf16[208,2048]{1,0:T(8,128)(2,1)} %get-tuple-element.218), channel_id=1, source_target_pairs={{0,4},{4,0},{8,12},{12,8},{1,5},{5,1},{9,13},{13,9},{2,6},{6,2},{1... | collective-permute-start | bytes 2555912 | tf_op jit(solution)/shard_map/token_grads_core/ppermute | solution.py:23
  135.8 19.3 %collective-permute-start.31 = (bf16[768,512]{1,0:T(8,128)(2,1)}, bf16[768,512]{1,0:T(8,128)(2,1)}, u32[]{:S(2)}, u32[]{:S(2)}) collective-permute-start(bf16[768,512]{1,0:T(8,128)(2,1)} %get-tuple-element.195.refs_12_), channel_id=1, source_target_pairs={{1,2},{2,1},{5,6},{6,5},{9,10},{10,9},{13,14},{14,13},{17,18},{18,... | collective-permute-start | bytes 2359304 | tf_op jit(solution)/shard_map/up_far_sums_across/ppermute | solution.py:23
  137.5 42.5 %collective-permute-start.32 = (bf16[768,512]{1,0:T(8,128)(2,1)}, bf16[768,512]{1,0:T(8,128)(2,1)}, u32[]{:S(2)}, u32[]{:S(2)}) collective-permute-start(bf16[768,512]{1,0:T(8,128)(2,1)} %get-tuple-element.196.refs_13_), channel_id=1, source_target_pairs={{1,2},{2,1},{5,6},{6,5},{9,10},{10,9},{13,14},{14,13},{17,18},{18,... | collective-permute-start | bytes 2359304 | tf_op jit(solution)/shard_map/up_sums_across/ppermute | solution.py:23
  140.2 27.9 %collective-permute-start.33 = (bf16[512,768]{1,0:T(8,128)(2,1)}, bf16[512,768]{1,0:T(8,128)(2,1)}, u32[]{:S(2)}, u32[]{:S(2)}) collective-permute-start(bf16[512,768]{1,0:T(8,128)(2,1)} %turned_sum.5), channel_id=1, source_target_pairs={{1,0},{2,3},{5,4},{6,7},{9,8},{10,11},{13,12},{14,15},{17,16},{18,... | collective-permute-start | bytes 2359304 | tf_op jit(solution)/shard_map/gate_sums_outward/ppermute | solution.py:23
  141.5 41.1 %collective-permute-start.28 = (bf16[208,2048]{1,0:T(8,128)(2,1)}, bf16[208,2048]{1,0:T(8,128)(2,1)}, u32[]{:S(2)}, u32[]{:S(2)}) collective-permute-start(bf16[208,2048]{1,0:T(8,128)(2,1)} %get-tuple-element.216), channel_id=1, source_target_pairs={{0,4},{4,0},{8,12},{12,8},{1,5},{5,1},{9,13},{13,9},{2,6},{6,2},{1... | collective-permute-start | bytes 2555912 | tf_op jit(solution)/shard_map/token_grads_core/ppermute | solution.py:23
  143.1 9.4 %copy-start.17 = (bf16[768,512]{1,0:T(8,128)(2,1)S(1)}, bf16[768,512]{1,0:T(8,128)(2,1)}, u32[]{:S(2)}) copy-start(bf16[768,512]{1,0:T(8,128)(2,1)} %get-tuple-element.223.refs_8_.refs_0_) | copy-start | bytes 2359300
  143.1 41.0 %collective-permute-start.30 = (bf16[208,2048]{1,0:T(8,128)(2,1)}, bf16[208,2048]{1,0:T(8,128)(2,1)}, u32[]{:S(2)}, u32[]{:S(2)}) collective-permute-start(bf16[208,2048]{1,0:T(8,128)(2,1)} %add_convert_fusion), channel_id=1, source_target_pairs={{8,0},{12,4},{0,8},{4,12},{9,1},{13,5},{1,9},{5,13},{10,2},{14,6},... | collective-permute-start | bytes 2555912 | tf_op jit(solution)/shard_map/token_grads_chip/ppermute | solution.py:23
  152.5 1.1 copy-start.13
  153.6 1.1 copy-start.15
  154.7 1.1 copy-start.16
  157.3 28.9 %collective-permute-start.34 = (bf16[512,768]{1,0:T(8,128)(2,1)S(1)}, bf16[512,768]{1,0:T(8,128)(2,1)S(1)}, u32[]{:S(2)}, u32[]{:S(2)}) collective-permute-start(bf16[512,768]{1,0:T(8,128)(2,1)S(1)} %turned_sum.6.refs_3_), channel_id=1, source_target_pairs={{1,0},{2,3},{5,4},{6,7},{9,8},{10,11},{13,12},{14,15},{17,16},{18,... | collective-permute-start | bytes 2359304 | tf_op jit(solution)/shard_map/up_sums_outward/ppermute | solution.py:23
  170.3 9.7 %copy-start.14 = (bf16[768,512]{1,0:T(8,128)(2,1)S(1)}, bf16[768,512]{1,0:T(8,128)(2,1)}, u32[]{:S(2)}) copy-start(bf16[768,512]{1,0:T(8,128)(2,1)} %get-tuple-element.225.refs_2_.refs_0_) | copy-start | bytes 2359300
  170.3 12.3 %copy-start.30 = (bf16[208,2048]{1,0:T(8,128)(2,1)S(1)}, bf16[208,2048]{1,0:T(8,128)(2,1)}, u32[]{:S(2)}) copy-start(bf16[208,2048]{1,0:T(8,128)(2,1)} %get-tuple-element.215) | copy-start | bytes 2555908
  180.0 1.1 copy-start.18
  186.3 1.1 copy-start.22
  (5 other events, 4.2 us)
